TPU v7x, 32 devices: a whole 2x2x4 slice. The times are simulated.
32 devices in a mesh: seq: 8 (over z, x), fsdp: 4 (over y, core).
Axes of the slice: x: 2, y: 2, z: 4, core: 2. Of those that a mesh axis runs over, the one named last changes fastest.
Arguments:
- block_input: float32 [8, 1024, 1536], P('fsdp', 'seq'), may hold values from -6 to 6
- teacher: float32 [8, 1024, 1536], P('fsdp', 'seq'), may hold values from -6 to 6
- valid_lengths: int32 [8], replicated, may hold values from 128 to 1024, as said below
- norm_gain: bfloat16 [1536], P('fsdp'), may hold values from 0.5 to 1.5
- w_gate: bfloat16 [1536, 2048], P('fsdp'), may hold values from -0.15625 to 0.15625
- w_input: bfloat16 [1536, 2048], P('fsdp'), may hold values from -0.15625 to 0.15625
- conv_weight: bfloat16 [4, 2048], P(None, 'fsdp'), may hold values from -3 to 3
- conv_bias: bfloat16 [2048], P('fsdp'), may hold values from -1.5 to 1.5
- w_rate: bfloat16 [2048, 128], P('fsdp'), may hold values from -0.5 to 0.5
- bias_rate: bfloat16 [2048], P('fsdp'), may hold values from -2.5 to 2.5
- w_inlet: bfloat16 [2048, 128], P('fsdp'), may hold values from -0.5 to 0.5
- bias_inlet: bfloat16 [2048], P('fsdp'), may hold values from -2.5 to 2.5
- decay_param: bfloat16 [2048], P('fsdp'), may hold values from 4 to 16
- w_out: bfloat16 [2048, 1536], P('fsdp'), may hold values from -0.25 to 0.25
- mlp_gain: bfloat16 [1536], P('fsdp'), may hold values from 0.5 to 1.5
- w_up: bfloat16 [1536, 4608], P('fsdp'), may hold values from -0.15625 to 0.15625
- w_value: bfloat16 [1536, 4608], P('fsdp'), may hold values from -0.15625 to 0.15625
- w_down: bfloat16 [4608, 1536], P('fsdp'), may hold values from -0.09375 to 0.09375
Outputs:
- block_output: float32 [8, 1024, 1536], P('fsdp', 'seq')
- grad_input: float32 [8, 1024, 1536], P('fsdp', 'seq')
- grad_norm_gain: float32 [1536], P(('seq', 'fsdp'))
- grad_w_gate: float32 [1536, 2048], P(('seq', 'fsdp'))
- grad_w_input: float32 [1536, 2048], P(('seq', 'fsdp'))
- grad_conv_weight: float32 [4, 2048], P(None, ('seq', 'fsdp'))
- grad_conv_bias: float32 [2048], P(('seq', 'fsdp'))
- grad_w_rate: float32 [2048, 128], P(('seq', 'fsdp'))
- grad_bias_rate: float32 [2048], P(('seq', 'fsdp'))
- grad_w_inlet: float32 [2048, 128], P(('seq', 'fsdp'))
- grad_bias_inlet: float32 [2048], P(('seq', 'fsdp'))
- grad_decay_param: float32 [2048], P(('seq', 'fsdp'))
- grad_w_out: float32 [2048, 1536], P(('seq', 'fsdp'))
- grad_mlp_gain: float32 [1536], P(('seq', 'fsdp'))
- grad_w_up: float32 [1536, 4608], P(('seq', 'fsdp'))
- grad_w_value: float32 [1536, 4608], P(('seq', 'fsdp'))
- grad_w_down: float32 [4608, 1536], P(('seq', 'fsdp'))
Inputs may be any that keep to these rules, and one draw needn't show every extreme that they name: `valid_lengths`: on each index of fsdp one of its 2 sequences is valid to its end.
All inputs are finite; a program needn't handle non-finite values.
Results may differ from a plain program's by a relative error of at most 0.012.
Values may be sent and summed in bfloat16 or wider, within the bound.
A program may use at most 448 MiB of HBM per device.

v0:
```python
import jax
import jax.numpy as jnp
from jax import lax
from jax.sharding import PartitionSpec as P

EPS_NORM = 1e-06
EPS_MULT = 0.0001
RATE_SCALE = 8.0


def shifted(shard, axis, by):
    length = lax.axis_size(axis)
    pairs = [(i, i + by) for i in range(length) if 0 <= i + by < length]
    return lax.ppermute(shard, axis, pairs)


def entering(shard, axis, join, neutral):
    place = lax.axis_index(axis)
    gathered = jax.tree.map(
        lambda a, kind: lax.all_gather(a.astype(kind), axis), shard, (jnp.bfloat16, jnp.bfloat16)
    )
    state = jax.tree.map(lambda a, e: jnp.zeros_like(a) + jnp.asarray(e, a.dtype), shard, neutral)

    def one(hop, state):
        return join(
            state,
            jax.tree.map(
                lambda a, own: lax.dynamic_index_in_dim(a, hop, 0, False).astype(own.dtype),
                gathered,
                shard,
            ),
        )

    return lax.fori_loop(0, place, one, state)


def entering_2(shard, axis, combine, identity):
    length, index = (lax.axis_size(axis), lax.axis_index(axis))
    everything = jax.tree.map(
        lambda part, kind: lax.all_gather(part.astype(kind), axis),
        shard,
        jax.tree.map(lambda a: jnp.bfloat16 if a.dtype == jnp.float32 else a.dtype, shard),
    )
    start = jax.tree.map(
        lambda part, zero: jnp.broadcast_to(jnp.asarray(zero, part.dtype), part.shape),
        shard,
        identity,
    )

    def hop(k, before):
        at = length - 1 - k
        reached = at > index
        new = combine(
            before, jax.tree.map(lambda part, own: part[at].astype(own.dtype), everything, shard)
        )
        return jax.tree.map(lambda a, b: jnp.where(reached, a, b), new, before)

    return lax.fori_loop(0, length, hop, start)


def matmul(left, right):
    return jnp.dot(left, right, preferred_element_type=jnp.float32)


def matmul_left_t(left, right):
    return lax.dot_general(
        left, right, (((0,), (0,)), ((), ())), preferred_element_type=jnp.float32
    )


def matmul_right_t(left, right):
    return lax.dot_general(
        left, right, (((1,), (1,)), ((), ())), preferred_element_type=jnp.float32
    )


def rms_scale(values, gain_vec):
    return (
        values * lax.rsqrt(jnp.mean(values * values, axis=-1, keepdims=True) + EPS_NORM) * gain_vec
    )


def gate_terms(rate_pre, inlet_pre, decay_vec, values):
    rate_gate = jax.nn.sigmoid(rate_pre)
    inlet_gate = jax.nn.sigmoid(inlet_pre)
    log_decay = -RATE_SCALE * rate_gate * jax.nn.softplus(-decay_vec)
    decay_now = jnp.exp(log_decay)
    factor = jnp.sqrt(EPS_MULT - jnp.expm1(2.0 * log_decay))
    return (decay_now, factor * inlet_gate * values)


def linear_step(first_pair, second_pair):
    return (first_pair[0] * second_pair[0], second_pair[1] + second_pair[0] * first_pair[1])


def conv_apply(padded, conv_w, conv_b):
    taps_count = conv_w.shape[0]
    length = padded.shape[1] - taps_count + 1
    conv_sum = conv_b
    for offset in range(taps_count):
        conv_sum = (
            conv_sum
            + conv_w[offset] * padded[:, taps_count - 1 - offset : taps_count - 1 - offset + length]
        )
    return conv_sum


def gelu_product(first_in, gate_in):
    return first_in * jax.nn.gelu(gate_in)


def body(
    block_input,
    teacher,
    valid_lengths,
    norm_gain,
    w_gate,
    w_input,
    conv_weight,
    conv_bias,
    w_rate,
    bias_rate,
    w_inlet,
    bias_inlet,
    decay_param,
    w_out,
    mlp_gain,
    w_up,
    w_value,
    w_down,
):
    (
        gain_one,
        gate_full,
        input_full,
        conv_full,
        conv_bias_full,
        rate_full,
        rate_bias_full,
        inlet_full,
        inlet_bias_full,
        decay_full,
        out_full,
    ) = (
        lax.all_gather(norm_gain, "fsdp", axis=0, tiled=True),
        lax.all_gather(w_gate, "fsdp", axis=0, tiled=True),
        lax.all_gather(w_input, "fsdp", axis=0, tiled=True),
        lax.all_gather(conv_weight, "fsdp", axis=1, tiled=True),
        lax.all_gather(conv_bias, "fsdp", axis=0, tiled=True),
        lax.all_gather(w_rate, "fsdp", axis=0, tiled=True),
        lax.all_gather(bias_rate, "fsdp", axis=0, tiled=True),
        lax.all_gather(w_inlet, "fsdp", axis=0, tiled=True),
        lax.all_gather(bias_inlet, "fsdp", axis=0, tiled=True),
        lax.all_gather(decay_param, "fsdp", axis=0, tiled=True),
        lax.all_gather(w_out, "fsdp", axis=0, tiled=True),
    )
    gain_two, up_full, value_full, down_full = (
        lax.all_gather(mlp_gain, "fsdp", axis=0, tiled=True),
        lax.all_gather(w_up, "fsdp", axis=0, tiled=True),
        lax.all_gather(w_value, "fsdp", axis=0, tiled=True),
        lax.all_gather(w_down, "fsdp", axis=0, tiled=True),
    )
    rows_dev, tok_dev, model_width = block_input.shape
    branch_width = gate_full.shape[1]
    block_width = rate_full.shape[1]
    ff_width = up_full.shape[1]
    head_count = branch_width // block_width
    taps_count = conv_full.shape[0]
    count_rows = rows_dev * tok_dev
    devices = lax.axis_size("seq") * lax.axis_size("fsdp")
    flat_in = block_input.reshape(count_rows, model_width)
    norm_one, norm_one_back = jax.vjp(rms_scale, flat_in, gain_one.astype(jnp.float32))
    normed = norm_one.astype(jnp.bfloat16)
    gate_pre = matmul(normed, gate_full)
    branch_in = (
        matmul(normed, input_full).astype(jnp.bfloat16).reshape(rows_dev, tok_dev, branch_width)
    )
    tail_prev = shifted(branch_in[:, tok_dev - (taps_count - 1) :], "seq", 1)
    padded = jnp.concatenate([tail_prev, branch_in], axis=1).astype(jnp.float32)
    conv_out, conv_back = jax.vjp(
        conv_apply, padded, conv_full.astype(jnp.float32), conv_bias_full.astype(jnp.float32)
    )
    conv_low = conv_out.astype(jnp.bfloat16).reshape(count_rows, branch_width)
    heads_in = conv_low.reshape(count_rows, head_count, block_width)
    rate_blocks = rate_full.reshape(head_count, block_width, block_width)
    inlet_blocks = inlet_full.reshape(head_count, block_width, block_width)
    rate_pre = jnp.einsum(
        "nhi,hij->nhj", heads_in, rate_blocks, preferred_element_type=jnp.float32
    ).reshape(count_rows, branch_width) + rate_bias_full.astype(jnp.float32)
    inlet_pre = jnp.einsum(
        "nhi,hij->nhj", heads_in, inlet_blocks, preferred_element_type=jnp.float32
    ).reshape(count_rows, branch_width) + inlet_bias_full.astype(jnp.float32)
    (decay_flat, pushed_flat), gates_back = jax.vjp(
        gate_terms,
        rate_pre,
        inlet_pre,
        decay_full.astype(jnp.float32),
        conv_low.astype(jnp.float32),
    )
    decay_now = decay_flat.reshape(rows_dev, tok_dev, branch_width)
    pushed = pushed_flat.reshape(rows_dev, tok_dev, branch_width)
    cum_decay, local_state = lax.associative_scan(linear_step, (decay_now, pushed), axis=1)
    ones_state = jnp.ones((rows_dev, branch_width), jnp.float32)
    zero_state = jnp.zeros((rows_dev, branch_width), jnp.float32)
    unused_prod, state_in = entering(
        (cum_decay[:, -1], local_state[:, -1]), "seq", linear_step, (ones_state, zero_state)
    )
    states = local_state + cum_decay * state_in[:, None]
    prev_states = jnp.concatenate([state_in[:, None], states[:, :-1]], axis=1)
    merged, merge_back = jax.vjp(gelu_product, states.reshape(count_rows, branch_width), gate_pre)
    merged_low = merged.astype(jnp.bfloat16)
    middle = flat_in + matmul(merged_low, out_full)
    norm_two, norm_two_back = jax.vjp(rms_scale, middle, gain_two.astype(jnp.float32))
    normed_two = norm_two.astype(jnp.bfloat16)
    up_pre = matmul(normed_two, up_full)
    value_pre = matmul(normed_two, value_full)
    hidden, hidden_back = jax.vjp(gelu_product, up_pre, value_pre)
    hidden_low = hidden.astype(jnp.bfloat16)
    result = middle + matmul(hidden_low, down_full)
    row_start = lax.axis_index("fsdp") * rows_dev
    my_lengths = lax.dynamic_slice_in_dim(valid_lengths, row_start, rows_dev)
    positions = lax.axis_index("seq") * tok_dev + jnp.arange(tok_dev, dtype=jnp.int32)
    valid_mask = (positions[None, :] < my_lengths[:, None]).reshape(count_rows, 1)
    slot_count = valid_lengths.shape[0] * tok_dev * lax.axis_size("seq")
    count = jnp.sum(valid_lengths).astype(jnp.float32)
    grad_out = jnp.where(valid_mask, result - teacher.reshape(count_rows, model_width), 0.0) * (
        slot_count / count
    )
    grad_down_in = grad_out.astype(jnp.bfloat16)
    grad_hidden = matmul_right_t(grad_down_in, down_full)
    grad_up_pre, grad_value_pre = hidden_back(grad_hidden)
    grad_up_low = grad_up_pre.astype(jnp.bfloat16)
    grad_value_low = grad_value_pre.astype(jnp.bfloat16)
    grad_normed_two = matmul_right_t(grad_up_low, up_full) + matmul_right_t(
        grad_value_low, value_full
    )
    grad_mid_norm, grad_gain_two = norm_two_back(grad_normed_two)
    grad_middle = grad_out + grad_mid_norm
    grad_upvalue = jnp.concatenate([grad_up_low, grad_value_low], axis=1)
    upvalue_sum = lax.psum_scatter(
        matmul_left_t(normed_two, grad_upvalue), ("seq", "fsdp"), scatter_dimension=0, tiled=True
    )
    sum_up = upvalue_sum[:, :ff_width]
    sum_value = upvalue_sum[:, ff_width:]
    sum_down = lax.psum_scatter(
        matmul_left_t(hidden_low, grad_down_in), ("seq", "fsdp"), scatter_dimension=0, tiled=True
    )
    grad_mid_low = grad_middle.astype(jnp.bfloat16)
    grad_merged = matmul_right_t(grad_mid_low, out_full)
    grad_states, grad_gate_pre = merge_back(grad_merged)
    grad_gate_low = grad_gate_pre.astype(jnp.bfloat16)
    grad_states = grad_states.reshape(rows_dev, tok_dev, branch_width)
    next_decay = jnp.concatenate(
        [decay_now[:, 1:], jnp.ones((rows_dev, 1, branch_width), jnp.float32)], axis=1
    )
    carry_decay, local_adjoint = lax.associative_scan(
        linear_step, (next_decay, grad_states), axis=1, reverse=True
    )
    unused_back, adjoint_after = entering_2(
        (cum_decay[:, -1], decay_now[:, 0] * local_adjoint[:, 0]),
        "seq",
        linear_step,
        (ones_state, zero_state),
    )
    adjoint = local_adjoint + carry_decay * adjoint_after[:, None]
    grad_decay = (adjoint * prev_states).reshape(count_rows, branch_width)
    grad_pushed = adjoint.reshape(count_rows, branch_width)
    grad_rate_pre, grad_inlet_pre, grad_decay_param, grad_conv_direct = gates_back(
        (grad_decay, grad_pushed)
    )
    grad_rate_bias = jnp.sum(grad_rate_pre, axis=0)
    grad_inlet_bias = jnp.sum(grad_inlet_pre, axis=0)
    rate_flat = grad_rate_pre.astype(jnp.bfloat16)
    inlet_flat = grad_inlet_pre.astype(jnp.bfloat16)
    rate_low = rate_flat.reshape(count_rows, head_count, block_width)
    inlet_low = inlet_flat.reshape(count_rows, head_count, block_width)
    out_part = matmul_left_t(merged_low, grad_mid_low)
    rate_all = matmul_left_t(conv_low, rate_flat).reshape(
        branch_width // devices * lax.axis_size(("seq", "fsdp")), head_count, block_width
    )
    inlet_all = matmul_left_t(conv_low, inlet_flat).reshape(
        branch_width // devices * lax.axis_size(("seq", "fsdp")), head_count, block_width
    )
    head_of = (
        jnp.arange(branch_width // devices * lax.axis_size(("seq", "fsdp")), dtype=jnp.int32)
        // block_width
    )
    one_hot = (head_of[:, None] == jnp.arange(head_count, dtype=jnp.int32)[None, :]).astype(
        jnp.float32
    )[:, :, None]
    rate_part = jnp.sum(rate_all * one_hot, axis=1)
    inlet_part = jnp.sum(inlet_all * one_hot, axis=1)
    out_sum = lax.psum_scatter(
        jnp.concatenate([out_part, rate_part, inlet_part], axis=1),
        ("seq", "fsdp"),
        scatter_dimension=0,
        tiled=True,
    )
    sum_out = out_sum[:, :model_width]
    sum_rate = out_sum[:, model_width : model_width + block_width]
    sum_inlet = out_sum[:, model_width + block_width :]
    grad_conv = grad_conv_direct
    grad_conv = grad_conv + jnp.einsum(
        "nhj,hij->nhi", rate_low, rate_blocks, preferred_element_type=jnp.float32
    ).reshape(count_rows, branch_width)
    grad_conv = grad_conv + jnp.einsum(
        "nhj,hij->nhi", inlet_low, inlet_blocks, preferred_element_type=jnp.float32
    ).reshape(count_rows, branch_width)
    grad_padded, grad_conv_w, grad_conv_b = conv_back(
        grad_conv.reshape(rows_dev, tok_dev, branch_width)
    )
    edge_in = shifted(grad_padded[:, : taps_count - 1].astype(jnp.bfloat16), "seq", -1).astype(
        jnp.float32
    )
    grad_branch = grad_padded[:, taps_count - 1 :].at[:, tok_dev - (taps_count - 1) :].add(edge_in)
    grad_branch_low = grad_branch.reshape(count_rows, branch_width).astype(jnp.bfloat16)
    grad_gatebranch = jnp.concatenate([grad_gate_low, grad_branch_low], axis=1)
    input_sum = lax.psum_scatter(
        matmul_left_t(normed, grad_gatebranch), ("seq", "fsdp"), scatter_dimension=0, tiled=True
    )
    sum_gate = input_sum[:, :branch_width]
    sum_input = input_sum[:, branch_width:]
    grad_normed = matmul_right_t(grad_gate_low, gate_full) + matmul_right_t(
        grad_branch_low, input_full
    )
    grad_flat_norm, grad_gain_one = norm_one_back(grad_normed)
    grad_input = grad_middle + grad_flat_norm
    sum_gain_one, sum_conv_w, sum_conv_b, sum_rate_b, sum_inlet_b, sum_decay, sum_gain_two = (
        lax.psum_scatter(grad_gain_one, ("seq", "fsdp"), scatter_dimension=0, tiled=True),
        lax.psum_scatter(grad_conv_w, ("seq", "fsdp"), scatter_dimension=1, tiled=True),
        lax.psum_scatter(grad_conv_b, ("seq", "fsdp"), scatter_dimension=0, tiled=True),
        lax.psum_scatter(grad_rate_bias, ("seq", "fsdp"), scatter_dimension=0, tiled=True),
        lax.psum_scatter(grad_inlet_bias, ("seq", "fsdp"), scatter_dimension=0, tiled=True),
        lax.psum_scatter(grad_decay_param, ("seq", "fsdp"), scatter_dimension=0, tiled=True),
        lax.psum_scatter(grad_gain_two, ("seq", "fsdp"), scatter_dimension=0, tiled=True),
    )
    block_output = result.reshape(rows_dev, tok_dev, model_width)
    grad_block = grad_input.reshape(rows_dev, tok_dev, model_width)
    return (
        block_output,
        grad_block,
        sum_gain_one,
        sum_gate,
        sum_input,
        sum_conv_w,
        sum_conv_b,
        sum_rate,
        sum_rate_b,
        sum_inlet,
        sum_inlet_b,
        sum_decay,
        sum_out,
        sum_gain_two,
        sum_up,
        sum_value,
        sum_down,
    )


def solution(mesh):
    return jax.shard_map(
        body,
        mesh=mesh,
        in_specs=(
            P("fsdp", "seq", None),
            P("fsdp", "seq", None),
            P(),
            P("fsdp"),
            P("fsdp", None),
            P("fsdp", None),
            P(None, "fsdp"),
            P("fsdp"),
            P("fsdp", None),
            P("fsdp"),
            P("fsdp", None),
            P("fsdp"),
            P("fsdp"),
            P("fsdp", None),
            P("fsdp"),
            P("fsdp", None),
            P("fsdp", None),
            P("fsdp", None),
        ),
        out_specs=(
            P("fsdp", "seq", None),
            P("fsdp", "seq", None),
            P(("seq", "fsdp")),
            P(("seq", "fsdp"), None),
            P(("seq", "fsdp"), None),
            P(None, ("seq", "fsdp")),
            P(("seq", "fsdp")),
            P(("seq", "fsdp"), None),
            P(("seq", "fsdp")),
            P(("seq", "fsdp"), None),
            P(("seq", "fsdp")),
            P(("seq", "fsdp")),
            P(("seq", "fsdp"), None),
            P(("seq", "fsdp")),
            P(("seq", "fsdp"), None),
            P(("seq", "fsdp"), None),
            P(("seq", "fsdp"), None),
        ),
        check_vma=False,
    )
```

profile of v0, /device:TPU:0, one launch (start us, length us, event | category | flops | bytes accessed | tf_op | source)
XLA Modules:
  0.0 2092.0 jit_solution(11404252996247414256)
XLA Ops:
  11.3 6.1 all-gather.4
  18.3 5.4 all_gather.60
  23.8 11.0 all_gather.66
  34.8 5.2 all-gather.6
  40.6 10.9 all_gather.63
  52.0 5.2 all-gather.8
  57.8 6.6 all-gather.16.cloned.1.call-done
  64.4 4.6 convolution_convert_fusion
  73.8 5.2 all-gather.3
  79.0 5.2 all-gather.7
  84.2 5.2 all-gather.5
  100.4 4.2 copy.84
  110.8 4.2 copy.81
  115.0 6.0 convert_multiply_fusion.3
  121.1 5.9 slice.528
  127.0 5.4 slice.530
  138.1 5.4 slice.532
  246.3 5.8 pad.212
  256.6 30.5 %all-gather = bf16[16,1,2048]{2,1,0:T(2,128)(2,1)S(1)} all-gather(bf16[2,1,2048]{2,1,0:T(2,128)(2,1)S(1)} %add_convert_fusion.2), channel_id=2, replica_groups=mesh['seq'=8,'fsdp'=4] {'seq'}, dimensions={0}, use_global_device_ids=true | all-gather | bytes 73728 | tf_op jit(solution)/shard_map/all_gather | solution.py:20
  288.5 30.5 %all-gather.1 = bf16[16,1,2048]{2,1,0:T(2,128)(2,1)S(1)} all-gather(bf16[2,1,2048]{2,1,0:T(2,128)(2,1)S(1)} %add_convert_fusion.1), channel_id=3, replica_groups=mesh['seq'=8,'fsdp'=4] {'seq'}, dimensions={0}, use_global_device_ids=true | all-gather | bytes 73728 | tf_op jit(solution)/shard_map/all_gather | solution.py:20
  320.7 9.1 slice.598
  329.8 5.2 slice.608
  335.0 5.3 slice.602
  345.2 5.9 multiply_add_fusion.2
  351.2 8.5 fusion.44
  359.6 6.7 multiply_reduce_fusion.10
  366.6 10.9 fusion.115
  377.5 13.1 multiply_convert_fusion.1
  390.6 47.4 %all-gather.26.cloned.1.call-done = bf16[4608,1536]{1,0:T(8,128)(2,1)} async-done(((bf16[1152,1536]{1,0:T(8,128)(2,1)}), bf16[4608,1536]{1,0:T(8,128)(2,1)}) %all-gather.26.cloned.1.call-update) | async-done | bytes 14155792 | tf_op jit(solution)/shard_map/all_gather | solution.py:161
  438.0 11.1 fusion.49
  449.1 11.5 fusion.9
  460.6 9.9 fusion.116
  470.6 11.1 multiply_reduce_fusion.7
  484.4 7.4 fusion.58
  491.8 5.4 slice.599
  501.2 8.9 slice.600
  510.1 5.3 slice.604
  579.7 5.4 slice.594
  610.7 9.0 slice.595
  632.9 5.4 pad.240
  646.8 6.4 fusion.61
  653.2 16.8 rev.8
  680.2 16.8 rev.9
  697.0 30.6 %all-gather.2 = bf16[16,1,2048]{2,1,0:T(2,128)(2,1)S(1)} all-gather(bf16[2,1,2048]{2,1,0:T(2,128)(2,1)S(1)} %fusion.84), channel_id=4, replica_groups=mesh['seq'=8,'fsdp'=4] {'seq'}, dimensions={0}, use_global_device_ids=true | all-gather | bytes 73728 | tf_op jit(solution)/shard_map/all_gather | solution.py:40
  728.0 6.4 while.30
  734.6 7.5 fusion.45
  753.2 7.5 multiply_reduce_fusion.2
  774.8 7.0 multiply_reduce_fusion.6
  783.8 6.6 fusion.34
  791.9 8.2 multiply_reduce_fusion
  803.2 8.9 multiply_reduce_fusion.1
  813.6 10.0 pad_maximum_fusion
  823.6 14.3 copy.123
  843.4 4.3 collective-permute-done.1
  848.3 10.2 fusion.37
  860.4 22.0 %fusion.10 = f32[1536,9216]{1,0:T(8,128)} fusion(bf16[256,1536]{1,0:T(8,128)(2,1)S(1)} %copy-done.41, bf16[256,4608]{1,0:T(8,128)(2,1)S(1)} %copy-done.46, bf16[256,4608]{1,0:T(8,128)(2,1)} %copy-done.47), kind=kOutput, calls=%fused_computation.17 | convolution fusion | flops 7257194496 | bytes 62128128 | tf_op jit(solution)/shard_map/dot_general | solution.py:66
  883.8 13.1 fusion.65
  898.2 4.8 fusion.117
  903.0 6.3 multiply_reduce_fusion.8
  909.4 42.6 %all-reduce.72 = (f32[1536]{0:T(1024)S(1)}, f32[2048]{0:T(1024)S(1)}, f32[2048]{0:T(1024)S(1)}, f32[2048]{0:T(1024)S(1)}, f32[2048]{0:T(1024)S(1)}, /*index=5*/f32[1536]{0:T(1024)S(1)}) all-reduce(f32[1536]{0:T(1024)S(1)} %get-tuple-element.282, ...), channel_id=5, replica_groups=mesh['seq'=8,'fsdp'=4] {'seq','fsdp'}, use_global_device_ids=true, to_apply=%region_10.11.clone | all-reduce | flops 11264 | bytes 90112
  960.1 120.6 %reduce-scatter.18.cloned.1.call-done = f32[64,1792]{1,0:T(8,128)} async-done(((f32[2048,1792]{1,0:T(8,128)}), f32[64,1792]{1,0:T(8,128)}) %reduce-scatter.18.cloned.1.call-update) | async-done | bytes 458768
  1083.9 251.0 %reduce-scatter.10.cloned.1.call-done = f32[48,4096]{1,0:T(8,128)} async-done(((f32[1536,4096]{1,0:T(8,128)}), f32[48,4096]{1,0:T(8,128)}) %reduce-scatter.10.cloned.1.call-update) | async-done | bytes 786448 | tf_op jit(solution)/shard_map/reduce_scatter | solution.py:318
  1336.9 477.4 %reduce-scatter.12.cloned.1.call-done = f32[48,9216]{1,0:T(8,128)} async-done(((f32[1536,9216]{1,0:T(8,128)}), f32[48,9216]{1,0:T(8,128)}) %reduce-scatter.12.cloned.1.call-update) | async-done | bytes 1769488 | tf_op jit(solution)/shard_map/reduce_scatter | solution.py:240
  1817.1 268.2 %reduce-scatter.14.cloned.1.call-done = f32[144,1536]{1,0:T(8,128)} async-done(((f32[4608,1536]{1,0:T(8,128)}), f32[144,1536]{1,0:T(8,128)}) %reduce-scatter.14.cloned.1.call-update) | async-done | bytes 884752 | tf_op jit(solution)/shard_map/reduce_scatter | solution.py:245
  (573 shorter events, 342.6 us)
Async XLA Ops:
  7.2 57.2 %all-gather.16.cloned.1.call-start = ((), (), s32[]{:S(2)}) async-start(), calls=%async_computation.5 | async-start | bytes 7864320 | tf_op jit(solution)/shard_map/all_gather | solution.py:147
  7.9 343.2 %all-gather.18.cloned.1.call-start = ((), (), s32[]{:S(2)}) async-start(), calls=%async_computation.6 | async-start | bytes 7864320 | tf_op jit(solution)/shard_map/all_gather | solution.py:146
  8.7 351.0 %all-gather.20.cloned.1.call-start = ((), (), s32[]{:S(2)}) async-start(), calls=%async_computation.7 | async-start | bytes 7864320 | tf_op jit(solution)/shard_map/all_gather | solution.py:155
  9.4 357.1 %all-gather.24.cloned.1.call-start = ((), (), s32[]{:S(2)}) async-start(), calls=%async_computation.9 | async-start | bytes 17694720 | tf_op jit(solution)/shard_map/all_gather | solution.py:160
  10.0 367.5 %all-gather.22.cloned.1.call-start = ((), (), s32[]{:S(2)}) async-start(), calls=%async_computation.8 | async-start | bytes 17694720 | tf_op jit(solution)/shard_map/all_gather | solution.py:159
  10.6 13.1 copy-start.87
  10.6 24.1 %copy-start.113 = (bf16[512]{0:T(512)(128)(2,1)S(1)}, bf16[512]{0:T(512)(128)(2,1)}, u32[]{:S(2)}) copy-start(bf16[512]{0:T(512)(128)(2,1)} %param.36) | copy-start | bytes 3076
  10.6 427.4 %all-gather.26.cloned.1.call-start = ((), (), s32[]{:S(2)}) async-start(), calls=%async_computation.10 | async-start | bytes 17694720 | tf_op jit(solution)/shard_map/all_gather | solution.py:161
  11.2 29.4 %copy-start.88 = (bf16[512,128]{1,0:T(8,128)(2,1)S(1)}, bf16[512,128]{1,0:T(8,128)(2,1)}, u32[]{:S(2)}) copy-start(bf16[512,128]{1,0:T(8,128)(2,1)} %param.32) | copy-start | bytes 393220
  11.2 40.3 %copy-start.119 = (s32[8]{0:T(128)S(1)}, s32[8]{0:T(128)}, u32[]{:S(2)}) copy-start(s32[8]{0:T(128)} %param.26) | copy-start | bytes 100
  11.2 947.4 %reduce-scatter.16.cloned.1.call-start = ((), (), s32[]{:S(2)}) async-start(), calls=%async_computation.14 | async-start | bytes 1081344
  17.5 34.4 %copy-start.85 = (f32[1536]{0:T(1024)}, f32[1536]{0:T(1024)S(1)}, u32[]{:S(2)}) copy-start(f32[1536]{0:T(1024)S(1)} %reshape.482) | copy-start | bytes 18436
  18.2 33.7 %copy-start.118 = (bf16[384]{0:T(512)(128)(2,1)S(1)}, bf16[384]{0:T(512)(128)(2,1)}, u32[]{:S(2)}) copy-start(bf16[384]{0:T(512)(128)(2,1)} %param.38) | copy-start | bytes 2308
  18.3 33.5 %copy-start.107 = (f32[256]{0:T(256)}, f32[256]{0:T(256)S(1)}, u32[]{:S(2)}) copy-start(f32[256]{0:T(256)S(1)} %bitcast_rsqrt_fusion) | copy-start | bytes 3076
  23.7 91.2 %copy-start.75 = (f32[1,2048]{1,0:T(1,128)}, f32[1,2048]{1,0:T(1,128)S(1)}, u32[]{:S(2)}) copy-start(f32[1,2048]{1,0:T(1,128)S(1)} %get-tuple-element.399) | copy-start | bytes 24580
  23.8 91.2 %copy-start.77 = (f32[1,2048]{1,0:T(1,128)}, f32[1,2048]{1,0:T(1,128)S(1)}, u32[]{:S(2)}) copy-start(f32[1,2048]{1,0:T(1,128)S(1)} %get-tuple-element.400) | copy-start | bytes 24580
  23.8 91.2 %copy-start.79 = (f32[1,2048]{1,0:T(1,128)}, f32[1,2048]{1,0:T(1,128)S(1)}, u32[]{:S(2)}) copy-start(f32[1,2048]{1,0:T(1,128)S(1)} %get-tuple-element.401) | copy-start | bytes 24580
  23.8 91.2 %copy-start.81 = (f32[1,2048]{1,0:T(1,128)}, f32[1,2048]{1,0:T(1,128)S(1)}, u32[]{:S(2)}) copy-start(f32[1,2048]{1,0:T(1,128)S(1)} %get-tuple-element.402) | copy-start | bytes 24580
  40.0 11.7 copy-start.95
  40.6 74.4 %copy-start.73 = (f32[2048]{0:T(1024)}, f32[2048]{0:T(1024)S(1)}, u32[]{:S(2)}) copy-start(f32[2048]{0:T(1024)S(1)} %get-tuple-element.406) | copy-start | bytes 24580
  51.9 17.1 copy-start.42
  57.8 15.9 copy-start.114
  57.8 21.1 %copy-start.115 = (bf16[512]{0:T(512)(128)(2,1)S(1)}, bf16[512]{0:T(512)(128)(2,1)}, u32[]{:S(2)}) copy-start(bf16[512]{0:T(512)(128)(2,1)} %param.35) | copy-start | bytes 3076
  57.8 26.4 %copy-start.116 = (bf16[512]{0:T(512)(128)(2,1)S(1)}, bf16[512]{0:T(512)(128)(2,1)}, u32[]{:S(2)}) copy-start(bf16[512]{0:T(512)(128)(2,1)} %param.33) | copy-start | bytes 3076
  69.0 20.4 collective-permute-start
  79.0 36.1 %copy-start.83 = (f32[4,1,512]{2,1,0:T(1,128)}, f32[4,1,512]{2,1,0:T(1,128)S(1)}, u32[]{:S(2)}) copy-start(f32[4,1,512]{2,1,0:T(1,128)S(1)} %convert_element_type.219) | copy-start | bytes 24580
  84.2 30.8 %copy-start.65 = (f32[4,1,512]{2,1,0:T(1,128)}, f32[4,1,512]{2,1,0:T(1,128)S(1)}, u32[]{:S(2)}) copy-start(f32[4,1,512]{2,1,0:T(1,128)S(1)} %convert_element_type.223) | copy-start | bytes 24580
  89.4 25.6 %copy-start.67 = (f32[4,1,512]{2,1,0:T(1,128)}, f32[4,1,512]{2,1,0:T(1,128)S(1)}, u32[]{:S(2)}) copy-start(f32[4,1,512]{2,1,0:T(1,128)S(1)} %convert_element_type.221) | copy-start | bytes 24580
  89.8 25.2 %copy-start = (f32[2,131,2048]{2,1,0:T(8,128)}, f32[2,131,2048]{2,1,0:T(8,128)S(1)}, u32[]{:S(2)}) copy-start(f32[2,131,2048]{2,1,0:T(8,128)S(1)} %maximum_convert_fusion) | copy-start | bytes 6438916
  93.9 10.7 copy-start.9
  121.1 11.3 copy-start.4
  240.5 47.1 %copy-start.21 = (f32[2,128,2048]{2,1,0:T(8,128)}, f32[2,128,2048]{2,1,0:T(8,128)S(1)}, u32[]{:S(2)}) copy-start(f32[2,128,2048]{2,1,0:T(8,128)S(1)} %pad.226) | copy-start | bytes 6291460
  255.5 74.3 %copy-start.33 = (f32[2,64,2048]{2,1,0:T(8,128)S(1)}, f32[2,64,2048]{2,1,0:T(8,128)}, u32[]{:S(2)}) copy-start(f32[2,64,2048]{2,1,0:T(8,128)} %slice.607) | copy-start | bytes 3145732
  320.7 14.3 copy-start.32
  366.5 11.0 copy-start.40
  449.1 32.6 %copy-start.24 = (f32[256,1536]{1,0:T(8,128)}, f32[256,1536]{1,0:T(8,128)S(1)}, u32[]{:S(2)}) copy-start(f32[256,1536]{1,0:T(8,128)S(1)} %get-tuple-element.414) | copy-start | bytes 4718596
  483.7 163.1 %copy-start.11 = (f32[256,1536]{1,0:T(8,128)}, f32[256,1536]{1,0:T(8,128)S(1)}, u32[]{:S(2)}) copy-start(f32[256,1536]{1,0:T(8,128)S(1)} %fusion.46) | copy-start | bytes 4718596
  576.0 13.9 copy-start.71
  576.0 13.9 copy-start.72
  578.1 11.8 copy-start.105
  579.7 10.6 copy-start.104
  607.7 12.0 copy-start.49
  610.7 11.2 copy-start.98
  653.2 16.8 copy-start.34
  680.1 47.9 %copy-start.57 = (f32[2,2048]{1,0:T(2,128)S(1)}, f32[2,2048]{1,0:T(2,128)}, u32[]{:S(2)}) copy-start(f32[2,2048]{1,0:T(2,128)} %custom-call) | copy-start | bytes 49156
  680.1 54.3 %copy-start.1 = (f32[2,131,2048]{2,1,0:T(8,128)S(1)}, f32[2,131,2048]{2,1,0:T(8,128)}, u32[]{:S(2)}) copy-start(f32[2,131,2048]{2,1,0:T(8,128)} %copy-done) | copy-start | bytes 6438916
  680.1 54.3 %copy-start.66 = (f32[4,1,512]{2,1,0:T(1,128)S(1)}, f32[4,1,512]{2,1,0:T(1,128)}, u32[]{:S(2)}) copy-start(f32[4,1,512]{2,1,0:T(1,128)} %copy-done.65) | copy-start | bytes 24580
  680.1 54.4 %copy-start.68 = (f32[4,1,512]{2,1,0:T(1,128)S(1)}, f32[4,1,512]{2,1,0:T(1,128)}, u32[]{:S(2)}) copy-start(f32[4,1,512]{2,1,0:T(1,128)} %copy-done.67) | copy-start | bytes 24580
  680.1 54.4 %copy-start.74 = (f32[2048]{0:T(1024)S(1)}, f32[2048]{0:T(1024)}, u32[]{:S(2)}) copy-start(f32[2048]{0:T(1024)} %copy-done.73) | copy-start | bytes 24580
  680.1 54.4 %copy-start.76 = (f32[1,2048]{1,0:T(1,128)S(1)}, f32[1,2048]{1,0:T(1,128)}, u32[]{:S(2)}) copy-start(f32[1,2048]{1,0:T(1,128)} %copy-done.75) | copy-start | bytes 24580
  680.1 54.4 %copy-start.78 = (f32[1,2048]{1,0:T(1,128)S(1)}, f32[1,2048]{1,0:T(1,128)}, u32[]{:S(2)}) copy-start(f32[1,2048]{1,0:T(1,128)} %copy-done.77) | copy-start | bytes 24580
  680.2 54.4 %copy-start.80 = (f32[1,2048]{1,0:T(1,128)S(1)}, f32[1,2048]{1,0:T(1,128)}, u32[]{:S(2)}) copy-start(f32[1,2048]{1,0:T(1,128)} %copy-done.79) | copy-start | bytes 24580
  680.2 54.4 %copy-start.82 = (f32[1,2048]{1,0:T(1,128)S(1)}, f32[1,2048]{1,0:T(1,128)}, u32[]{:S(2)}) copy-start(f32[1,2048]{1,0:T(1,128)} %copy-done.81) | copy-start | bytes 24580
  680.2 54.4 %copy-start.84 = (f32[4,1,512]{2,1,0:T(1,128)S(1)}, f32[4,1,512]{2,1,0:T(1,128)}, u32[]{:S(2)}) copy-start(f32[4,1,512]{2,1,0:T(1,128)} %copy-done.83) | copy-start | bytes 24580
  680.2 54.4 %copy-start.94 = (f32[2048]{0:T(1024)S(1)}, f32[2048]{0:T(1024)}, u32[]{:S(2)}) copy-start(f32[2048]{0:T(1024)} %get-tuple-element.407) | copy-start | bytes 24580
  680.2 54.4 %copy-start.97 = (f32[2,1,2048]{2,1,0:T(1,128)S(1)}, f32[2,1,2048]{2,1,0:T(1,128)}, u32[]{:S(2)}) copy-start(f32[2,1,2048]{2,1,0:T(1,128)} %broadcast_in_dim.32) | copy-start | bytes 49156
  783.2 297.5 %reduce-scatter.18.cloned.1.call-start = ((), (), s32[]{:S(2)}) async-start(), calls=%async_computation.15 | async-start | bytes 15138816
  838.0 496.9 %reduce-scatter.10.cloned.1.call-start = ((), (), s32[]{:S(2)}) async-start(), calls=%async_computation.11 | async-start | bytes 25952256 | tf_op jit(solution)/shard_map/reduce_scatter | solution.py:318
  841.8 5.9 collective-permute-start.1
  848.2 10.3 copy-start.19
  858.5 955.8 %reduce-scatter.12.cloned.1.call-start = ((), (), s32[]{:S(2)}) async-start(), calls=%async_computation.12 | async-start | bytes 58392576 | tf_op jit(solution)/shard_map/reduce_scatter | solution.py:240
  882.5 1202.8 %reduce-scatter.14.cloned.1.call-start = ((), (), s32[]{:S(2)}) async-start(), calls=%async_computation.13 | async-start | bytes 29196288 | tf_op jit(solution)/shard_map/reduce_scatter | solution.py:245
  903.0 52.5 %copy-start.110 = (f32[2,128]{1,0:T(2,128)S(1)}, f32[2,128]{1,0:T(2,128)}, u32[]{:S(2)}) copy-start(f32[2,128]{1,0:T(2,128)} %copy-done.109) | copy-start | bytes 3076
  903.0 52.5 %copy-start.12 = (f32[256,1536]{1,0:T(8,128)S(1)}, f32[256,1536]{1,0:T(8,128)}, u32[]{:S(2)}) copy-start(f32[256,1536]{1,0:T(8,128)} %copy-done.11) | copy-start | bytes 4718596
  (70 other events, 255.7 us)
Sparse Core Ops, SparseCore 0:
  9.6 54.7 all-gather.15
  66.0 46.5 all-gather.17
  114.1 46.3 all-gather.19
  161.9 91.0 all-gather.23
  254.4 91.0 all-gather.21
  346.9 91.0 all-gather.25
  783.4 134.6 reduce-scatter.15
  920.5 160.2 reduce-scatter.17
  1088.3 246.5 reduce-scatter.9
  1341.2 473.0 reduce-scatter.11
  1822.4 262.7 reduce-scatter.13
where the time goes:
time: 2110 us; the launch traced here: 2090 us
  waiting for transfers between devices  1180 us (56%)
  local copies, waits for them, and re-layouts  372 us (18%)
  blocking collectives  194 us (9%)
  matrix products  184 us (9%)
  other arithmetic  140 us (7%)
    reduce_scatter x1, waiting for transfers between devices, body(): lax.psum_scatter(matmul_left_t(normed_two, grad_upvalue), ('seq', 'fsdp')...  477 us
    reduce_scatter x1, waiting for transfers between devices, body(): lax.psum_scatter(matmul_left_t(hidden_low, grad_down_in), ('seq', 'fsdp')...  268 us
    reduce_scatter x1, waiting for transfers between devices, body(): lax.psum_scatter(matmul_left_t(normed, grad_gatebranch), ('seq', 'fsdp'),...  251 us
    unnamed x13, waiting for transfers between devices  124 us
    slice x49, local copies, waits for them, and re-layouts, body(): lax.associative_scan(linear_step, (next_decay, grad_states), axis=1, reve...  117 us
    slice x44, local copies, waits for them, and re-layouts, body(): lax.associative_scan(linear_step, (decay_now, pushed), axis=1)  76.2 us
    dot_general x6, matrix products, matmul_left_t(): lax.dot_general(left, right, (((0,), (0,)), ((), ())), preferred_element_...  68.9 us
    all_gather x2, blocking collectives, entering(): lax.all_gather(a.astype(kind), axis)  61 us
  transfers between devices with their start and end apart: 13, of which 7 were waited for; matrix products, arithmetic and copies ran while one was open for 18% of the time, Pallas kernels for 0%

commit v1 on v0

v1 whole, which is shorter than its diff:
```python
import jax
import jax.numpy as jnp
from jax import lax
from jax.sharding import PartitionSpec as P
from jax.experimental import pallas as pl
from jax.experimental.pallas import tpu as pltpu

EPS_NORM = 1e-06
EPS_MULT = 0.0001
RATE_SCALE = 8.0
BF = jnp.bfloat16
F32 = jnp.float32
GROUP = "fsdp"
BOTH = ("seq", "fsdp")


def mm(left, right):
    return jnp.dot(left, right, preferred_element_type=F32)


def mm_lt(left, right):
    return lax.dot_general(left, right, (((0,), (0,)), ((), ())), preferred_element_type=F32)


def mm_rt(left, right):
    return lax.dot_general(left, right, (((1,), (1,)), ((), ())), preferred_element_type=F32)


def gelu_pair(v):
    c = 0.7978845608028654
    a = 0.044715
    u = c * (v + a * v * v * v)
    t = jnp.tanh(u)
    g = 0.5 * v * (1.0 + t)
    d = 0.5 * (1.0 + t) + 0.5 * v * (1.0 - t * t) * c * (1.0 + 3.0 * a * v * v)
    return g, d


def linear_step(first_pair, second_pair):
    return (first_pair[0] * second_pair[0], second_pair[1] + second_pair[0] * first_pair[1])


def rms(v, g):
    s = lax.rsqrt(jnp.mean(v * v, axis=-1, keepdims=True) + EPS_NORM)
    return (v * s * g).astype(BF), s


def rms_back(v, s, g, grad):
    gg = grad * g
    gain = jnp.sum(grad * v * s, axis=0)
    return s * gg - v * (s * s * s) * jnp.mean(gg * v, axis=-1, keepdims=True), gain


def ag(a):
    return lax.all_gather(a, GROUP, axis=0, tiled=True)


def rs(a):
    return lax.psum_scatter(a.astype(BF), GROUP, scatter_dimension=0, tiled=True).astype(F32)


def grads_cols(g):
    part = lax.psum_scatter(g.astype(BF), "seq", scatter_dimension=0, tiled=True)
    return lax.all_to_all(part, GROUP, split_axis=0, concat_axis=1, tiled=True).astype(F32)


def grads_rows(g):
    n, m = lax.axis_size("seq"), lax.axis_size(GROUP)
    part = lax.psum_scatter(g.astype(BF), "seq", scatter_dimension=0, tiled=True)
    pairs = [(j * m + f, f * n + j) for j in range(n) for f in range(m)]
    return lax.ppermute(part, BOTH, pairs).astype(F32)


def shifted(shard, axis, by):
    length = lax.axis_size(axis)
    pairs = [(i, i + by) for i in range(length) if 0 <= i + by < length]
    return lax.ppermute(shard, axis, pairs)


MESH = pl.DeviceIdType.MESH
VMEM = pl.BlockSpec(memory_space=pltpu.VMEM)
ANY = pl.BlockSpec(memory_space=pl.ANY)
LIMIT = 60 * 2**20


def ds(start, size):
    if not isinstance(start, int):
        start = pl.multiple_of(start, size if size % 128 else 128)
    return pl.ds(start, size)


def rows_at(block, size):
    return pl.ds(pl.multiple_of(block * size, size), size)


class Place:
    def __init__(self):
        self.n = lax.axis_size("seq")
        self.s, self.f = lax.axis_index("seq"), lax.axis_index("fsdp")
        f = self.f
        self.p1 = f + 1 - 2 * lax.rem(f, 2)
        self.p2 = lax.rem(f + 2, 4)
        self.p3 = lax.rem(self.p1 + 2, 4)
        self.sx = self.s + 1 - 2 * lax.rem(self.s, 2)

    def group(self, f):
        return (self.s, f)

    def line(self, s):
        return (s, self.f)

    def greet(self, whole_line=True):
        barrier = pltpu.get_barrier_semaphore()
        for f in (self.p1, self.p2, self.p3):
            pl.semaphore_signal(barrier, inc=1, device_id=self.group(f), device_id_type=MESH)

        def one(j, _):
            pl.semaphore_signal(
                barrier, inc=1, device_id=self.line(lax.rem(self.s + j, self.n)), device_id_type=MESH
            )
            return 0

        lax.fori_loop(1, self.n, one, 0)
        pl.semaphore_wait(barrier, 3 + self.n - 1)


class Sems:
    def __init__(self, ref):
        self.ref, self.used = ref, 0

    def take(self):
        self.used += 1
        return self.ref.at[self.used - 1]

    def remote(self, src, dst, device):
        return pltpu.make_async_remote_copy(
            src_ref=src, dst_ref=dst, send_sem=self.take(), recv_sem=self.take(),
            device_id=device, device_id_type=MESH,
        )

    def local(self, src, dst):
        copy = pltpu.make_async_copy(src, dst, self.take())
        copy.start()
        return copy


class Gather:
    def __init__(self, at, sems, buf, chunk):
        self.at, self.buf, self.chunk = at, buf, chunk
        mine = lambda f, r: buf.at[rows_at(f * 2 + r, chunk)]
        self.core = [sems.remote(mine(at.f, r), mine(at.f, r), at.group(at.p1)) for r in range(2)]
        self.over = [sems.remote(mine(at.f, r), mine(at.f, r), at.group(at.p2)) for r in range(2)]
        self.pass_on = [sems.remote(mine(at.p2, r), mine(at.p2, r), at.group(at.p1)) for r in range(2)]

    def send(self, r):
        self.over[r].start()
        self.core[r].start()

    def relay(self, r):
        self.over[r].wait_recv()
        self.pass_on[r].start()

    def finish(self):
        for r in range(2):
            self.core[r].wait()
            self.over[r].wait_send()
            self.pass_on[r].wait()


class Scatter:
    def __init__(self, at, sems, core_out, core_in, over_out, over_in, chunk):
        self.at, self.chunk = at, chunk
        self.core_out, self.core_in, self.over_out, self.over_in = core_out, core_in, over_out, over_in
        self.core = [sems.remote(core_out.at[k], core_in.at[k], at.group(at.p1)) for k in range(2)]
        self.over = [
            sems.remote(
                over_out.at[pl.ds(r * chunk, chunk)], over_in.at[pl.ds(r * chunk, chunk)], at.group(at.p2)
            )
            for r in range(2)
        ]

    def run(self, partial, own, between=lambda k: None):
        at = self.at

        def put(ref):
            def store(sl, cols, tile):
                ref[sl, cols] = tile.astype(BF)

            return store

        partial(at.p3, put(self.core_out.at[0]))
        self.core[0].start()
        between(0)

        def add_over(sl, cols, tile):
            self.over_out[sl, cols] = (tile + self.core_in[0, sl, cols].astype(F32)).astype(BF)

        self.core[0].wait_recv()
        partial(at.p2, add_over)
        for r in range(2):
            self.over[r].start()
        between(1)
        partial(at.p1, put(self.core_out.at[1]))
        self.core[1].start()
        between(2)
        self.core[1].wait_recv()

        def add_own(sl, cols, tile):
            own[sl, cols] = own[sl, cols] + tile + self.core_in[1, sl, cols].astype(F32)

        partial(at.f, add_own)
        between(3)

    def arrived(self, r):
        self.over[r].wait_recv()
        return self.over_in[pl.ds(r * self.chunk, self.chunk), :].astype(F32)

    def finish(self):
        for copy in self.core + self.over:
            copy.wait_send()


class Columns:
    def __init__(self, at, sems, weights, buf):
        self.at = at
        rows, width = weights[0].shape
        part = width // 4
        half = rows // 2
        h = lax.rem(at.s, 2)
        self.half, self.rows, self.part, self.buf, self.sems = half, rows, part, buf, sems
        self.near, self.own, self.far, self.side = [], [], [], []
        for k, w in enumerate(weights):
            cols = pl.ds(k * part, part)
            take = lambda f: pl.ds(pl.multiple_of(f * part, 128), part)
            mine = pl.ds(pl.multiple_of(at.f * rows, rows), rows)
            cut = pl.ds(pl.multiple_of(h * half, half), half)
            mine_cut = pl.ds(pl.multiple_of(at.f * rows + h * half, half), half)
            self.own.append(pltpu.make_async_copy(w.at[:, take(at.f)], buf.at[mine, cols], sems.take()))
            self.near.append(sems.remote(w.at[:, take(at.p1)], buf.at[mine, cols], at.group(at.p1)))
            for p in (at.p2, at.p3):
                self.far.append(sems.remote(w.at[cut, take(p)], buf.at[mine_cut, cols], at.group(p)))
                came = buf.at[pl.ds(pl.multiple_of(p * rows + h * half, half), half), cols]
                self.side.append(sems.remote(came, came, at.line(at.sx)))

    def start_far(self):
        for c in self.far:
            c.start()

    def start_near(self):
        for c in self.near + self.own:
            c.start()

    def relay(self, k):
        self.far[k].wait_recv()
        self.side[k].start()

    def finish(self):
        for c in self.own + self.near + self.side:
            c.wait()
        for c in self.far:
            c.wait_send()


def expm1_neg(v):
    series = v * (1 + v * (1 / 2) * (1 + v * (1 / 3) * (1 + v * (1 / 4) * (1 + v * (1 / 5) * (1 + v * (1 / 6))))))
    return jnp.where(v > -0.25, series, jnp.exp(v) - 1.0)


def swap_rows(src, dst, outer, kind):
    total, width = src.shape
    inner = total // outer

    def one(c, _):
        cols = pl.ds(pl.multiple_of(c * 128, 128), 128)
        v = src[:, cols].reshape(outer, inner, 128)
        dst[:, cols] = jnp.swapaxes(v, 0, 1).reshape(total, 128).astype(kind)
        return 0

    lax.fori_loop(0, width // 128, one, 0)


def forward_branch(x, gains, chan, wr, wl, wo, wg, wi, wu, wv,
                   wgi_o, wuv_o, normed_o, n2_o, middle_o, gate_o, pad_o, conv_o, rate_o, inlet_o, decay_o, states_o,
                   merged_o, ends_o, gain_o,
                   wgi, normed, n2, middle, gain, gate, pad, conv, rate, inlet, decay, states, work, merged, ends,
                   tot, core_out, core_in, over_out, over_in, sem, tsend, trecv):
    at = Place()
    here, width = x.shape
    toks = here // 2
    chans = chan.shape[1]
    part = width // 4
    taps = 4
    steps = toks
    group = 8
    halo = (taps - 1) * group
    sems = Sems(sem)
    at.greet()

    shares = [
        sems.remote(gains, gain.at[at.f], at.group(p)) for p in (at.p1, at.p2, at.p3)
    ]
    for c in shares:
        c.start()
    gain[at.f] = gains[...]
    gi = Columns(at, sems, [wg, wi], wgi)
    gi.start_far()
    gi.start_near()
    uv = Columns(at, sems, [wu, wv], wuv_o)
    uv.start_near()
    ag1 = Gather(at, sems, normed, toks)
    for c in shares:
        c.wait()
    for r in range(2):
        sl = pl.ds(r * toks, toks)
        v = x[sl, :]
        scale = lax.rsqrt(jnp.mean(v * v, axis=-1, keepdims=True) + EPS_NORM)
        for p in range(4):
            cols = pl.ds(p * part, part)
            normed[rows_at(at.f * 2 + r, toks), cols] = (x[sl, cols] * scale * gain[p, 0:1, :]).astype(BF)
        ag1.send(r)
    for k in range(4):
        gi.relay(k)
    ag1.relay(0)
    uv.start_far()
    ag1.relay(1)
    ag1.finish()
    gi.finish()
    saves = [sems.local(normed, normed_o), sems.local(wgi, wgi_o), sems.local(gain, gain_o)]

    def branch_rows(m, _):
        sl = rows_at(m, here)
        work[sl, :] = mm(normed[sl, :], wgi[:, chans:]).astype(BF).astype(F32)
        return 0

    lax.fori_loop(0, 4, branch_rows, 0)
    swap_rows(work, pad.at[pl.ds(halo, steps * group)], group, F32)
    edge = pad.at[pl.ds(steps * group, halo)]
    next_one = lax.rem(at.s + 1, at.n)
    tail = sems.remote(edge, pad.at[pl.ds(0, halo)], at.line(next_one))

    @pl.when(at.s < at.n - 1)
    def _():
        tail.start()

    @pl.when(at.s == 0)
    def _():
        pad[0:halo, :] = jnp.zeros((halo, chans), F32)

    def gate_rows(m, _):
        sl = rows_at(m, here)
        work[sl, :] = mm(normed[sl, :], wgi[:, :chans])
        return 0

    lax.fori_loop(0, 4, gate_rows, 0)
    swap_rows(work, gate, group, F32)

    @pl.when(at.s > 0)
    def _():
        tail.wait_recv()

    @pl.when(at.s < at.n - 1)
    def _():
        tail.wait_send()

    uv.relay(0)

    def gates(b, _):
        for h in range(chans // 128):
            cols = pl.ds(h * 128, 128)
            size = 128
            start = pl.multiple_of(b * size, size)
            sl = pl.ds(start, size)
            total = chan[taps : taps + 1, cols]
            for k in range(taps):
                total = total + chan[k : k + 1, cols] * pad[pl.ds(start + (halo - group * k), size), cols]
            low = total.astype(BF)
            blocks = pl.ds(h * 128, 128)
            r = jax.nn.sigmoid(mm(low, wr[blocks, :]) + chan[5:6, cols])
            i = jax.nn.sigmoid(mm(low, wl[blocks, :]) + chan[6:7, cols])
            ld = r * chan[7:8, cols]
            low = low.astype(F32)
            decay[sl, cols] = jnp.exp(ld)
            work[sl, cols] = jnp.sqrt(EPS_MULT - expm1_neg(2.0 * ld)) * i * low
            conv[sl, cols] = low
            rate[sl, cols] = r
            inlet[sl, cols] = i
        return 0

    lax.fori_loop(0, steps * group // 128, gates, 0)
    saves += [
        sems.local(gate, gate_o), sems.local(pad, pad_o), sems.local(conv, conv_o), sems.local(rate, rate_o),
        sems.local(inlet, inlet_o), sems.local(decay, decay_o),
    ]

    unroll = 8

    def totals(b, carry):
        h, p = carry
        for u in range(unroll):
            sl = pl.ds(pl.multiple_of((b * unroll + u) * group, group), group)
            a = decay[sl, :]
            h = a * h + work[sl, :]
            p = p * a
        return h, p

    zero = jnp.zeros((group, chans), F32)
    h, p = lax.fori_loop(0, steps // unroll, totals, (zero, zero + 1.0))
    ends[0:8, :] = p
    ends[8:16, :] = h

    def total_copy(src, to):
        return pltpu.make_async_remote_copy(
            src_ref=ends.at[pl.ds(0, 16)], dst_ref=tot.at[src], send_sem=tsend.at[to], recv_sem=trecv.at[src],
            device_id=at.line(to), device_id_type=MESH,
        )

    def send_total(j, _):
        total_copy(at.s, j).start()
        return 0

    lax.fori_loop(at.s + 1, at.n, send_total, 0)
    uv.relay(1)

    def enter(j, state):
        total_copy(j, j).wait_recv()
        return tot[j, 0:8, :] * state + tot[j, 8:16, :]

    state_in = lax.fori_loop(0, at.s, enter, zero)

    def sent_total(j, _):
        total_copy(at.s, j).wait_send()
        return 0

    lax.fori_loop(at.s + 1, at.n, sent_total, 0)
    ends[16:24, :] = state_in

    def scan(b, h):
        for u in range(unroll):
            sl = pl.ds(pl.multiple_of((b * unroll + u) * group, group), group)
            h = decay[sl, :] * h + work[sl, :]
            states[sl, :] = h
        return h

    lax.fori_loop(0, steps // unroll, scan, state_in)
    saves += [sems.local(states, states_o), sems.local(ends, ends_o)]

    def merge(c, _):
        cols = pl.ds(pl.multiple_of(c * 128, 128), 128)

        def some(b, _):
            sl = rows_at(b, 128)
            work[sl, cols] = states[sl, cols] * gelu_pair(gate[sl, cols])[0]
            return 0

        lax.fori_loop(0, steps * group // 128, some, 0)
        return 0

    lax.fori_loop(0, chans // 128, merge, 0)
    swap_rows(work, merged, steps, BF)
    saves += [sems.local(merged, merged_o)]

    middle[...] = x[...]
    sc = Scatter(at, sems, core_out, core_in, over_out, over_in, toks)

    def partial(o, store):
        def half(r, _):
            sl = rows_at(r, toks)
            tile = mm(merged[rows_at(o * 2 + r, toks), :], wo[...])
            store(sl, slice(None), tile)
            return 0

        lax.fori_loop(0, 2, half, 0)

    sc.run(partial, middle)
    ag2 = Gather(at, sems, n2, toks)
    for r in range(2):
        sl = pl.ds(r * toks, toks)
        v = middle[sl, :] + sc.arrived(r)
        middle[sl, :] = v
        scale = lax.rsqrt(jnp.mean(v * v, axis=-1, keepdims=True) + EPS_NORM)
        for p in range(4):
            cols = pl.ds(p * part, part)
            n2[rows_at(at.f * 2 + r, toks), cols] = (middle[sl, cols] * scale * gain[p, 1:2, :]).astype(BF)
        ag2.send(r)
    saves += [sems.local(middle, middle_o)]
    uv.relay(2)
    uv.relay(3)
    for r in range(2):
        ag2.relay(r)
    ag2.finish()
    sc.finish()
    saves += [sems.local(n2, n2_o)]
    uv.finish()
    for c in saves:
        c.wait()


def call_forward(x, gains, chan, wr, wl, wo, wg, wi, wu, wv):
    here, width = x.shape
    chans = chan.shape[1]
    ffl = wu.shape[1] // 4
    every = here * 4
    n = lax.axis_size("seq")
    f32 = lambda *s: jax.ShapeDtypeStruct(s, F32)
    bf = lambda *s: jax.ShapeDtypeStruct(s, BF)
    vf = lambda *s: pltpu.VMEM(s, F32)
    vb = lambda *s: pltpu.VMEM(s, BF)
    outs = [
        bf(width, 2 * chans), bf(width, 2 * ffl), bf(every, width), bf(every, width), f32(here, width),
        f32(every, chans), f32(every + 24, chans), f32(every, chans), f32(every, chans), f32(every, chans),
        f32(every, chans), f32(every, chans), bf(every, chans), f32(24, chans), f32(4, 8, width // 4),
    ]
    scratch = [
        vb(width, 2 * chans), vb(every, width), vb(every, width), vf(here, width), vf(4, 8, width // 4),
        vf(every, chans), vf(every + 24, chans), vf(every, chans), vf(every, chans), vf(every, chans),
        vf(every, chans), vf(every, chans), vf(every, chans), vb(every, chans), vf(24, chans),
        vf(n, 16, chans), vb(2, here, width), vb(2, here, width), vb(here, width), vb(here, width),
        pltpu.SemaphoreType.DMA((120,)), pltpu.SemaphoreType.DMA((n,)), pltpu.SemaphoreType.DMA((n,)),
    ]
    return pl.pallas_call(
        forward_branch,
        out_shape=outs,
        in_specs=[VMEM] * 6 + [ANY] * 4,
        out_specs=[ANY] * len(outs),
        scratch_shapes=scratch,
        compiler_params=pltpu.CompilerParams(collective_id=1, has_side_effects=True, vmem_limit_bytes=LIMIT),
        name="forward_branch",
    )(x, gains, chan, wr, wl, wo, wg, wi, wu, wv)


def body(
    block_input, teacher, valid_lengths, norm_gain, w_gate, w_input, conv_weight, conv_bias,
    w_rate, bias_rate, w_inlet, bias_inlet, decay_param, w_out, mlp_gain, w_up, w_value, w_down,
):
    n_seq, n_fs = lax.axis_size("seq"), lax.axis_size(GROUP)
    si, fi = lax.axis_index("seq"), lax.axis_index(GROUP)
    rows_dev, toks, width = block_input.shape
    rows = rows_dev * n_fs
    here = rows_dev * toks
    chans = conv_bias.shape[0]
    hb = w_rate.shape[1]
    heads = chans // hb
    taps = conv_weight.shape[0]

    cw = conv_weight.astype(F32)
    heads_shape = (heads, hb, hb)
    wr, wl = w_rate.reshape(heads_shape), w_inlet.reshape(heads_shape)
    sp = jax.nn.softplus(-decay_param.astype(F32))
    x = block_input.reshape(here, width)
    gains = jnp.concatenate([norm_gain[None].astype(F32), mlp_gain[None].astype(F32), jnp.zeros((6, width // 4), F32)])
    vec = lambda v: v.astype(F32)[None]
    chan = jnp.concatenate([cw, vec(conv_bias), vec(bias_rate), vec(bias_inlet), vec(-RATE_SCALE * sp), jnp.zeros((8, chans), F32)])
    (wgi, wuv, normed, n2, middle, gate_tm, pad_tm, conv_tm, rate_tm, inlet_tm, decay_tm, states_tm, merged, ends, gain) = call_forward(
        x, gains, chan, w_rate, w_inlet, w_out, w_gate, w_input, w_up, w_value)
    wg, wi = wgi[:, :chans], wgi[:, chans:]
    wu, wv = wuv[:, :wuv.shape[1]//2], wuv[:, wuv.shape[1]//2:]
    gain_one, gain_two = gain[:, 0].reshape(-1), gain[:, 1].reshape(-1)
    s1 = lax.rsqrt(jnp.mean(x * x, axis=-1, keepdims=True) + EPS_NORM)
    s2 = lax.rsqrt(jnp.mean(middle * middle, axis=-1, keepdims=True) + EPS_NORM)
    tok = lambda v: v.reshape(-1, rows, chans).swapaxes(0, 1)
    padded, clf, r, i, decay, states = tok(pad_tm), tok(conv_tm), tok(rate_tm), tok(inlet_tm), tok(decay_tm), tok(states_tm)
    conv_low = clf.astype(BF)
    heads_in = conv_low.reshape(rows * toks, heads, hb)
    gate_pre = tok(gate_tm).reshape(-1, chans)
    gg, gd = gelu_pair(gate_pre)
    cum_end, state_in = ends[:8], ends[16:24]
    prev = jnp.concatenate([state_in[:, None], states[:, :-1]], axis=1)
    ld = -RATE_SCALE * r * sp
    factor = jnp.sqrt(EPS_MULT - jnp.expm1(2.0 * ld))
    up = mm(n2, wu)
    value = mm(n2, wv)
    vg, vd = gelu_pair(value)
    hidden = (vg * up).astype(BF)
    result = middle + rs(mm(hidden, w_down))
    lens = lax.dynamic_slice_in_dim(valid_lengths, fi * rows_dev, rows_dev)
    pos = si * toks + jnp.arange(toks, dtype=jnp.int32)
    mask = (pos[None, :] < lens[:, None]).reshape(here, 1)
    slots = valid_lengths.shape[0] * toks * n_seq
    count = jnp.sum(valid_lengths).astype(F32)
    grad_out = jnp.where(mask, result - teacher.reshape(here, width), 0.0) * (slots / count)
    gdi = ag(grad_out.astype(BF))
    g_down = mm_lt(hidden, gdi)
    gh = mm_rt(gdi, w_down)
    gu = (gh * vg).astype(BF)
    gv = (gh * up * vd).astype(BF)
    g_up = mm_lt(n2, gu)
    g_value = mm_lt(n2, gv)
    gn2 = rs(mm_rt(gu, wu) + mm_rt(gv, wv))
    gm_norm, gain2 = rms_back(middle, s2, gain_two, gn2)
    grad_middle = grad_out + gm_norm
    gml = ag(grad_middle.astype(BF))
    g_out = mm_lt(merged, gml)
    gmer = mm_rt(gml, w_out)
    gst = (gmer * gg).reshape(rows, toks, chans)
    ggate = (gmer * states.reshape(-1, chans) * gd).astype(BF)
    nextd = jnp.concatenate([decay[:, 1:], jnp.ones((rows, 1, chans), F32)], axis=1)
    carry, ladj = lax.associative_scan(linear_step, (nextd, gst), axis=1, reverse=True)
    tot2 = lax.all_gather(jnp.stack([cum_end, decay[:, 0] * ladj[:, 0]]), "seq")
    adj_in = jnp.zeros((rows, chans), F32)
    for j in reversed(range(n_seq)):
        adj_in = jnp.where(j > si, tot2[j, 0] * adj_in + tot2[j, 1], adj_in)
    adj = ladj + carry * adj_in[:, None]
    gdec = adj * prev
    gfac = adj * i * clf
    gld = gdec * decay - gfac * (decay * decay) / factor
    grate = gld * (-RATE_SCALE * sp) * r * (1.0 - r)
    ginl = adj * factor * clf * i * (1.0 - i)
    gdp = jnp.sum(gld * r, axis=(0, 1)) * RATE_SCALE * jax.nn.sigmoid(-decay_param.astype(F32))
    gcd = adj * factor * i
    grb, gib = jnp.sum(grate, (0, 1)), jnp.sum(ginl, (0, 1))
    grl, gil = grate.astype(BF).reshape(-1, heads, hb), ginl.astype(BF).reshape(-1, heads, hb)
    gwr = jnp.einsum("nhi,nhj->hij", heads_in, grl, preferred_element_type=F32).reshape(chans, hb)
    gwi = jnp.einsum("nhi,nhj->hij", heads_in, gil, preferred_element_type=F32).reshape(chans, hb)
    bk = lambda a, w: jnp.einsum("nhj,hij->nhi", a, w, preferred_element_type=F32).reshape(rows, toks, chans)
    gconv = gcd + bk(grl, wr) + bk(gil, wl)
    gcw = jnp.stack([jnp.sum(gconv * padded[:, taps - 1 - k: taps - 1 - k + toks], (0, 1)) for k in range(taps)])
    gcb = jnp.sum(gconv, (0, 1))
    gpad = jnp.zeros((rows, toks + taps - 1, chans), F32)
    for k in range(taps):
        gpad = gpad.at[:, taps - 1 - k: taps - 1 - k + toks].add(cw[k] * gconv)
    edge = shifted(gpad[:, : taps - 1], "seq", -1)
    gbr = gpad[:, taps - 1:].at[:, toks - (taps - 1):].add(edge).reshape(-1, chans).astype(BF)
    g_gate = mm_lt(normed, ggate)
    g_input = mm_lt(normed, gbr)
    gn1 = rs(mm_rt(ggate, wg) + mm_rt(gbr, wi))
    gi_norm, gain1 = rms_back(x, s1, gain_one, gn1)
    grad_input = grad_middle + gi_norm

    chan = jnp.concatenate([gcw, gcb[None], grb[None], gib[None], gdp[None]], 0)
    per = chans // n_seq
    chan = chan.reshape(8, n_seq, per).transpose(1, 0, 2).reshape(n_seq, 8 * per)
    blk = jnp.zeros((n_fs, n_seq, 8 * per), F32).at[fi].set(chan).reshape(n_fs * n_seq, 8 * per)
    gw = jnp.stack([gain1, gain2]).reshape(2, n_fs * n_seq, -1).transpose(1, 0, 2).reshape(n_fs * n_seq, -1)
    small = lax.psum_scatter(jnp.concatenate([blk, gw], 1), BOTH, scatter_dimension=0, tiled=True)[0]
    ch = small[: 8 * per].reshape(8, per)
    gn = small[8 * per:].reshape(2, -1)
    og = grads_rows(jnp.concatenate([g_out, gwr, gwi], 1))
    return (
        result.reshape(block_input.shape), grad_input.reshape(block_input.shape), gn[0],
        grads_cols(g_gate), grads_cols(g_input), ch[:4], ch[4], og[:, width: width + hb], ch[5],
        og[:, width + hb:], ch[6], ch[7], og[:, :width], gn[1], grads_cols(g_up), grads_cols(g_value), grads_rows(g_down),
    )


def solution(mesh):
    rowsh, vec, mat = P("fsdp", "seq", None), P("fsdp"), P("fsdp", None)
    ov, om = P(BOTH), P(BOTH, None)
    return jax.shard_map(
        body,
        mesh=mesh,
        in_specs=(rowsh, rowsh, P(), vec, mat, mat, P(None, "fsdp"), vec, mat, vec, mat, vec, vec, mat, vec, mat, mat, mat),
        out_specs=(rowsh, rowsh, ov, om, om, P(None, BOTH), ov, om, ov, om, ov, ov, om, ov, om, om, om),
        check_vma=False,
    )
```

time: 2110 us -> 1030 us (0.49)
  waiting for transfers between devices: 1180 us -> 397 us
  blocking collectives: 194 us -> 31.7 us
  local copies, waits for them, and re-layouts: 372 us -> 240 us
  Pallas kernels: 0 us -> 120 us
  matrix products: 184 us -> 96.3 us
  other arithmetic: 140 us -> 83.4 us
    reduce_scatter x3 -> x9, waiting for transfers between devices: 997 us -> 233 us  [the longest x3 107 us: rs(): lax.psum_scatter(a.astype(BF), GROUP, scatter_dimension=0, tiled=True)]
    slice x102 -> x24, local copies, waits for them, and re-layouts: 201 us -> 25.7 us  [the longest x14 18.9 us: body(): lax.associative_scan(linear_step, (nextd, gst), axis=1, reverse=True)]
    pallas_call x0 -> x1, Pallas kernels: none -> 120 us  [call_forward(): pl.pallas_call(forward_branch, out_shape=outs, in_specs=[VMEM] * 6 + [ANY...]
    all_gather x12 -> x1, blocking collectives: 151 us -> 31.7 us  [body(): tot2 = lax.all_gather(jnp.stack([cum_end, decay[:, 0] * ladj[:, 0]]), 'seq')]
    pad x48 -> x24, local copies, waits for them, and re-layouts: 50.6 us -> 152 us  [body(): lax.associative_scan(linear_step, (nextd, gst), axis=1, reverse=True)]
    dot_general x22 -> x19, matrix products: 184 us -> 96.3 us  [the longest x6 41.4 us: mm_rt(): lax.dot_general(left, right, (((1,), (1,)), ((), ())), preferred_element_...]
    unnamed x1 -> x0, blocking collectives: 42.6 us -> none
    rev x2 -> x0, local copies, waits for them, and re-layouts: 33.6 us -> none  [body(): lax.associative_scan(linear_step, (next_decay, grad_states), axis=1, reve...]
  transfers between devices with their start and end apart: 13 -> 19, of which waited for: 7 -> 10; matrix products, arithmetic and copies ran while one was open for 18% -> 33% of each run, Pallas kernels for 0% -> 0%
where the time goes in v1:
time: 1030 us; the launch traced here: 1010 us
  waiting for transfers between devices  397 us (39%)
  local copies, waits for them, and re-layouts  240 us (23%)
  Pallas kernels  120 us (12%)
  matrix products  96.3 us (9%)
  other arithmetic  83.4 us (8%)
  blocking collectives  31.7 us (3%)
  starting transfers between devices  23.6 us (2%)
  between operations  16.4 us (2%)
    pad x24, local copies, waits for them, and re-layouts, body(): lax.associative_scan(linear_step, (nextd, gst), axis=1, reverse=True)  152 us
    pallas_call x1, Pallas kernels, call_forward(): pl.pallas_call(forward_branch, out_shape=outs, in_specs=[VMEM] * 6 + [ANY...  120 us
    unnamed x13, waiting for transfers between devices  119 us
    reduce_scatter x3, waiting for transfers between devices, rs(): lax.psum_scatter(a.astype(BF), GROUP, scatter_dimension=0, tiled=True)  107 us
    reduce_scatter x2, waiting for transfers between devices, grads_rows(): lax.psum_scatter(g.astype(BF), 'seq', scatter_dimension=0, tiled=True)  64.5 us
    reduce_scatter x4, waiting for transfers between devices, grads_cols(): lax.psum_scatter(g.astype(BF), 'seq', scatter_dimension=0, tiled=True)  62.1 us
    dot_general x6, matrix products, mm_rt(): lax.dot_general(left, right, (((1,), (1,)), ((), ())), preferred_element_...  41.4 us
    all_gather x1, blocking collectives, body(): tot2 = lax.all_gather(jnp.stack([cum_end, decay[:, 0] * ladj[:, 0]]), 'seq')  31.7 us
  transfers between devices with their start and end apart: 19, of which 10 were waited for; matrix products, arithmetic and copies ran while one was open for 33% of the time, Pallas kernels for 0%

profile of v1, /device:TPU:0, one launch (start us, length us, event | category | flops | bytes accessed | tf_op | source)
XLA Modules:
  0.0 1008.3 jit_solution(2624770234662227830)
XLA Ops:
  16.5 120.1 %forward_branch.1 = (bf16[1536,1024]{1,0:T(8,128)(2,1)}, bf16[1536,2304]{1,0:T(8,128)(2,1)}, bf16[1024,1536]{1,0:T(8,128)(2,1)}, bf16[1024,1536]{1,0:T(8,128)(2,...) custom-call(f32[256,1536]{1,0:T(8,128)} %bitcast.422, ...), custom_call_target="tpu_custom_call" | custom-call | tf_op jit(solution)/shard_map/forward_branch/pallas_call | solution.py:520
  136.6 7.3 fusion.12
  144.0 6.1 multiply_convert_fusion.1
  151.5 5.7 convolution_convert_fusion.3
  159.3 34.5 %reduce-scatter.10.cloned.1.call-done = bf16[256,1536]{1,0:T(8,128)(2,1)} async-done(((bf16[1024,1536]{1,0:T(8,128)(2,1)}), bf16[256,1536]{1,0:T(8,128)(2,1)}) %reduce-scatter.10.cloned.1.call-update) | async-done | bytes 786448 | tf_op jit(solution)/shard_map/reduce_scatter | solution.py:59
  193.7 3.4 multiply_reduce_fusion.1
  197.4 28.5 %all-gather.4.cloned.1.call-done = bf16[1024,1536]{1,0:T(8,128)(2,1)} async-done(((bf16[256,1536]{1,0:T(8,128)(2,1)}), bf16[1024,1536]{1,0:T(8,128)(2,1)}) %all-gather.4.cloned.1.call-update) | async-done | bytes 3145744 | tf_op jit(solution)/shard_map/all_gather | solution.py:55
  225.9 10.8 %fusion.6 = (bf16[1024,1152]{1,0:T(8,128)(2,1)S(1)}, bf16[1024,1152]{1,0:T(8,128)(2,1)S(1)}) fusion(f32[1024,1152]{1,0:T(8,128)} %copy-done.70, f32[1024,1152]{1,0:T(8,128)} %get-tuple-element.198, bf16[1024,1536]{1,0:T(8,128)(2,1)} %all-gather.4.cloned.1.call-done, bf16[1152,1536]{1,0:T(8,128)(2,1)S(1)} %copy-done), kind=kOutput, calls=%fused_computation.13 | convolution fusion | flops 3651010560 | bytes 20840448 | tf_op jit(solution)/shard_map/dot_general | solution.py:26
  236.7 8.0 fusion.7
  244.7 7.6 add_convert_fusion.1
  254.0 36.4 %reduce-scatter.12.cloned.1.call-done = bf16[256,1536]{1,0:T(8,128)(2,1)} async-done(((bf16[1024,1536]{1,0:T(8,128)(2,1)}), bf16[256,1536]{1,0:T(8,128)(2,1)}) %reduce-scatter.12.cloned.1.call-update) | async-done | bytes 786448 | tf_op jit(solution)/shard_map/reduce_scatter | solution.py:59
  290.5 2.3 fusion.51
  292.8 2.6 fusion.111
  295.5 8.7 convolution_convert_fusion.2
  306.1 7.1 convolution_convert_fusion
  314.8 2.5 copy.62
  319.6 2.6 copy.63
  326.4 5.7 convolution_convert_fusion.1
  332.6 7.9 multiply_multiply_fusion.2
  340.5 3.3 slice.532
  350.9 5.4 slice.527
  382.7 3.3 pad.106
  387.4 3.3 pad.119
  390.7 3.3 pad.120
  399.1 4.8 pad.108
  403.9 4.8 pad.122
  409.7 3.1 pad.121
  416.3 2.2 add_multiply_fusion.5
  418.6 5.8 pad.110
  426.1 8.7 pad.123
  434.8 5.6 pad.124
  440.5 2.2 add.392
  446.0 11.6 %pad.112 = f32[8,64,512]{2,0,1:T(8,128)S(1)} pad(f32[8,32,512]{2,0,1:T(8,128)} %add.383, f32[]{:T(128)} %constant.200.clone.1), padding=0_0_0x1_0_1x0_0_0 | pad | bytes 1572868 | tf_op jit(solution)/shard_map/pad | solution.py:597
  459.5 15.6 %pad.111 = f32[8,64,512]{2,0,1:T(8,128)} pad(f32[8,32,512]{2,0,1:T(8,128)} %pad_maximum_fusion.2, f32[]{:T(128)} %constant.200.clone.1), padding=0_0_0x0_1_1x0_0_0 | pad | bytes 1572868 | tf_op jit(solution)/shard_map/pad | solution.py:597
  482.1 30.3 %pad.114 = f32[8,128,512]{2,0,1:T(8,128)} pad(f32[8,64,512]{2,0,1:T(8,128)} %add.385, f32[]{:T(128)} %constant.200.clone.1), padding=0_0_0x1_0_1x0_0_0 | pad | bytes 3145732 | tf_op jit(solution)/shard_map/pad | solution.py:597
  512.4 20.5 %pad.128 = f32[8,128,512]{2,0,1:T(8,128)} pad(f32[8,64,512]{2,0,1:T(8,128)S(1)} %copy-done.25, f32[]{:T(128)} %constant.200.clone.1), padding=0_0_0x1_0_1x0_0_0 | pad | bytes 3145732 | tf_op jit(solution)/shard_map/pad | solution.py:597
  534.2 20.6 %pad.127 = f32[8,128,512]{2,0,1:T(8,128)} pad(f32[8,64,512]{2,0,1:T(8,128)S(1)} %concatenate.104, f32[]{:T(128)} %constant.200.clone.1), padding=0_0_0x0_1_1x0_0_0 | pad | bytes 3145732 | tf_op jit(solution)/shard_map/pad | solution.py:597
  554.8 2.2 add.387
  560.4 31.7 %all-gather = f32[16,8,512]{2,1,0:T(8,128)S(1)} all-gather(f32[2,8,512]{2,1,0:T(8,128)S(1)} %pad_maximum_fusion.13), channel_id=2, replica_groups=mesh['seq'=8,'fsdp'=4] {'seq'}, dimensions={0}, use_global_device_ids=true | all-gather | bytes 294912 | tf_op jit(solution)/shard_map/all_gather | solution.py:598
  592.1 4.2 fusion.37
  596.3 2.4 fusion.62
  600.5 2.3 copy.72
  605.2 3.0 copy.70
  608.1 3.4 copy.96
  611.5 3.3 copy.71
  614.8 4.9 convolution_convert_fusion.6
  625.7 3.3 copy.75
  629.0 4.6 fusion.21
  638.3 4.8 collective-permute-done
  644.4 3.0 convolution_convert_fusion.5
  648.6 3.0 copy.79
  658.9 3.4 fusion.57
  662.4 3.7 add_convert_fusion
  667.7 3.5 all-to-all-start.2
  672.0 5.0 collective-permute-start.2
  679.1 3.5 all-to-all-start.3
  683.6 9.7 all-to-all-done.3
  697.1 3.7 all-to-all-start
  701.5 62.1 %reduce-scatter.18.cloned.1.call-done = bf16[192,512]{1,0:T(8,128)(2,1)} async-done(((bf16[1536,512]{1,0:T(8,128)(2,1)}), bf16[192,512]{1,0:T(8,128)(2,1)}) %reduce-scatter.18.cloned.1.call-update) | async-done | bytes 196624 | tf_op jit(solution)/shard_map/reduce_scatter | solution.py:63
  763.6 3.4 all-to-all-start.1
  767.8 64.5 %reduce-scatter.20.cloned.1.call-done = bf16[64,1792]{1,0:T(8,128)(2,1)} async-done(((bf16[512,1792]{1,0:T(8,128)(2,1)}), bf16[64,1792]{1,0:T(8,128)(2,1)}) %reduce-scatter.20.cloned.1.call-update) | async-done | bytes 229392 | tf_op jit(solution)/shard_map/reduce_scatter | solution.py:69
  836.1 35.8 %reduce-scatter.14.cloned.1.call-done = bf16[256,1536]{1,0:T(8,128)(2,1)} async-done(((bf16[1024,1536]{1,0:T(8,128)(2,1)}), bf16[256,1536]{1,0:T(8,128)(2,1)}) %reduce-scatter.14.cloned.1.call-update) | async-done | bytes 786448 | tf_op jit(solution)/shard_map/reduce_scatter | solution.py:59
  874.4 3.8 fusion.45
  878.3 118.6 %all-reduce.34.cloned.1.call-done = f32[32,608]{1,0:T(8,128)} async-done(((f32[32,608]{1,0:T(8,128)}), f32[32,608]{1,0:T(8,128)}) %all-reduce.34.cloned.1.call-update) | async-done | bytes 77840
  (337 shorter events, 133.1 us)
Async XLA Ops:
  7.2 144.3 %copy-start = (bf16[1152,1536]{1,0:T(8,128)(2,1)S(1)}, bf16[1152,1536]{1,0:T(8,128)(2,1)}, u32[]{:S(2)}) copy-start(bf16[1152,1536]{1,0:T(8,128)(2,1)} %param.47) | copy-start | bytes 10616836
  7.2 186.5 %reduce-scatter.10.cloned.1.call-start = ((), (), s32[]{:S(2)}) async-start(), calls=%async_computation.13 | async-start | bytes 3932160 | tf_op jit(solution)/shard_map/reduce_scatter | solution.py:59
  136.6 7.3 copy-start.60
  136.6 7.3 copy-start.63
  143.9 6.2 copy-start.70
  157.2 68.7 %all-gather.4.cloned.1.call-start = ((), (), s32[]{:S(2)}) async-start(), calls=%async_computation.14 | async-start | bytes 3932160 | tf_op jit(solution)/shard_map/all_gather | solution.py:55
  197.2 93.3 %reduce-scatter.12.cloned.1.call-start = ((), (), s32[]{:S(2)}) async-start(), calls=%async_computation.15 | async-start | bytes 3932160 | tf_op jit(solution)/shard_map/reduce_scatter | solution.py:59
  236.7 8.0 copy-start.72
  236.7 8.0 copy-start.73
  252.3 38.1 %copy-start.8 = (f32[256,1536]{1,0:T(8,128)S(1)}, f32[256,1536]{1,0:T(8,128)}, u32[]{:S(2)}) copy-start(f32[256,1536]{1,0:T(8,128)} %get-tuple-element.104) | copy-start | bytes 4718596
  252.3 40.4 %copy-start.19 = (f32[2,128,1536]{2,1,0:T(8,128)S(1)}, f32[2,128,1536]{2,1,0:T(8,128)}, u32[]{:S(2)}) copy-start(f32[2,128,1536]{2,1,0:T(8,128)} %param.31) | copy-start | bytes 4718596
  252.4 80.2 %all-gather.6.cloned.1.call-start = ((), (), s32[]{:S(2)}) async-start(), calls=%async_computation.16 | async-start | bytes 3932160 | tf_op jit(solution)/shard_map/all_gather | solution.py:55
  295.4 372.3 %reduce-scatter.22.cloned.1.call-start = ((), (), s32[]{:S(2)}) async-start(), calls=%async_computation.21 | async-start | bytes 3981312 | tf_op jit(solution)/shard_map/reduce_scatter | solution.py:63
  304.1 367.9 %reduce-scatter.26.cloned.1.call-start = ((), (), s32[]{:S(2)}) async-start(), calls=%async_computation.23 | async-start | bytes 3981312 | tf_op jit(solution)/shard_map/reduce_scatter | solution.py:69
  313.2 363.9 %reduce-scatter.24.cloned.1.call-start = ((), (), s32[]{:S(2)}) async-start(), calls=%async_computation.22 | async-start | bytes 3981312 | tf_op jit(solution)/shard_map/reduce_scatter | solution.py:63
  319.6 2.6 copy-start.13
  322.4 3.9 copy-start.74
  323.5 2.9 copy-start.64
  332.1 365.0 %reduce-scatter.16.cloned.1.call-start = ((), (), s32[]{:S(2)}) async-start(), calls=%async_computation.18 | async-start | bytes 1769472 | tf_op jit(solution)/shard_map/reduce_scatter | solution.py:63
  340.5 3.8 copy-start.20
  344.3 2.6 copy-start.26
  344.4 2.6 copy-start.27
  370.0 29.0 %copy-start.46 = (f32[8,1,512]{2,0,1:T(8,128)S(1)}, f32[8,1,512]{2,0,1:T(8,128)}, u32[]{:S(2)}) copy-start(f32[8,1,512]{2,0,1:T(8,128)} %slice.648) | copy-start | bytes 49156
  408.7 9.7 copy-start.45
  416.3 8.2 copy-start.44
  418.4 16.4 %copy-start.33 = (f32[8,16,512]{2,0,1:T(8,128)S(1)}, f32[8,16,512]{2,0,1:T(8,128)}, u32[]{:S(2)}) copy-start(f32[8,16,512]{2,0,1:T(8,128)} %add.391) | copy-start | bytes 786436
  440.5 3.1 copy-start.21
  440.5 3.1 copy-start.22
  444.7 12.9 %copy-start.41 = (f32[8,1,512]{2,0,1:T(8,128)S(1)}, f32[8,1,512]{2,0,1:T(8,128)}, u32[]{:S(2)}) copy-start(f32[8,1,512]{2,0,1:T(8,128)} %slice.646) | copy-start | bytes 49156
  457.6 19.5 %copy-start.47 = (f32[8,1,512]{2,1,0:T(1,128)S(1)}, f32[8,1,512]{2,1,0:T(1,128)}, u32[]{:S(2)}) copy-start(f32[8,1,512]{2,1,0:T(1,128)} %slice.644) | copy-start | bytes 49156
  482.1 72.7 %copy-start.12 = (f32[8,128,512]{2,0,1:T(8,128)}, f32[8,128,512]{2,0,1:T(8,128)S(1)}, u32[]{:S(2)}) copy-start(f32[8,128,512]{2,0,1:T(8,128)S(1)} %pad.113) | copy-start | bytes 6291460
  482.1 30.3 %copy-start.25 = (f32[8,64,512]{2,0,1:T(8,128)S(1)}, f32[8,64,512]{2,0,1:T(8,128)}, u32[]{:S(2)}) copy-start(f32[8,64,512]{2,0,1:T(8,128)} %add.393) | copy-start | bytes 3145732
  554.8 2.9 copy-start.16
  554.8 37.2 %copy-start.17 = (f32[1024,512]{1,0:T(8,128)S(1)}, f32[1024,512]{1,0:T(8,128)}, u32[]{:S(2)}) copy-start(f32[1024,512]{1,0:T(8,128)} %get-tuple-element.113) | copy-start | bytes 6291460
  557.7 2.7 copy-start.48
  557.7 34.4 %copy-start.4 = (f32[1024,512]{1,0:T(8,128)S(1)}, f32[1024,512]{1,0:T(8,128)}, u32[]{:S(2)}) copy-start(f32[1024,512]{1,0:T(8,128)} %get-tuple-element.114) | copy-start | bytes 6291460
  557.7 34.4 %copy-start.6 = (f32[1024,512]{1,0:T(8,128)S(1)}, f32[1024,512]{1,0:T(8,128)}, u32[]{:S(2)}) copy-start(f32[1024,512]{1,0:T(8,128)} %get-tuple-element.115) | copy-start | bytes 6291460
  557.7 34.4 %copy-start.43 = (f32[8,1,512]{2,0,1:T(8,128)S(1)}, f32[8,1,512]{2,0,1:T(8,128)}, u32[]{:S(2)}) copy-start(f32[8,1,512]{2,0,1:T(8,128)} %get-tuple-element.185) | copy-start | bytes 49156
  557.7 34.4 %copy-start.51 = (f32[512]{0:T(512)S(1)}, f32[512]{0:T(512)}, u32[]{:S(2)}) copy-start(f32[512]{0:T(512)} %fusion.104) | copy-start | bytes 6148
  600.5 2.8 copy-start.36
  603.3 16.7 %copy-start.9 = (bf16[1024,4,128]{0,2,1:T(8,128)(2,1)}, bf16[1024,4,128]{0,2,1:T(8,128)(2,1)S(1)}, u32[]{:S(2)}) copy-start(bf16[1024,4,128]{0,2,1:T(8,128)(2,1)S(1)} %reshape.572) | copy-start | bytes 3145732
  611.5 3.3 copy-start.68
  614.8 5.2 copy-start.37
  619.7 143.9 %reduce-scatter.18.cloned.1.call-start = ((), (), s32[]{:S(2)}) async-start(), calls=%async_computation.19 | async-start | bytes 1769472 | tf_op jit(solution)/shard_map/reduce_scatter | solution.py:63
  625.7 3.3 copy-start.2
  629.0 4.6 copy-start.57
  636.8 6.2 collective-permute-start
  638.1 6.2 copy-start.61
  644.4 3.1 copy-start.7
  647.4 184.9 %reduce-scatter.20.cloned.1.call-start = ((), (), s32[]{:S(2)}) async-start(), calls=%async_computation.20 | async-start | bytes 2064384 | tf_op jit(solution)/shard_map/reduce_scatter | solution.py:69
  658.6 213.3 %reduce-scatter.14.cloned.1.call-start = ((), (), s32[]{:S(2)}) async-start(), calls=%async_computation.17 | async-start | bytes 3932160 | tf_op jit(solution)/shard_map/reduce_scatter | solution.py:59
  658.9 3.4 copy-start.24
  658.9 3.4 copy-start.35
  666.0 5.1 copy-start.59
  666.0 5.9 copy-start.50
  667.7 11.4 %all-to-all-start.2 = ((bf16[4,48,1152]{2,1,0:T(8,128)(2,1)}), bf16[4,48,1152]{2,1,0:T(8,128)(2,1)S(1)}, u32[]{:S(2)}, u32[]{:S(2)}) async-start(bf16[4,48,1152]{2,1,0:T(8,128)(2,1)} %bitcast.447), calls=%async_computation.9 | async-start | bytes 884736 | tf_op jit(solution)/shard_map/all_to_all | solution.py:64
  672.0 22.3 %collective-permute-start.2 = (bf16[144,1536]{1,0:T(8,128)(2,1)}, bf16[144,1536]{1,0:T(8,128)(2,1)}, u32[]{:S(2)}, u32[]{:S(2)}) collective-permute-start(bf16[144,1536]{1,0:T(8,128)(2,1)} %reduce-scatter.26.cloned.1.call-done), channel_id=1, source_target_pairs={{0,0},{1,8},{2,16},{3,24},{4,1},{5,9},{6,17},{7,25},{8,2},{9,10},{... | collective-permute-start | bytes 1327112 | tf_op jit(solution)/shard_map/ppermute | solution.py:71
  679.1 14.2 %all-to-all-start.3 = ((bf16[4,48,1152]{2,1,0:T(8,128)(2,1)}), bf16[4,48,1152]{2,1,0:T(8,128)(2,1)S(1)}, u32[]{:S(2)}, u32[]{:S(2)}) async-start(bf16[4,48,1152]{2,1,0:T(8,128)(2,1)} %bitcast.448), calls=%async_computation.11 | async-start | bytes 884736 | tf_op jit(solution)/shard_map/all_to_all | solution.py:64
  683.6 13.1 %copy-start.58 = (bf16[512]{0:T(512)(128)(2,1)S(1)}, bf16[512]{0:T(512)(128)(2,1)}, u32[]{:S(2)}) copy-start(bf16[512]{0:T(512)(128)(2,1)} %param.42) | copy-start | bytes 3076
  697.1 66.5 %all-to-all-start = ((bf16[4,48,512]{2,1,0:T(8,128)(2,1)}), bf16[4,48,512]{2,1,0:T(8,128)(2,1)S(1)}, u32[]{:S(2)}, u32[]{:S(2)}) async-start(bf16[4,48,512]{2,1,0:T(8,128)(2,1)} %bitcast.452), calls=%async_computation.4 | async-start | bytes 393216 | tf_op jit(solution)/shard_map/all_to_all | solution.py:64
  763.6 70.3 %all-to-all-start.1 = ((bf16[4,48,512]{2,1,0:T(8,128)(2,1)}), bf16[4,48,512]{2,1,0:T(8,128)(2,1)S(1)}, u32[]{:S(2)}, u32[]{:S(2)}) async-start(bf16[4,48,512]{2,1,0:T(8,128)(2,1)} %bitcast.453), calls=%async_computation.6 | async-start | bytes 393216 | tf_op jit(solution)/shard_map/all_to_all | solution.py:64
  767.0 229.9 %all-reduce.34.cloned.1.call-start = ((), (), s32[]{:S(2)}) async-start(), calls=%async_computation.24 | async-start | bytes 163840
  832.3 2.4 collective-permute-start.1
  874.4 126.6 %copy-start.1 = (bf16[1152,1536]{1,0:T(8,128)(2,1)S(1)}, bf16[1152,1536]{1,0:T(8,128)(2,1)}, u32[]{:S(2)}) copy-start(bf16[1152,1536]{1,0:T(8,128)(2,1)} %param.47) | copy-start | bytes 10616836
  (30 other events, 44.4 us)
Sparse Core Ops, SparseCore 0:
  157.3 36.4 reduce-scatter.9
  197.3 28.5 all-gather.3
  252.5 37.9 reduce-scatter.11
  295.5 28.5 all-gather.5
  327.6 79.0 reduce-scatter.21
  410.2 78.7 reduce-scatter.25
  492.6 79.3 reduce-scatter.23
  619.8 74.7 reduce-scatter.15
  698.5 65.0 reduce-scatter.17
  766.9 65.3 reduce-scatter.19
  835.0 36.8 reduce-scatter.13
  877.4 119.4 all-reduce.33

commit v2 on v1

--- a/solution.py
+++ b/solution.py
@@ -109,7 +109,7 @@
     def line(self, s):
         return (s, self.f)
 
-    def greet(self, whole_line=True):
+    def greet(self, hop=None):
         barrier = pltpu.get_barrier_semaphore()
         for f in (self.p1, self.p2, self.p3):
             pl.semaphore_signal(barrier, inc=1, device_id=self.group(f), device_id_type=MESH)
@@ -121,7 +121,7 @@
             return 0
 
         lax.fori_loop(1, self.n, one, 0)
-        pl.semaphore_wait(barrier, 3 + self.n - 1)
+        pl.semaphore_wait(barrier, 3 + self.n - 1 + (0 if hop is None else hop.greet(barrier)))
 
 
 class Sems:
@@ -210,6 +210,43 @@
 
         partial(at.f, add_own)
         between(3)
+
+    def run_tile(self, compute, tile, own, between=lambda k: None):
+        at = self.at
+
+        def one(k, _):
+            compute(jnp.where(k == 0, at.p3, jnp.where(k == 1, at.p2, jnp.where(k == 2, at.p1, at.f))))
+
+            @pl.when(k == 0)
+            def _():
+                self.core_out[0] = tile[...].astype(BF)
+                self.core[0].start()
+
+            @pl.when(k == 1)
+            def _():
+                self.core[0].wait_recv()
+                for r in range(2):
+                    sl = pl.ds(r * self.chunk, self.chunk)
+                    self.over_out[sl, :] = (tile[sl, :] + self.core_in[0, sl, :].astype(F32)).astype(BF)
+                    self.over[r].start()
+
+            @pl.when(k == 2)
+            def _():
+                self.core_out[1] = tile[...].astype(BF)
+                self.core[1].start()
+
+            @pl.when(k == 3)
+            def _():
+                self.core[1].wait_recv()
+                if own is None:
+                    tile[...] = tile[...] + self.core_in[1].astype(F32)
+                else:
+                    own[...] = own[...] + tile[...] + self.core_in[1].astype(F32)
+
+            between(k)
+            return 0
+
+        lax.fori_loop(0, 4, one, 0)
 
     def arrived(self, r):
         self.over[r].wait_recv()
@@ -378,10 +415,10 @@
             r = jax.nn.sigmoid(mm(low, wr[blocks, :]) + chan[5:6, cols])
             i = jax.nn.sigmoid(mm(low, wl[blocks, :]) + chan[6:7, cols])
             ld = r * chan[7:8, cols]
+            conv[sl, cols] = low
             low = low.astype(F32)
             decay[sl, cols] = jnp.exp(ld)
             work[sl, cols] = jnp.sqrt(EPS_MULT - expm1_neg(2.0 * ld)) * i * low
-            conv[sl, cols] = low
             rate[sl, cols] = r
             inlet[sl, cols] = i
         return 0
@@ -507,12 +544,12 @@
     vb = lambda *s: pltpu.VMEM(s, BF)
     outs = [
         bf(width, 2 * chans), bf(width, 2 * ffl), bf(every, width), bf(every, width), f32(here, width),
-        f32(every, chans), f32(every + 24, chans), f32(every, chans), f32(every, chans), f32(every, chans),
+        f32(every, chans), f32(every + 24, chans), bf(every, chans), f32(every, chans), f32(every, chans),
         f32(every, chans), f32(every, chans), bf(every, chans), f32(24, chans), f32(4, 8, width // 4),
     ]
     scratch = [
         vb(width, 2 * chans), vb(every, width), vb(every, width), vf(here, width), vf(4, 8, width // 4),
-        vf(every, chans), vf(every + 24, chans), vf(every, chans), vf(every, chans), vf(every, chans),
+        vf(every, chans), vf(every + 24, chans), vb(every, chans), vf(every, chans), vf(every, chans),
         vf(every, chans), vf(every, chans), vf(every, chans), vb(every, chans), vf(24, chans),
         vf(n, 16, chans), vb(2, here, width), vb(2, here, width), vb(here, width), vb(here, width),
         pltpu.SemaphoreType.DMA((120,)), pltpu.SemaphoreType.DMA((n,)), pltpu.SemaphoreType.DMA((n,)),
@@ -528,6 +565,667 @@
     )(x, gains, chan, wr, wl, wo, wg, wi, wu, wv)
 
 
+class Hop:
+    def __init__(self, at):
+        b = at.f * at.n + at.s
+        self.to = (lax.div(b, 4), lax.rem(b, 4))
+        c = at.s * 4 + at.f
+        self.source = (lax.rem(c, at.n), lax.div(c, at.n))
+        self.stays = b == c
+
+    def greet(self, barrier):
+        @pl.when(jnp.logical_not(self.stays))
+        def _():
+            for device in (self.to, self.source):
+                pl.semaphore_signal(barrier, inc=1, device_id=device, device_id_type=MESH)
+
+        return jnp.where(self.stays, 0, 2)
+
+    def start(self, sems, src, dst):
+        far = sems.remote(src, dst, self.to)
+        near = pltpu.make_async_copy(src, dst, sems.take())
+
+        @pl.when(self.stays)
+        def _():
+            near.start()
+
+        @pl.when(jnp.logical_not(self.stays))
+        def _():
+            far.start()
+
+        return near, far
+
+    def wait(self, pair):
+        near, far = pair
+
+        @pl.when(self.stays)
+        def _():
+            near.wait()
+
+        @pl.when(jnp.logical_not(self.stays))
+        def _():
+            far.wait()
+
+
+class Ring:
+    def __init__(self, at, grads, slots, send, recv, by_rows):
+        self.at, self.grads, self.slots, self.sem, self.rem = at, grads, slots, send, recv
+        n = at.n
+        self.q = self.place(at.s)
+        rows, width = slots.shape[1:]
+        self.rows = rows
+        if by_rows:
+            self.cut = [(pl.ds(i * rows // 4, rows // 4), pl.ds(0, width)) for i in range(4)]
+        else:
+            self.cut = [(pl.ds(0, rows), pl.ds(i * width // 4, width // 4)) for i in range(4)]
+        self.way = (1, -1, 1, -1)
+        self.to = {w: at.line(self.owner(lax.rem(self.q + w + n, n))) for w in (1, -1)}
+
+    def place(self, s):
+        half = lax.div(s, 2)
+        return jnp.where(lax.rem(s, 2) == 0, half, self.at.n - 1 - half)
+
+    def owner(self, q):
+        n = self.at.n
+        return jnp.where(q < n // 2, 2 * q, 2 * (n - 1 - q) + 1)
+
+    def block(self, i, behind):
+        n = self.at.n
+        s = self.owner(lax.rem(self.q - self.way[i] * behind + 2 * n, n))
+        r, c = self.cut[i]
+        return self.grads.at[pl.ds(pl.multiple_of(s * self.rows + r.start, 16), r.size), c]
+
+    def copy(self, i, k, src):
+        r, c = self.cut[i]
+        return pltpu.make_async_remote_copy(
+            src_ref=src, dst_ref=self.slots.at[k, r, c], send_sem=self.sem.at[i, k], recv_sem=self.rem.at[i, k],
+            device_id=self.to[self.way[i]], device_id_type=MESH,
+        )
+
+    def start(self):
+        for i in range(4):
+            self.copy(i, 0, self.block(i, 1)).start()
+
+    def summed(self, i, k):
+        r, c = self.cut[i]
+        slot = self.slots.at[k, r, c]
+        self.copy(i, k, slot).wait_recv()
+        return slot, slot[...].astype(F32) + self.block(i, k + 2)[...].astype(F32)
+
+    def step(self, k):
+        for i in range(4):
+            slot, value = self.summed(i, k)
+            slot[...] = value.astype(BF)
+            self.copy(i, k + 1, slot).start()
+
+    def last(self, out, after=lambda i: None):
+        k = self.at.n - 2
+        for i in range(4):
+            _, value = self.summed(i, k)
+            out[self.cut[i]] = value
+            after(i)
+
+    def finish(self):
+        def one(k, _):
+            for i in range(4):
+                r, c = self.cut[i]
+                self.copy(i, k, self.slots.at[k, r, c]).wait_send()
+            return 0
+
+        lax.fori_loop(0, self.at.n - 1, one, 0)
+
+
+class Spread:
+    def __init__(self, at, sems, src, out, col=0, width=None):
+        self.at = at
+        rows = src.shape[0] // 4
+        width = width or src.shape[1]
+        self.copies = []
+        cols = pl.ds(pl.multiple_of(at.f * width, 128), width)
+        for p in (at.p1, at.p2, at.p3):
+            piece = src.at[pl.ds(pl.multiple_of(p * rows, 8), rows), pl.ds(col, width)]
+            self.copies.append(sems.remote(piece, out.at[:, cols], at.group(p)))
+        piece = src.at[pl.ds(pl.multiple_of(at.f * rows, 8), rows), pl.ds(col, width)]
+        self.copies.append(pltpu.make_async_copy(piece, out.at[:, cols], sems.take()))
+
+    def start(self):
+        for c in self.copies:
+            c.start()
+
+    def wait(self):
+        for c in self.copies:
+            c.wait()
+
+
+def mlp(n2_h, wuv_h, wd_h, middle_h, teacher_h, scale, gain,
+        result_o, gmid_o, gml_o, gain_o, down_o, up_o, value_o,
+        n2, wuv, wd, hidden, ge, gdi, gml, middle, own, gout, tile, core_out, core_in, over_out, over_in,
+        gwd, gwu, gwv, slots_d, slots_u, last_d, last_u, gain_acc, sem, ring_sem):
+    at = Place()
+    sems = Sems(sem)
+    here, width = middle.shape
+    toks = here // 2
+    ffl = hidden.shape[1]
+    part = width // 4
+    col = 384
+    loads = [sems.local(n2_h, n2), sems.local(wuv_h, wuv), sems.local(wd_h, wd)]
+    loads2 = [sems.local(middle_h, middle), sems.local(middle_h, own), sems.local(teacher_h, gout)]
+    hop = Hop(at)
+    at.greet(hop)
+    for c in loads + loads2:
+        c.wait()
+
+    def forward(o):
+        sl = rows_at(o, here)
+
+        def some(c, _):
+            cols = pl.ds(pl.multiple_of(c * col, 128), col)
+            cols2 = pl.ds(pl.multiple_of(c * col + ffl, 128), col)
+            up = mm(n2[sl, :], wuv[:, cols])
+            g, d = gelu_pair(mm(n2[sl, :], wuv[:, cols2]))
+            hidden[sl, cols] = (g * up).astype(BF)
+            ge[sl, cols] = g.astype(BF)
+            ge[sl, cols2] = (up * d).astype(BF)
+            return 0
+
+        lax.fori_loop(0, ffl // col, some, 0)
+
+        def out(c, _):
+            cols = pl.ds(pl.multiple_of(c * 512, 128), 512)
+            tile[:, cols] = mm(hidden[sl, :], wd[:, cols])
+            return 0
+
+        lax.fori_loop(0, width // 512, out, 0)
+
+    sc = Scatter(at, sems, core_out, core_in, over_out, over_in, toks)
+    sc.run_tile(forward, tile, own)
+    ag = Gather(at, sems, gdi, toks)
+    for r in range(2):
+        sl = pl.ds(r * toks, toks)
+        v = own[sl, :] + sc.arrived(r)
+        own[sl, :] = v
+        v = (v - gout[sl, :]) * scale[sl, 0:1]
+        v = jnp.where(scale[sl, 0:1] > 0.0, v, 0.0)
+        gout[sl, :] = v
+        gdi[rows_at(at.f * 2 + r, toks), :] = v.astype(BF)
+        ag.send(r)
+    saves = [sems.local(own, result_o)]
+    for r in range(2):
+        ag.relay(r)
+    ag.finish()
+    sc.finish()
+    saves[0].wait()
+
+    def down_rows(m, _):
+        cols = pl.ds(pl.multiple_of(m * 128, 128), 128)
+        gwd[rows_at(m, 128), :] = mm_lt(hidden[:, cols], gdi[...]).astype(BF)
+        return 0
+
+    lax.fori_loop(0, ffl // 128, down_rows, 0)
+    ring_d = Ring(at, gwd, slots_d, ring_sem.at[0], ring_sem.at[1], False)
+    ring_u = Ring(at, gwu, slots_u, ring_sem.at[2], ring_sem.at[3], True)
+    ring_d.start()
+
+    def backward(o):
+        sl = rows_at(o, here)
+
+        def some(c, _):
+            cols = pl.ds(pl.multiple_of(c * col, 128), col)
+            cols2 = pl.ds(pl.multiple_of(c * col + ffl, 128), col)
+            gh = mm_rt(gdi[sl, :], wd[cols, :])
+            ge[sl, cols] = (gh * ge[sl, cols].astype(F32)).astype(BF)
+            ge[sl, cols2] = (gh * ge[sl, cols2].astype(F32)).astype(BF)
+            return 0
+
+        lax.fori_loop(0, ffl // col, some, 0)
+
+        def out(c, _):
+            cols = pl.ds(pl.multiple_of(c * 512, 128), 512)
+            tile[:, cols] = mm_rt(ge[sl, :], wuv[cols, :])
+            return 0
+
+        lax.fori_loop(0, width // 512, out, 0)
+
+    sc2 = Scatter(at, sems, core_out, core_in, over_out, over_in, toks)
+    sc2.run_tile(backward, tile, None, ring_d.step)
+
+    def weight_rows(grads, first):
+        def one(m, _):
+            cols = pl.ds(pl.multiple_of(m * 256, 256), 256)
+            grads[rows_at(m, 256), :] = mm_lt(n2[:, cols], ge[:, first : first + ffl]).astype(BF)
+            return 0
+
+        return one
+
+    up_rows, value_rows = weight_rows(gwu, 0), weight_rows(gwv, ffl)
+    six = width // 256
+    lax.fori_loop(0, six, up_rows, 0)
+    ring_d.step(4)
+    lax.fori_loop(0, six // 2, value_rows, 0)
+    ring_d.step(5)
+    ring_u.start()
+    lax.fori_loop(six // 2, six, value_rows, 0)
+    saves = [sems.local(gwv, value_o)]
+    ring_d.last(last_d)
+    hopping = hop.start(sems, last_d, down_o)
+    ring_u.step(0)
+    ag2 = Gather(at, sems, gml, toks)
+    acc = jnp.zeros((1, width), F32)
+    for r in range(2):
+        sl = pl.ds(r * toks, toks)
+        g = tile[sl, :] + sc2.arrived(r)
+        v = middle[sl, :]
+        s = lax.rsqrt(jnp.mean(v * v, axis=-1, keepdims=True) + EPS_NORM)
+        acc = acc + jnp.sum(g * v * s, axis=0, keepdims=True)
+        gg = g * gain[...]
+        mean = jnp.mean(gg * v, axis=-1, keepdims=True)
+        new = gout[sl, :] + s * gg - v * (s * s * s * mean)
+        own[sl, :] = new
+        gml[rows_at(at.f * 2 + r, toks), :] = new.astype(BF)
+        ag2.send(r)
+        ring_u.step(1 + r)
+    gain_acc[...] = jnp.broadcast_to(acc, gain_acc.shape)
+    saves += [sems.local(own, gmid_o), sems.local(gain_acc, gain_o)]
+    ag2.relay(0)
+    ring_u.step(3)
+    ag2.relay(1)
+    ring_u.step(4)
+    ag2.finish()
+    sc2.finish()
+    saves += [sems.local(gml, gml_o)]
+    ring_u.step(5)
+    spread = Spread(at, sems, last_u, up_o)
+    ring_u.last(last_u)
+    spread.start()
+    hop.wait(hopping)
+    ring_d.finish()
+    ring_u.finish()
+    spread.wait()
+    for c in saves:
+        c.wait()
+
+
+def call_mlp(n2, wuv, wd, middle, teacher, scale, gain):
+    every, width = n2.shape
+    here = middle.shape[0]
+    ffl = wd.shape[0]
+    n = lax.axis_size("seq")
+    f32 = lambda *s: jax.ShapeDtypeStruct(s, F32)
+    bf = lambda *s: jax.ShapeDtypeStruct(s, BF)
+    vf = lambda *s: pltpu.VMEM(s, F32)
+    vb = lambda *s: pltpu.VMEM(s, BF)
+    outs = [
+        f32(here, width), f32(here, width), bf(every, width), f32(8, width), f32(ffl // n, width),
+        f32(width // n // 4, 4 * ffl), bf(width, ffl),
+    ]
+    scratch = [
+        vb(every, width), vb(width, 2 * ffl), vb(ffl, width), vb(every, ffl), vb(every, 2 * ffl), vb(every, width),
+        vb(every, width), vf(here, width), vf(here, width), vf(here, width), vf(here, width),
+        vb(2, here, width), vb(2, here, width), vb(here, width), vb(here, width),
+        vb(ffl, width), vb(width, ffl), vb(width, ffl), vb(n - 1, ffl // n, width), vb(n - 1, width // n, ffl),
+        vf(ffl // n, width), vf(width // n, ffl), vf(8, width),
+        pltpu.SemaphoreType.DMA((100,)), pltpu.SemaphoreType.DMA((4, 4, n - 1)),
+    ]
+    return pl.pallas_call(
+        mlp,
+        out_shape=outs,
+        in_specs=[ANY] * 5 + [VMEM] * 2,
+        out_specs=[ANY] * len(outs),
+        scratch_shapes=scratch,
+        compiler_params=pltpu.CompilerParams(collective_id=2, has_side_effects=True, vmem_limit_bytes=LIMIT),
+        name="mlp",
+    )(n2, wuv, wd, middle, teacher, scale, gain)
+
+
+class Line:
+    def __init__(self, at, src, tot, send, recv):
+        self.at, self.src, self.tot, self.send_sem, self.recv_sem = at, src, tot, send, recv
+
+    def copy(self, slot, to):
+        return pltpu.make_async_remote_copy(
+            src_ref=self.src, dst_ref=self.tot.at[slot], send_sem=self.send_sem.at[to], recv_sem=self.recv_sem.at[slot],
+            device_id=self.at.line(to), device_id_type=MESH,
+        )
+
+    def send(self, first, end):
+        def one(j, _):
+            @pl.when(j != self.at.s)
+            def _():
+                self.copy(self.at.s, j).start()
+
+            return 0
+
+        lax.fori_loop(first, end, one, 0)
+
+    def sent(self, first, end):
+        def one(j, _):
+            @pl.when(j != self.at.s)
+            def _():
+                self.copy(self.at.s, j).wait_send()
+
+            return 0
+
+        lax.fori_loop(first, end, one, 0)
+
+    def wait(self, j):
+        self.copy(j, j).wait_recv()
+
+
+def branch_back(chan, wr, wl, gain, gain2,
+                gml_h, merged_h, wo_h, wgi_h, normed_h, gate_h, pad_h, conv_h, rate_h, inlet_h, decay_h, states_h, ends_h,
+                gwv_h, x_h, gmid_h,
+                ginput_o, value_o, gate_o, input_o, out_o, rate_o, inlet_o, chan_o, gains_o,
+                gml, merged, wo, wgi, normed, gate, pad, conv, rate, inlet, decay, states, ends, gwv, own,
+                work, gconv, pair, heads_r, heads_l, acc, tile, core_out, core_in, over_out, over_in,
+                go, ggi, slots_v, slots_o, slots_g, last_v, last_o, last_g,
+                passed, tot, small, small_in, small_sum, group_in, gains,
+                sem, ring_sem, line_sem):
+    at = Place()
+    sems = Sems(sem)
+    here, width = own.shape
+    toks = here // 2
+    chans = chan.shape[1]
+    group, taps = 8, 4
+    steps = toks
+    every = steps * group
+    halo = (taps - 1) * group
+    n = at.n
+    early = [sems.local(gwv_h, gwv), sems.local(gml_h, gml), sems.local(wo_h, wo)]
+    second = [sems.local(gate_h, gate), sems.local(states_h, states.at[pl.ds(group, every)]), sems.local(ends_h, ends)]
+    third = [sems.local(decay_h, decay), sems.local(merged_h, merged), sems.local(normed_h, normed)]
+    fourth = [
+        sems.local(a, b)
+        for a, b in ((pad_h, pad), (conv_h, conv), (rate_h, rate), (inlet_h, inlet), (wgi_h, wgi), (gmid_h, own))
+    ]
+    hop = Hop(at)
+    at.greet(hop)
+    ring_v = Ring(at, gwv, slots_v, ring_sem.at[0], ring_sem.at[1], True)
+    ring_o = Ring(at, go, slots_o, ring_sem.at[2], ring_sem.at[3], True)
+    ring_g = Ring(at, ggi, slots_g, ring_sem.at[4], ring_sem.at[5], True)
+    for c in early:
+        c.wait()
+    ring_v.start()
+
+    def merged_rows(m, _):
+        sl = rows_at(m, here)
+        work[sl, :] = mm_rt(gml[sl, :], wo[...])
+        return 0
+
+    lax.fori_loop(0, 4, merged_rows, 0)
+    for c in second:
+        c.wait()
+    states[0:group, :] = ends[16:24, :]
+    ring_v.step(0)
+
+    def split(c, _):
+        cols = pl.ds(pl.multiple_of(c * 128, 128), 128)
+        g = jnp.swapaxes(work[:, cols].reshape(group, steps, 128), 0, 1).reshape(every, 128)
+        act, slope = gelu_pair(gate[:, cols])
+        gate[:, cols] = g * act
+        down = g * states[pl.ds(group, every), cols] * slope
+        pair[:, cols] = jnp.swapaxes(down.reshape(steps, group, 128), 0, 1).reshape(every, 128).astype(BF)
+        return 0
+
+    lax.fori_loop(0, chans // 128, split, 0)
+    for c in third:
+        c.wait()
+    unroll = 8
+    blocks = steps // unroll
+
+    def totals(b, carry):
+        for u in range(unroll):
+            sl = pl.ds(pl.multiple_of((steps - 1 - (b * unroll + u)) * group, group), group)
+            carry = decay[sl, :] * (gate[sl, :] + carry)
+        return carry
+
+    zero = jnp.zeros((group, chans), F32)
+    passed[0:8, :] = ends[0:8, :]
+    passed[8:16, :] = lax.fori_loop(0, blocks, totals, zero)
+    line = Line(at, passed, tot, line_sem.at[0], line_sem.at[1])
+    line.send(0, at.s)
+    ring_v.step(1)
+
+    def out_rows(m, _):
+        cols = pl.ds(pl.multiple_of(m * 256, 256), 256)
+        go[rows_at(m, 256), 0:width] = mm_lt(merged[:, cols], gml[...]).astype(BF)
+        return 0
+
+    lax.fori_loop(0, chans // 256, out_rows, 0)
+    ring_v.step(2)
+
+    def normed_rows(first):
+        def one(m, _):
+            cols = pl.ds(pl.multiple_of(m * 256, 256), 256)
+            ggi[rows_at(m, 256), first : first + chans] = mm_lt(normed[:, cols], pair[:, first : first + chans]).astype(BF)
+            return 0
+
+        return one
+
+    lax.fori_loop(0, width // 256, normed_rows(0), 0)
+    ring_v.step(3)
+
+    def enter(k, state):
+        j = n - 1 - k
+        line.wait(j)
+        return tot[j, 0:8, :] * state + tot[j, 8:16, :]
+
+    carry_in = lax.fori_loop(0, n - 1 - at.s, enter, zero)
+    line.sent(0, at.s)
+
+    def scan(b, carry):
+        for u in range(unroll):
+            sl = pl.ds(pl.multiple_of((steps - 1 - (b * unroll + u)) * group, group), group)
+            adjoint = gate[sl, :] + carry
+            gate[sl, :] = adjoint
+            carry = decay[sl, :] * adjoint
+        return carry
+
+    lax.fori_loop(0, blocks, scan, carry_in)
+    ring_v.step(4)
+    for c in fourth:
+        c.wait()
+    heads_r[...] = jnp.zeros_like(heads_r)
+    heads_l[...] = jnp.zeros_like(heads_l)
+    acc[...] = jnp.zeros_like(acc)
+    edge = sems.remote(
+        gconv.at[pl.ds(0, halo)], gconv.at[pl.ds(every, halo)], at.line(lax.rem(at.s + n - 1, n))
+    )
+
+    def gates(b, _):
+        size = 128
+        start = pl.multiple_of(b * size, size)
+        sl = pl.ds(start, size)
+        for h in range(chans // 128):
+            cols = pl.ds(h * 128, 128)
+            sp8 = chan[7:8, cols]
+            r, i, dec, adj = rate[sl, cols], inlet[sl, cols], decay[sl, cols], gate[sl, cols]
+            low_bf = conv[sl, cols]
+            low = low_bf.astype(F32)
+            factor = jnp.sqrt(EPS_MULT - expm1_neg(2.0 * (r * sp8)))
+            ai = adj * i
+            af = adj * factor
+            gld = adj * states[sl, cols] * dec - ai * low * (dec * dec) / factor
+            gldr = gld * r
+            grate = gldr * sp8 * (1.0 - r)
+            ginl = af * low * i * (1.0 - i)
+            grl, gil = grate.astype(BF), ginl.astype(BF)
+            hb = pl.ds(h * 128, 128)
+            gc = af * i + mm_rt(grl, wr[hb, :]) + mm_rt(gil, wl[hb, :])
+            heads_r[hb, :] += mm_lt(low_bf, grl)
+            heads_l[hb, :] += mm_lt(low_bf, gil)
+            gconv[sl, cols] = gc
+            fold = lambda v: jnp.sum(v.reshape(size // 8, 8, 128), axis=0)
+            for k in range(taps):
+                acc[k, :, cols] += fold(gc * pad[pl.ds(start + (halo - group * k), size), cols])
+            acc[4, :, cols] += fold(gc)
+            acc[5, :, cols] += fold(grate)
+            acc[6, :, cols] += fold(ginl)
+            acc[7, :, cols] += fold(gldr)
+
+        @pl.when(jnp.logical_and(b == 0, at.s > 0))
+        def _():
+            edge.start()
+
+        return 0
+
+    lax.fori_loop(0, every // 128, gates, 0)
+
+    @pl.when(at.s == n - 1)
+    def _():
+        gconv[pl.ds(every, halo), :] = jnp.zeros((halo, chans), F32)
+
+    thirds = width // chans
+    inputs = [
+        sems.local(x_h.at[:, pl.ds(k * chans, chans)], pad.at[pl.ds(k * here, here)]) for k in range(thirds)
+    ]
+    go[:, width : width + 128] = heads_r[...].astype(BF)
+    go[:, width + 128 :] = heads_l[...].astype(BF)
+    ring_o.start()
+    ring_v.step(5)
+    for k in range(8):
+        small[k : k + 1, :] = jnp.sum(acc[k], axis=0, keepdims=True)
+    small[7:8, :] = small[7:8, :] * chan[8:9, :]
+
+    @pl.when(at.s < n - 1)
+    def _():
+        edge.wait_recv()
+
+    @pl.when(at.s > 0)
+    def _():
+        edge.wait_send()
+
+    def taps_back(b, _):
+        start = pl.multiple_of(b * 128, 128)
+        for h in range(chans // 128):
+            cols = pl.ds(h * 128, 128)
+            total = chan[0:1, cols] * gconv[pl.ds(start, 128), cols]
+            for k in range(1, taps):
+                total = total + chan[k : k + 1, cols] * gconv[pl.ds(start + group * k, 128), cols]
+            work[pl.ds(start, 128), cols] = total
+        return 0
+
+    lax.fori_loop(0, every // 128, taps_back, 0)
+    swap_rows(work, pair.at[:, pl.ds(chans, chans)], steps, BF)
+    spread_v = Spread(at, sems, last_v, value_o)
+    ring_v.last(last_v)
+    spread_v.start()
+    lax.fori_loop(0, width // 256, normed_rows(chans), 0)
+    ring_g.start()
+    ring_o.step(0)
+
+    def back(o):
+        sl = rows_at(o, here)
+
+        def some(c, _):
+            cols = pl.ds(pl.multiple_of(c * 512, 128), 512)
+            tile[:, cols] = mm_rt(pair[sl, :], wgi[cols, :])
+            return 0
+
+        lax.fori_loop(0, width // 512, some, 0)
+
+    sc = Scatter(at, sems, core_out, core_in, over_out, over_in, toks)
+    sc.run_tile(back, tile, None, lambda k: ring_o.step(k + 1))
+    ring_g.step(0)
+    ring_o.step(5)
+    ring_g.step(1)
+    ring_o.last(last_o)
+    hops = [
+        hop.start(sems, last_o.at[:, pl.ds(0, width)], out_o),
+        hop.start(sems, last_o.at[:, pl.ds(width, 128)], rate_o),
+        hop.start(sems, last_o.at[:, pl.ds(width + 128, 128)], inlet_o),
+    ]
+    gain1 = jnp.zeros((1, width), F32)
+    for c in inputs:
+        c.wait()
+    for r in range(2):
+        sl = pl.ds(r * toks, toks)
+        g = tile[sl, :] + sc.arrived(r)
+        v = jnp.concatenate([pad[pl.ds(k * here + r * toks, toks), :] for k in range(thirds)], axis=1)
+        s = lax.rsqrt(jnp.mean(v * v, axis=-1, keepdims=True) + EPS_NORM)
+        gain1 = gain1 + jnp.sum(g * v * s, axis=0, keepdims=True)
+        gg = g * gain[...]
+        mean = jnp.mean(gg * v, axis=-1, keepdims=True)
+        own[sl, :] = own[sl, :] + s * gg - v * (s * s * s * mean)
+        ring_g.step(2 + r)
+    saves = [sems.local(own, ginput_o)]
+    for k in range(3):
+        small[8 + k : 9 + k, :] = gain1[:, k * chans : (k + 1) * chans]
+        small[11 + k : 12 + k, :] = gain2[0:1, k * chans : (k + 1) * chans]
+    small[14:16, :] = jnp.zeros((2, chans), F32)
+    share = Line(at, small, small_in, line_sem.at[2], line_sem.at[3])
+    share.send(0, n)
+    ring_g.step(4)
+    small_in[at.s] = small[...]
+
+    def arrive(j, total):
+        @pl.when(j != at.s)
+        def _():
+            share.wait(j)
+
+        return total + small_in[j]
+
+    small_sum[...] = lax.fori_loop(0, n, arrive, jnp.zeros(small.shape, F32))
+    hops.append(hop.start(sems, small_sum.at[pl.ds(0, 8)], chan_o))
+    lower = small_sum.at[pl.ds(8, 8)]
+    around = [sems.remote(lower, group_in.at[at.f], at.group(p)) for p in (at.p1, at.p2, at.p3)]
+    for c in around:
+        c.start()
+    group_in[at.f] = small_sum[8:16, :]
+    ring_g.step(5)
+    spreads = [Spread(at, sems, last_g, gate_o, 0, chans), Spread(at, sems, last_g, input_o, chans, chans)]
+    ring_g.last(last_g)
+    for c in spreads:
+        c.start()
+    for c in around:
+        c.wait()
+    gains[...] = group_in[0] + group_in[1] + group_in[2] + group_in[3]
+    saves += [sems.local(gains, gains_o)]
+    share.sent(0, n)
+    sc.finish()
+    for h in hops:
+        hop.wait(h)
+    for r in (ring_v, ring_o, ring_g):
+        r.finish()
+    for c in [spread_v] + spreads + saves:
+        c.wait()
+
+
+def call_back(chan, wr, wl, gain, gain2, gml, merged, wo, wgi, normed, gate, pad, conv, rate, inlet, decay, states, ends, gwv, x, gmid):
+    every, width = gml.shape
+    here = x.shape[0]
+    chans = chan.shape[1]
+    ffl = gwv.shape[1]
+    n = lax.axis_size("seq")
+    f32 = lambda *s: jax.ShapeDtypeStruct(s, F32)
+    vf = lambda *s: pltpu.VMEM(s, F32)
+    vb = lambda *s: pltpu.VMEM(s, BF)
+    rows, crow = width // n, chans // n
+    outs = [
+        f32(here, width), f32(rows // 4, 4 * ffl), f32(rows // 4, 4 * chans), f32(rows // 4, 4 * chans), f32(crow, width),
+        f32(crow, 128), f32(crow, 128), f32(8, chans), f32(8, chans),
+    ]
+    scratch = [
+        vb(every, width), vb(every, chans), vb(chans, width), vb(width, 2 * chans), vb(every, width),
+        vf(every, chans), vf(every + 24, chans), vb(every, chans), vf(every, chans), vf(every, chans), vf(every, chans),
+        vf(every + 8, chans), vf(24, chans), vb(width, ffl), vf(here, width),
+        vf(every, chans), vf(every + 24, chans), vb(every, 2 * chans), vf(chans, 128), vf(chans, 128), vf(8, 8, chans),
+        vf(here, width), vb(2, here, width), vb(2, here, width), vb(here, width), vb(here, width),
+        vb(chans, width + 256), vb(width, 2 * chans), vb(n - 1, rows, ffl), vb(n - 1, crow, width + 256), vb(n - 1, rows, 2 * chans),
+        vf(rows, ffl), vf(crow, width + 256), vf(rows, 2 * chans),
+        vf(16, chans), vf(n, 16, chans), vf(16, chans), vf(n, 16, chans), vf(16, chans), vf(4, 8, chans), vf(8, chans),
+        pltpu.SemaphoreType.DMA((90,)), pltpu.SemaphoreType.DMA((6, 4, n - 1)), pltpu.SemaphoreType.DMA((4, n)),
+    ]
+    return pl.pallas_call(
+        branch_back,
+        out_shape=outs,
+        in_specs=[VMEM] * 5 + [ANY] * 16,
+        out_specs=[ANY] * len(outs),
+        scratch_shapes=scratch,
+        compiler_params=pltpu.CompilerParams(collective_id=3, has_side_effects=True, vmem_limit_bytes=LIMIT),
+        name="branch_back",
+    )(chan, wr, wl, gain, gain2, gml, merged, wo, wgi, normed, gate, pad, conv, rate, inlet, decay, states, ends, gwv, x, gmid)
+
+
 def body(
     block_input, teacher, valid_lengths, norm_gain, w_gate, w_input, conv_weight, conv_bias,
     w_rate, bias_rate, w_inlet, bias_inlet, decay_param, w_out, mlp_gain, w_up, w_value, w_down,
@@ -543,15 +1241,37 @@
     taps = conv_weight.shape[0]
 
     cw = conv_weight.astype(F32)
-    heads_shape = (heads, hb, hb)
-    wr, wl = w_rate.reshape(heads_shape), w_inlet.reshape(heads_shape)
     sp = jax.nn.softplus(-decay_param.astype(F32))
     x = block_input.reshape(here, width)
     gains = jnp.concatenate([norm_gain[None].astype(F32), mlp_gain[None].astype(F32), jnp.zeros((6, width // 4), F32)])
     vec = lambda v: v.astype(F32)[None]
-    chan = jnp.concatenate([cw, vec(conv_bias), vec(bias_rate), vec(bias_inlet), vec(-RATE_SCALE * sp), jnp.zeros((8, chans), F32)])
+    chan = jnp.concatenate([cw, vec(conv_bias), vec(bias_rate), vec(bias_inlet), vec(-RATE_SCALE * sp), vec(RATE_SCALE * jax.nn.sigmoid(-decay_param.astype(F32))), jnp.zeros((7, chans), F32)])
     (wgi, wuv, normed, n2, middle, gate_tm, pad_tm, conv_tm, rate_tm, inlet_tm, decay_tm, states_tm, merged, ends, gain) = call_forward(
         x, gains, chan, w_rate, w_inlet, w_out, w_gate, w_input, w_up, w_value)
+    lens = lax.dynamic_slice_in_dim(valid_lengths, fi * rows_dev, rows_dev)
+    pos = si * toks + jnp.arange(toks, dtype=jnp.int32)
+    mask = (pos[None, :] < lens[:, None]).reshape(here, 1)
+    slots = valid_lengths.shape[0] * toks * n_seq
+    count = jnp.sum(valid_lengths).astype(F32)
+    if all((v // n_seq) % 64 == 0 for v in (width, chans)):
+        scale = jnp.broadcast_to(jnp.where(mask, slots / count, 0.0), (here, 128))
+        result, grad_middle, gml, gain2, down_sum, up_sum, g_value = call_mlp(
+            n2, wuv, w_down, middle, teacher.reshape(here, width), scale, gain[:, 1].reshape(1, -1))
+        grad_input, value_sum, gate_sum, input_sum, out_sum, rate_sum, inlet_sum, ch, gn = call_back(
+            chan, w_rate, w_inlet, gain[:, 0].reshape(1, -1), gain2, gml, merged, w_out, wgi, normed, gate_tm, pad_tm,
+            conv_tm, rate_tm, inlet_tm, decay_tm, states_tm, ends, g_value, x, grad_middle)
+        place = si * n_fs + fi
+        per = chans // n_seq
+        ch = lax.dynamic_slice_in_dim(ch, lax.rem(place, n_seq) * per, per, 1)
+        per = width // (n_seq * n_fs)
+        gn = lax.dynamic_slice_in_dim(gn[:6].reshape(2, width), place * per, per, 1)
+        return (
+            result.reshape(block_input.shape), grad_input.reshape(block_input.shape), gn[0], gate_sum, input_sum,
+            ch[:4], ch[4], rate_sum, ch[5], inlet_sum, ch[6], ch[7], out_sum, gn[1], up_sum, value_sum, down_sum,
+        )
+
+    heads_shape = (heads, hb, hb)
+    wr, wl = w_rate.reshape(heads_shape), w_inlet.reshape(heads_shape)
     wg, wi = wgi[:, :chans], wgi[:, chans:]
     wu, wv = wuv[:, :wuv.shape[1]//2], wuv[:, wuv.shape[1]//2:]
     gain_one, gain_two = gain[:, 0].reshape(-1), gain[:, 1].reshape(-1)
@@ -559,7 +1279,7 @@
     s2 = lax.rsqrt(jnp.mean(middle * middle, axis=-1, keepdims=True) + EPS_NORM)
     tok = lambda v: v.reshape(-1, rows, chans).swapaxes(0, 1)
     padded, clf, r, i, decay, states = tok(pad_tm), tok(conv_tm), tok(rate_tm), tok(inlet_tm), tok(decay_tm), tok(states_tm)
-    conv_low = clf.astype(BF)
+    conv_low, clf = clf, clf.astype(F32)
     heads_in = conv_low.reshape(rows * toks, heads, hb)
     gate_pre = tok(gate_tm).reshape(-1, chans)
     gg, gd = gelu_pair(gate_pre)
@@ -572,11 +1292,6 @@
     vg, vd = gelu_pair(value)
     hidden = (vg * up).astype(BF)
     result = middle + rs(mm(hidden, w_down))
-    lens = lax.dynamic_slice_in_dim(valid_lengths, fi * rows_dev, rows_dev)
-    pos = si * toks + jnp.arange(toks, dtype=jnp.int32)
-    mask = (pos[None, :] < lens[:, None]).reshape(here, 1)
-    slots = valid_lengths.shape[0] * toks * n_seq
-    count = jnp.sum(valid_lengths).astype(F32)
     grad_out = jnp.where(mask, result - teacher.reshape(here, width), 0.0) * (slots / count)
     gdi = ag(grad_out.astype(BF))
     g_down = mm_lt(hidden, gdi)

time: 1030 us -> 464 us (0.45); the launches traced: 1010 us -> 463 us
  waiting for transfers between devices: 397 us -> 0 us
  Pallas kernels: 120 us -> 439 us
  local copies, waits for them, and re-layouts: 240 us -> 18.2 us
  matrix products: 96.3 us -> 0 us
  other arithmetic: 83.4 us -> 4.78 us
  blocking collectives: 31.7 us -> 0 us
  starting transfers between devices: 23.6 us -> 0 us
  between operations: 16.4 us -> 1.45 us
    pallas_call x0 -> x2, Pallas kernels: none -> 319 us  [the longest x1 180 us: call_mlp(): pl.pallas_call(mlp, out_shape=outs, in_specs=[ANY] * 5 + [VMEM] * 2, out_...]
    reduce_scatter x9 -> x0, waiting for transfers between devices: 233 us -> none  [the longest x3 107 us: rs(): lax.psum_scatter(a.astype(BF), GROUP, scatter_dimension=0, tiled=True)]
    pad x24 -> x0, local copies, waits for them, and re-layouts: 152 us -> none  [body(): lax.associative_scan(linear_step, (nextd, gst), axis=1, reverse=True)]
    unnamed x13 -> x0, waiting for transfers between devices: 119 us -> none
    dot_general x19 -> x0, matrix products: 96.3 us -> none  [the longest x6 41.4 us: mm_rt(): lax.dot_general(left, right, (((1,), (1,)), ((), ())), preferred_element_...]
    all_gather x1 -> x0, blocking collectives: 31.7 us -> none  [body(): tot2 = lax.all_gather(jnp.stack([cum_end, decay[:, 0] * ladj[:, 0]]), 'seq')]
    all_gather x2 -> x0, waiting for transfers between devices: 28.5 us -> none  [ag(): return lax.all_gather(a, GROUP, axis=0, tiled=True)]
    add x15 -> x0, other arithmetic: 24.4 us -> none  [the longest x14 20.5 us: body(): lax.associative_scan(linear_step, (nextd, gst), axis=1, reverse=True)]
  transfers between devices with their start and end apart: 19 -> 0, of which waited for: 10 -> 0; matrix products, arithmetic and copies ran while one was open for 33% -> 0% of each run, Pallas kernels for 0% -> 0%
where the time goes in v2:
time: 464 us; the launch traced here: 463 us
  Pallas kernels  439 us (95%)
  local copies, waits for them, and re-layouts  18.2 us (4%)
  other arithmetic  4.78 us (1%)
    pallas_call x1, Pallas kernels, call_mlp(): pl.pallas_call(mlp, out_shape=outs, in_specs=[ANY] * 5 + [VMEM] * 2, out_...  180 us
    pallas_call x1, Pallas kernels, call_back(): pl.pallas_call(branch_back, out_shape=outs, in_specs=[VMEM] * 5 + [ANY] *...  139 us
    pallas_call x1, Pallas kernels, call_forward(): pl.pallas_call(forward_branch, out_shape=outs, in_specs=[VMEM] * 6 + [ANY...  120 us

profile of v2, /device:TPU:0, one launch (start us, length us, event | category | flops | bytes accessed | tf_op | source)
XLA Modules:
  0.0 463.0 jit_solution(18003047667596084262)
XLA Ops:
  0.7 1.3 reduce_sum.9
  2.7 0.7 dynamic_slice.9
  3.4 0.1 fusion.10
  3.5 0.1 pad.2.clone
  3.5 0.7 reshape.82
  4.2 0.7 reshape.83
  4.9 0.7 broadcast_in_dim.60
  5.6 0.7 broadcast_in_dim.61
  6.3 0.7 broadcast_in_dim.62
  7.0 0.7 fusion.9
  7.6 0.7 maximum_maximum_fusion.gains
  8.3 1.9 concatenate.7.chan
  10.3 0.8 broadcast_in_dim.59.scale
  11.0 120.1 %forward_branch.1 = (bf16[1536,1024]{1,0:T(8,128)(2,1)}, bf16[1536,2304]{1,0:T(8,128)(2,1)}, bf16[1024,1536]{1,0:T(8,128)(2,1)}, bf16[1024,1536]{1,0:T(8,128)(2,...) custom-call(f32[256,1536]{1,0:T(8,128)} %bitcast.26, ...), custom_call_target="tpu_custom_call" | custom-call | tf_op jit(solution)/shard_map/forward_branch/pallas_call | solution.py:557
  131.1 1.5 fusion.11
  132.5 179.5 %mlp.1 = (f32[256,1536]{1,0:T(8,128)}, f32[256,1536]{1,0:T(8,128)}, bf16[1024,1536]{1,0:T(8,128)(2,1)}, f32[8,1536]{1,0:T(8,128)}, f32[144,1536]{1,0:T(8,128)}, ...) custom-call(bf16[1024,1536]{1,0:T(8,128)(2,1)} %get-tuple-element.48.n2_h, bf16[1536,2304]{1,0:T(8,128)(2,1)} %get-tuple-element.49.wuv_h, ...), custom_call_target="tpu_custom_call" | custom-call | tf_op jit(solution)/shard_map/mlp/pallas_call | solution.py:869
  312.1 0.0 copy-start
  312.1 139.0 %branch_back.1 = (f32[256,1536]{1,0:T(8,128)}, f32[48,4608]{1,0:T(8,128)}, f32[48,2048]{1,0:T(8,128)}, f32[48,2048]{1,0:T(8,128)}, f32[64,1536]{1,0:T(8,128)}, /...) custom-call(f32[16,512]{1,0:T(8,128)} %concatenate.7.chan, bf16[512,128]{1,0:T(8,128)(2,1)} %wr.3, ...), custom_call_target="tpu_custom_call" | custom-call | tf_op jit(solution)/shard_map/branch_back/pallas_call | solution.py:1218
  451.1 0.0 copy-start.1
  451.1 0.8 reshape.81
  452.0 0.1 constant_dynamic-slice_fusion.1
  452.1 0.5 slice_bitcast_fusion
  452.6 0.7 constant_dynamic-slice_fusion
  453.3 0.6 slice.34
  453.9 0.5 slice_bitcast_fusion.1
  454.4 0.0 copy-done
  454.5 1.1 copy.45
  455.6 0.0 copy-done.1
  455.6 0.0 copy-start.7
  455.6 0.0 copy-start.6
  455.6 0.0 copy-start.9
  455.6 0.0 copy-start.8
  455.6 0.0 copy-start.5
  455.6 0.0 copy-start.3
  455.6 1.1 copy.46
  456.8 0.0 copy-done.7
  456.8 0.0 copy-start.4
  456.8 0.7 copy.47
  457.5 0.0 copy-done.6
  457.5 0.7 copy.48
  458.3 0.0 copy-done.9
  458.3 0.6 copy.49
  458.9 0.0 copy-done.8
  458.9 0.6 copy.50
  459.5 0.0 copy-done.5
  459.5 0.0 copy-start.2
  459.5 0.7 copy.51
  460.3 0.0 copy-done.3
  460.3 0.9 copy.52
  461.2 0.0 copy-done.4
  461.2 0.9 copy.53
  462.1 0.0 copy-done.2
  462.1 0.9 copy.54
  (3 shorter events, 0.0 us)
Async XLA Ops:
  312.1 142.3 %copy-start = (f32[256,1536]{1,0:T(8,128)S(1)}, f32[256,1536]{1,0:T(8,128)}, u32[]{:S(2)}) copy-start(f32[256,1536]{1,0:T(8,128)} %get-tuple-element.52) | copy-start | bytes 4718596
  451.1 4.5 copy-start.1
  455.6 1.2 copy-start.7
  455.6 1.9 copy-start.6
  455.6 2.7 copy-start.9
  455.6 3.3 copy-start.8
  455.6 3.9 copy-start.5
  455.6 4.6 %copy-start.3 = (f32[48,4608]{1,0:T(8,128)S(1)}, f32[48,4608]{1,0:T(8,128)}, u32[]{:S(2)}) copy-start(f32[48,4608]{1,0:T(8,128)} %get-tuple-element.120) | copy-start | bytes 2654212
  456.8 4.4 copy-start.4
  459.5 2.6 copy-start.2

commit v3 on v2

--- a/solution.py
+++ b/solution.py
@@ -80,7 +80,7 @@
 MESH = pl.DeviceIdType.MESH
 VMEM = pl.BlockSpec(memory_space=pltpu.VMEM)
 ANY = pl.BlockSpec(memory_space=pl.ANY)
-LIMIT = 60 * 2**20
+LIMIT = 63 * 2**20
 
 
 def ds(start, size):
@@ -259,25 +259,25 @@
 
 class Columns:
     def __init__(self, at, sems, weights, buf):
-        self.at = at
         rows, width = weights[0].shape
         part = width // 4
-        half = rows // 2
-        h = lax.rem(at.s, 2)
-        self.half, self.rows, self.part, self.buf, self.sems = half, rows, part, buf, sems
+        cut = rows // 4
+        h = lax.rem(at.s, 4)
+        one = h + 1 - 2 * lax.rem(h, 2)
+        mates = [at.line(at.s - h + m) for m in (one, lax.rem(h + 2, 4), lax.rem(one + 2, 4))]
         self.near, self.own, self.far, self.side = [], [], [], []
         for k, w in enumerate(weights):
             cols = pl.ds(k * part, part)
             take = lambda f: pl.ds(pl.multiple_of(f * part, 128), part)
             mine = pl.ds(pl.multiple_of(at.f * rows, rows), rows)
-            cut = pl.ds(pl.multiple_of(h * half, half), half)
-            mine_cut = pl.ds(pl.multiple_of(at.f * rows + h * half, half), half)
+            quarter = pl.ds(pl.multiple_of(h * cut, cut), cut)
+            mine_cut = pl.ds(pl.multiple_of(at.f * rows + h * cut, cut), cut)
             self.own.append(pltpu.make_async_copy(w.at[:, take(at.f)], buf.at[mine, cols], sems.take()))
             self.near.append(sems.remote(w.at[:, take(at.p1)], buf.at[mine, cols], at.group(at.p1)))
             for p in (at.p2, at.p3):
-                self.far.append(sems.remote(w.at[cut, take(p)], buf.at[mine_cut, cols], at.group(p)))
-                came = buf.at[pl.ds(pl.multiple_of(p * rows + h * half, half), half), cols]
-                self.side.append(sems.remote(came, came, at.line(at.sx)))
+                self.far.append(sems.remote(w.at[quarter, take(p)], buf.at[mine_cut, cols], at.group(p)))
+                came = buf.at[pl.ds(pl.multiple_of(p * rows + h * cut, cut), cut), cols]
+                self.side.append([sems.remote(came, came, mate) for mate in mates])
 
     def start_far(self):
         for c in self.far:
@@ -289,10 +289,11 @@
 
     def relay(self, k):
         self.far[k].wait_recv()
-        self.side[k].start()
+        for c in self.side[k]:
+            c.start()
 
     def finish(self):
-        for c in self.own + self.near + self.side:
+        for c in self.own + self.near + sum(self.side, []):
             c.wait()
         for c in self.far:
             c.wait_send()
@@ -399,7 +400,6 @@
     def _():
         tail.wait_send()
 
-    uv.relay(0)
 
     def gates(b, _):
         for h in range(chans // 128):
@@ -456,7 +456,6 @@
         return 0
 
     lax.fori_loop(at.s + 1, at.n, send_total, 0)
-    uv.relay(1)
 
     def enter(j, state):
         total_copy(j, j).wait_recv()
@@ -508,7 +507,12 @@
 
         lax.fori_loop(0, 2, half, 0)
 
-    sc.run(partial, middle)
+    def between(k):
+        if k >= 2:
+            uv.relay(2 * k - 4)
+            uv.relay(2 * k - 3)
+
+    sc.run(partial, middle, between)
     ag2 = Gather(at, sems, n2, toks)
     for r in range(2):
         sl = pl.ds(r * toks, toks)
@@ -520,8 +524,6 @@
             n2[rows_at(at.f * 2 + r, toks), cols] = (middle[sl, cols] * scale * gain[p, 1:2, :]).astype(BF)
         ag2.send(r)
     saves += [sems.local(middle, middle_o)]
-    uv.relay(2)
-    uv.relay(3)
     for r in range(2):
         ag2.relay(r)
     ag2.finish()
@@ -552,7 +554,7 @@
         vf(every, chans), vf(every + 24, chans), vb(every, chans), vf(every, chans), vf(every, chans),
         vf(every, chans), vf(every, chans), vf(every, chans), vb(every, chans), vf(24, chans),
         vf(n, 16, chans), vb(2, here, width), vb(2, here, width), vb(here, width), vb(here, width),
-        pltpu.SemaphoreType.DMA((120,)), pltpu.SemaphoreType.DMA((n,)), pltpu.SemaphoreType.DMA((n,)),
+        pltpu.SemaphoreType.DMA((170,)), pltpu.SemaphoreType.DMA((n,)), pltpu.SemaphoreType.DMA((n,)),
     ]
     return pl.pallas_call(
         forward_branch,
@@ -662,7 +664,7 @@
         k = self.at.n - 2
         for i in range(4):
             _, value = self.summed(i, k)
-            out[self.cut[i]] = value
+            out[self.cut[i]] = value.astype(out.dtype)
             after(i)
 
     def finish(self):
@@ -675,22 +677,47 @@
         lax.fori_loop(0, self.at.n - 1, one, 0)
 
 
+class Regroup:
+    def __init__(self, at, sems, src, dst):
+        size = src.shape[0] // at.n
+        self.far, self.near = [], []
+        for h in range(at.n // 4):
+            slot = dst.at[pl.ds(pl.multiple_of((at.f * (at.n // 4) + h) * size, 16), size)]
+            block = lambda p: src.at[pl.ds(pl.multiple_of((p + 4 * h) * size, 16), size)]
+            for p in (at.p2, at.p3, at.p1):
+                self.far.append(sems.remote(block(p), slot, at.group(p)))
+            self.near.append(pltpu.make_async_copy(block(at.f), slot, sems.take()))
+
+    def start(self):
+        for c in self.far + self.near:
+            c.start()
+
+    def wait(self):
+        for c in self.far + self.near:
+            c.wait()
+
+
 class Spread:
-    def __init__(self, at, sems, src, out, col=0, width=None):
-        self.at = at
-        rows = src.shape[0] // 4
-        width = width or src.shape[1]
+    def __init__(self, at, sems, src, came):
+        self.at, self.src, self.came = at, src, came
+        rows = came.shape[1]
+        send, recv = [sems.take() for _ in range(4)], [sems.take() for _ in range(4)]
         self.copies = []
-        cols = pl.ds(pl.multiple_of(at.f * width, 128), width)
-        for p in (at.p1, at.p2, at.p3):
-            piece = src.at[pl.ds(pl.multiple_of(p * rows, 8), rows), pl.ds(col, width)]
-            self.copies.append(sems.remote(piece, out.at[:, cols], at.group(p)))
-        piece = src.at[pl.ds(pl.multiple_of(at.f * rows, 8), rows), pl.ds(col, width)]
-        self.copies.append(pltpu.make_async_copy(piece, out.at[:, cols], sems.take()))
+        for k in range(1, 4):
+            to = lax.rem(at.f + k, 4)
+            piece = src.at[pl.ds(pl.multiple_of(to * rows, 16), rows)]
+            self.copies.append(
+                pltpu.make_async_remote_copy(
+                    src_ref=piece, dst_ref=came.at[at.f], send_sem=send[k], recv_sem=recv[k],
+                    device_id=at.group(to), device_id_type=MESH,
+                )
+            )
 
     def start(self):
+        rows = self.came.shape[1]
         for c in self.copies:
             c.start()
+        self.came[self.at.f] = self.src[pl.ds(pl.multiple_of(self.at.f * rows, 16), rows), :]
 
     def wait(self):
         for c in self.copies:
@@ -700,7 +727,7 @@
 def mlp(n2_h, wuv_h, wd_h, middle_h, teacher_h, scale, gain,
         result_o, gmid_o, gml_o, gain_o, down_o, up_o, value_o,
         n2, wuv, wd, hidden, ge, gdi, gml, middle, own, gout, tile, core_out, core_in, over_out, over_in,
-        gwd, gwu, gwv, slots_d, slots_u, last_d, last_u, gain_acc, sem, ring_sem):
+        gwd, gwu, gwv, slots_u, last_u, gain_acc, sem, ring_sem):
     at = Place()
     sems = Sems(sem)
     here, width = middle.shape
@@ -710,8 +737,7 @@
     col = 384
     loads = [sems.local(n2_h, n2), sems.local(wuv_h, wuv), sems.local(wd_h, wd)]
     loads2 = [sems.local(middle_h, middle), sems.local(middle_h, own), sems.local(teacher_h, gout)]
-    hop = Hop(at)
-    at.greet(hop)
+    at.greet()
     for c in loads + loads2:
         c.wait()
 
@@ -754,19 +780,14 @@
         ag.relay(r)
     ag.finish()
     sc.finish()
-    saves[0].wait()
+    saves.pop().wait()
 
     def down_rows(m, _):
         cols = pl.ds(pl.multiple_of(m * 128, 128), 128)
         gwd[rows_at(m, 128), :] = mm_lt(hidden[:, cols], gdi[...]).astype(BF)
         return 0
 
-    lax.fori_loop(0, ffl // 128, down_rows, 0)
-    ring_d = Ring(at, gwd, slots_d, ring_sem.at[0], ring_sem.at[1], False)
-    ring_u = Ring(at, gwu, slots_u, ring_sem.at[2], ring_sem.at[3], True)
-    ring_d.start()
-
-    def backward(o):
+    def hidden_rows(o, _):
         sl = rows_at(o, here)
 
         def some(c, _):
@@ -778,16 +799,7 @@
             return 0
 
         lax.fori_loop(0, ffl // col, some, 0)
-
-        def out(c, _):
-            cols = pl.ds(pl.multiple_of(c * 512, 128), 512)
-            tile[:, cols] = mm_rt(ge[sl, :], wuv[cols, :])
-            return 0
-
-        lax.fori_loop(0, width // 512, out, 0)
-
-    sc2 = Scatter(at, sems, core_out, core_in, over_out, over_in, toks)
-    sc2.run_tile(backward, tile, None, ring_d.step)
+        return 0
 
     def weight_rows(grads, first):
         def one(m, _):
@@ -797,18 +809,34 @@
 
         return one
 
-    up_rows, value_rows = weight_rows(gwu, 0), weight_rows(gwv, ffl)
+    def backward(o):
+        sl = rows_at(o, here)
+
+        def out(c, _):
+            cols = pl.ds(pl.multiple_of(c * 512, 128), 512)
+            tile[:, cols] = mm_rt(ge[sl, :], wuv[cols, :])
+            return 0
+
+        lax.fori_loop(0, width // 512, out, 0)
+
+    ring_u = Ring(at, gwu, slots_u, ring_sem.at[0], ring_sem.at[1], True)
     six = width // 256
-    lax.fori_loop(0, six, up_rows, 0)
-    ring_d.step(4)
-    lax.fori_loop(0, six // 2, value_rows, 0)
-    ring_d.step(5)
+    lax.fori_loop(0, 4, hidden_rows, 0)
+    lax.fori_loop(0, six, weight_rows(gwu, 0), 0)
     ring_u.start()
-    lax.fori_loop(six // 2, six, value_rows, 0)
-    saves = [sems.local(gwv, value_o)]
-    ring_d.last(last_d)
-    hopping = hop.start(sems, last_d, down_o)
-    ring_u.step(0)
+    sc2 = Scatter(at, sems, core_out, core_in, over_out, over_in, toks)
+
+    def between(k):
+        @pl.when(k >= 2)
+        def _():
+            ring_u.step(k - 2)
+
+    sc2.run_tile(backward, tile, None, between)
+    lax.fori_loop(0, six, weight_rows(gwv, ffl), 0)
+    ring_u.step(2)
+    lax.fori_loop(0, ffl // 128, down_rows, 0)
+    ring_u.step(3)
+    saves += [sems.local(gwv, value_o), sems.local(gwd, down_o)]
     ag2 = Gather(at, sems, gml, toks)
     acc = jnp.zeros((1, width), F32)
     for r in range(2):
@@ -823,24 +851,18 @@
         own[sl, :] = new
         gml[rows_at(at.f * 2 + r, toks), :] = new.astype(BF)
         ag2.send(r)
-        ring_u.step(1 + r)
     gain_acc[...] = jnp.broadcast_to(acc, gain_acc.shape)
     saves += [sems.local(own, gmid_o), sems.local(gain_acc, gain_o)]
+    ring_u.step(4)
     ag2.relay(0)
-    ring_u.step(3)
+    ring_u.step(5)
     ag2.relay(1)
-    ring_u.step(4)
+    ring_u.last(last_u)
+    saves += [sems.local(last_u, up_o)]
     ag2.finish()
     sc2.finish()
     saves += [sems.local(gml, gml_o)]
-    ring_u.step(5)
-    spread = Spread(at, sems, last_u, up_o)
-    ring_u.last(last_u)
-    spread.start()
-    hop.wait(hopping)
-    ring_d.finish()
     ring_u.finish()
-    spread.wait()
     for c in saves:
         c.wait()
 
@@ -855,16 +877,16 @@
     vf = lambda *s: pltpu.VMEM(s, F32)
     vb = lambda *s: pltpu.VMEM(s, BF)
     outs = [
-        f32(here, width), f32(here, width), bf(every, width), f32(8, width), f32(ffl // n, width),
-        f32(width // n // 4, 4 * ffl), bf(width, ffl),
+        f32(here, width), f32(here, width), bf(every, width), f32(8, width), bf(ffl, width),
+        bf(width // n, ffl), bf(width, ffl),
     ]
     scratch = [
         vb(every, width), vb(width, 2 * ffl), vb(ffl, width), vb(every, ffl), vb(every, 2 * ffl), vb(every, width),
         vb(every, width), vf(here, width), vf(here, width), vf(here, width), vf(here, width),
         vb(2, here, width), vb(2, here, width), vb(here, width), vb(here, width),
-        vb(ffl, width), vb(width, ffl), vb(width, ffl), vb(n - 1, ffl // n, width), vb(n - 1, width // n, ffl),
-        vf(ffl // n, width), vf(width // n, ffl), vf(8, width),
-        pltpu.SemaphoreType.DMA((100,)), pltpu.SemaphoreType.DMA((4, 4, n - 1)),
+        vb(ffl, width), vb(width, ffl), vb(width, ffl), vb(n - 1, width // n, ffl),
+        vb(width // n, ffl), vf(8, width),
+        pltpu.SemaphoreType.DMA((100,)), pltpu.SemaphoreType.DMA((2, 4, n - 1)),
     ]
     return pl.pallas_call(
         mlp,
@@ -913,11 +935,11 @@
 
 def branch_back(chan, wr, wl, gain, gain2,
                 gml_h, merged_h, wo_h, wgi_h, normed_h, gate_h, pad_h, conv_h, rate_h, inlet_h, decay_h, states_h, ends_h,
-                gwv_h, x_h, gmid_h,
-                ginput_o, value_o, gate_o, input_o, out_o, rate_o, inlet_o, chan_o, gains_o,
-                gml, merged, wo, wgi, normed, gate, pad, conv, rate, inlet, decay, states, ends, gwv, own,
-                work, gconv, pair, heads_r, heads_l, acc, tile, core_out, core_in, over_out, over_in,
-                go, ggi, slots_v, slots_o, slots_g, last_v, last_o, last_g,
+                gwd_h, x_h, gmid_h, up_h, value_h,
+                ginput_o, up_o, value_o, down_o, gate_o, input_o, out_o, rate_o, inlet_o, chan_o, gains_o,
+                gml, merged, wo, wgi, gate, pad, conv, rate, inlet, decay, states, ends, gwd, gwv, own,
+                work, gconv, pair, heads_r, heads_l, acc, tile, core_in, over_out, over_in,
+                go, ggi, slots_d, slots_v, slots_o, slots_g, last_u, last_o, last_g, came_u, came_v, came_o, came_g,
                 passed, tot, small, small_in, small_sum, group_in, gains,
                 sem, ring_sem, line_sem):
     at = Place()
@@ -930,32 +952,62 @@
     every = steps * group
     halo = (taps - 1) * group
     n = at.n
-    early = [sems.local(gwv_h, gwv), sems.local(gml_h, gml), sems.local(wo_h, wo)]
+    ffl = came_u.shape[2]
+    early = [
+        sems.local(value_h, gwv), sems.local(up_h, last_u), sems.local(gml_h, gml),
+        sems.local(wo_h.at[pl.ds(0, here)], wo.at[0]), sems.local(wo_h.at[pl.ds(here, here)], wo.at[1]),
+    ]
     second = [sems.local(gate_h, gate), sems.local(states_h, states.at[pl.ds(group, every)]), sems.local(ends_h, ends)]
-    third = [sems.local(decay_h, decay), sems.local(merged_h, merged), sems.local(normed_h, normed)]
+    third = [sems.local(decay_h, decay), sems.local(merged_h, merged)]
     fourth = [
         sems.local(a, b)
         for a, b in ((pad_h, pad), (conv_h, conv), (rate_h, rate), (inlet_h, inlet), (wgi_h, wgi), (gmid_h, own))
     ]
     hop = Hop(at)
     at.greet(hop)
-    ring_v = Ring(at, gwv, slots_v, ring_sem.at[0], ring_sem.at[1], True)
+    ring_d = Ring(at, gwd, slots_d, ring_sem.at[0], ring_sem.at[1], False)
+    ring_v = Ring(at, gwv, slots_v, ring_sem.at[6], ring_sem.at[7], True)
     ring_o = Ring(at, go, slots_o, ring_sem.at[2], ring_sem.at[3], True)
     ring_g = Ring(at, ggi, slots_g, ring_sem.at[4], ring_sem.at[5], True)
     for c in early:
         c.wait()
     ring_v.start()
+    regroup = Regroup(at, sems, gwd_h, gwd)
+    spread_u = Spread(at, sems, last_u, came_u)
+    spread_u.start()
+    regroup.start()
+
+    def staged(came, first, size, outs, base=0):
+        rows = came.shape[1]
+        for f in range(4):
+            at_col = f * size
+            done = 0
+            while done < size:
+                block, col = divmod(at_col + done, width)
+                step = min(size - done, width - col)
+                tile[base + block * rows : base + (block + 1) * rows, col : col + step] = came[
+                    f, :, first + done : first + done + step
+                ].astype(F32)
+                done += step
+        copies, done = [], 0
+        while done < 4 * size:
+            step = min(width, 4 * size - done)
+            copies.append(
+                sems.local(tile.at[pl.ds(base + done // width * rows, rows), pl.ds(0, step)], outs.at[:, pl.ds(done, step)])
+            )
+            done += step
+        return copies
 
     def merged_rows(m, _):
         sl = rows_at(m, here)
-        work[sl, :] = mm_rt(gml[sl, :], wo[...])
+        for h in range(2):
+            work[sl, pl.ds(h * here, here)] = mm_rt(gml[sl, :], wo[h])
         return 0
 
     lax.fori_loop(0, 4, merged_rows, 0)
     for c in second:
         c.wait()
     states[0:group, :] = ends[16:24, :]
-    ring_v.step(0)
 
     def split(c, _):
         cols = pl.ds(pl.multiple_of(c * 128, 128), 128)
@@ -967,6 +1019,7 @@
         return 0
 
     lax.fori_loop(0, chans // 128, split, 0)
+    ring_v.step(0)
     for c in third:
         c.wait()
     unroll = 8
@@ -983,7 +1036,6 @@
     passed[8:16, :] = lax.fori_loop(0, blocks, totals, zero)
     line = Line(at, passed, tot, line_sem.at[0], line_sem.at[1])
     line.send(0, at.s)
-    ring_v.step(1)
 
     def out_rows(m, _):
         cols = pl.ds(pl.multiple_of(m * 256, 256), 256)
@@ -991,18 +1043,8 @@
         return 0
 
     lax.fori_loop(0, chans // 256, out_rows, 0)
-    ring_v.step(2)
-
-    def normed_rows(first):
-        def one(m, _):
-            cols = pl.ds(pl.multiple_of(m * 256, 256), 256)
-            ggi[rows_at(m, 256), first : first + chans] = mm_lt(normed[:, cols], pair[:, first : first + chans]).astype(BF)
-            return 0
-
-        return one
-
-    lax.fori_loop(0, width // 256, normed_rows(0), 0)
-    ring_v.step(3)
+    normed, core_out = gml, wo
+    fourth.append(sems.local(normed_h, normed))
 
     def enter(k, state):
         j = n - 1 - k
@@ -1021,7 +1063,9 @@
         return carry
 
     lax.fori_loop(0, blocks, scan, carry_in)
-    ring_v.step(4)
+    ring_v.step(1)
+    spread_u.wait()
+    staging = staged(came_u, 0, ffl, up_o)
     for c in fourth:
         c.wait()
     heads_r[...] = jnp.zeros_like(heads_r)
@@ -1081,7 +1125,7 @@
     go[:, width : width + 128] = heads_r[...].astype(BF)
     go[:, width + 128 :] = heads_l[...].astype(BF)
     ring_o.start()
-    ring_v.step(5)
+    ring_v.step(2)
     for k in range(8):
         small[k : k + 1, :] = jnp.sum(acc[k], axis=0, keepdims=True)
     small[7:8, :] = small[7:8, :] * chan[8:9, :]
@@ -1106,12 +1150,17 @@
 
     lax.fori_loop(0, every // 128, taps_back, 0)
     swap_rows(work, pair.at[:, pl.ds(chans, chans)], steps, BF)
-    spread_v = Spread(at, sems, last_v, value_o)
-    ring_v.last(last_v)
-    spread_v.start()
-    lax.fori_loop(0, width // 256, normed_rows(chans), 0)
+    ring_v.step(3)
+
+    def normed_rows(m, _):
+        cols = pl.ds(pl.multiple_of(m * 256, 256), 256)
+        ggi[rows_at(m, 256), :] = mm_lt(normed[:, cols], pair[...]).astype(BF)
+        return 0
+
+    lax.fori_loop(0, width // 256, normed_rows, 0)
     ring_g.start()
-    ring_o.step(0)
+    for c in staging:
+        c.wait()
 
     def back(o):
         sl = rows_at(o, here)
@@ -1124,16 +1173,23 @@
         lax.fori_loop(0, width // 512, some, 0)
 
     sc = Scatter(at, sems, core_out, core_in, over_out, over_in, toks)
-    sc.run_tile(back, tile, None, lambda k: ring_o.step(k + 1))
+
+    def between(k):
+        for j, ring, step in ((1, ring_v, 4), (2, ring_o, 0), (3, ring_v, 5)):
+
+            @pl.when(k == j)
+            def _():
+                ring.step(step)
+
+    sc.run_tile(back, tile, None, between)
     ring_g.step(0)
-    ring_o.step(5)
+    spread_v = Spread(at, sems, last_u, came_v)
+    ring_v.last(last_u)
+    spread_v.start()
+    regroup.wait()
+    ring_d.start()
+    ring_o.step(1)
     ring_g.step(1)
-    ring_o.last(last_o)
-    hops = [
-        hop.start(sems, last_o.at[:, pl.ds(0, width)], out_o),
-        hop.start(sems, last_o.at[:, pl.ds(width, 128)], rate_o),
-        hop.start(sems, last_o.at[:, pl.ds(width + 128, 128)], inlet_o),
-    ]
     gain1 = jnp.zeros((1, width), F32)
     for c in inputs:
         c.wait()
@@ -1146,15 +1202,22 @@
         gg = g * gain[...]
         mean = jnp.mean(gg * v, axis=-1, keepdims=True)
         own[sl, :] = own[sl, :] + s * gg - v * (s * s * s * mean)
-        ring_g.step(2 + r)
     saves = [sems.local(own, ginput_o)]
+    ring_d.step(0)
+    ring_g.step(2)
+    ring_o.step(2)
     for k in range(3):
         small[8 + k : 9 + k, :] = gain1[:, k * chans : (k + 1) * chans]
         small[11 + k : 12 + k, :] = gain2[0:1, k * chans : (k + 1) * chans]
     small[14:16, :] = jnp.zeros((2, chans), F32)
     share = Line(at, small, small_in, line_sem.at[2], line_sem.at[3])
     share.send(0, n)
-    ring_g.step(4)
+    ring_d.step(1)
+    spread_v.wait()
+    saves += staged(came_v, 0, ffl, value_o)
+    ring_g.step(3)
+    ring_o.step(3)
+    ring_d.step(2)
     small_in[at.s] = small[...]
 
     def arrive(j, total):
@@ -1165,65 +1228,91 @@
         return total + small_in[j]
 
     small_sum[...] = lax.fori_loop(0, n, arrive, jnp.zeros(small.shape, F32))
-    hops.append(hop.start(sems, small_sum.at[pl.ds(0, 8)], chan_o))
+    ring_g.step(4)
+    ring_o.step(4)
+    ring_d.step(3)
+    hops = [hop.start(sems, small_sum.at[pl.ds(0, 8)], chan_o)]
     lower = small_sum.at[pl.ds(8, 8)]
     around = [sems.remote(lower, group_in.at[at.f], at.group(p)) for p in (at.p1, at.p2, at.p3)]
     for c in around:
         c.start()
     group_in[at.f] = small_sum[8:16, :]
     ring_g.step(5)
-    spreads = [Spread(at, sems, last_g, gate_o, 0, chans), Spread(at, sems, last_g, input_o, chans, chans)]
+    ring_o.step(5)
+    ring_d.step(4)
+    spread_g = Spread(at, sems, last_g, came_g)
     ring_g.last(last_g)
-    for c in spreads:
-        c.start()
+    spread_g.start()
+    ring_o.last(last_o)
+    hops.append(hop.start(sems, last_o, came_o))
+    for c in saves:
+        c.wait()
+    ring_d.step(5)
+    ring_d.last(tile)
+    saves = [sems.local(tile.at[pl.ds(0, gwd.shape[0] // n)], down_o)]
+    hop.wait(hops[1])
+    crow = came_o.shape[0]
+    for k in range(thirds + 1):
+        size = min(chans, came_o.shape[1] - k * chans)
+        rate[k * crow : (k + 1) * crow, 0:size] = came_o[:, k * chans : k * chans + size].astype(F32)
+    saves += [
+        sems.local(rate.at[pl.ds(k * crow, crow)], out_o.at[:, pl.ds(k * chans, chans)]) for k in range(thirds)
+    ]
+    saves += [
+        sems.local(rate.at[pl.ds(thirds * crow, crow), pl.ds(k * 128, 128)], o) for k, o in enumerate((rate_o, inlet_o))
+    ]
     for c in around:
         c.wait()
     gains[...] = group_in[0] + group_in[1] + group_in[2] + group_in[3]
     saves += [sems.local(gains, gains_o)]
     share.sent(0, n)
     sc.finish()
-    for h in hops:
-        hop.wait(h)
-    for r in (ring_v, ring_o, ring_g):
+    for r in (ring_v, ring_d, ring_o, ring_g):
         r.finish()
-    for c in [spread_v] + spreads + saves:
+    spread_g.wait()
+    for c in saves:
         c.wait()
-
-
-def call_back(chan, wr, wl, gain, gain2, gml, merged, wo, wgi, normed, gate, pad, conv, rate, inlet, decay, states, ends, gwv, x, gmid):
+    saves = staged(came_g, 0, chans, gate_o) + staged(came_g, chans, chans, input_o, here // 2)
+    hop.wait(hops[0])
+    for c in saves:
+        c.wait()
+
+
+def call_back(chan, wr, wl, gain, gain2, gml, merged, wo, wgi, normed, gate, pad, conv, rate, inlet, decay, states, ends, gwd, x, gmid, up, value):
     every, width = gml.shape
     here = x.shape[0]
     chans = chan.shape[1]
-    ffl = gwv.shape[1]
+    ffl = gwd.shape[0]
     n = lax.axis_size("seq")
     f32 = lambda *s: jax.ShapeDtypeStruct(s, F32)
     vf = lambda *s: pltpu.VMEM(s, F32)
     vb = lambda *s: pltpu.VMEM(s, BF)
     rows, crow = width // n, chans // n
     outs = [
-        f32(here, width), f32(rows // 4, 4 * ffl), f32(rows // 4, 4 * chans), f32(rows // 4, 4 * chans), f32(crow, width),
+        f32(here, width), f32(rows // 4, 4 * ffl), f32(rows // 4, 4 * ffl), f32(ffl // n, width), f32(rows // 4, 4 * chans), f32(rows // 4, 4 * chans), f32(crow, width),
         f32(crow, 128), f32(crow, 128), f32(8, chans), f32(8, chans),
     ]
     scratch = [
-        vb(every, width), vb(every, chans), vb(chans, width), vb(width, 2 * chans), vb(every, width),
+        vb(every, width), vb(every, chans), vb(2, here, width), vb(width, 2 * chans),
         vf(every, chans), vf(every + 24, chans), vb(every, chans), vf(every, chans), vf(every, chans), vf(every, chans),
-        vf(every + 8, chans), vf(24, chans), vb(width, ffl), vf(here, width),
+        vf(every + 8, chans), vf(24, chans), vb(ffl, width), vb(width, ffl), vf(here, width),
         vf(every, chans), vf(every + 24, chans), vb(every, 2 * chans), vf(chans, 128), vf(chans, 128), vf(8, 8, chans),
-        vf(here, width), vb(2, here, width), vb(2, here, width), vb(here, width), vb(here, width),
-        vb(chans, width + 256), vb(width, 2 * chans), vb(n - 1, rows, ffl), vb(n - 1, crow, width + 256), vb(n - 1, rows, 2 * chans),
-        vf(rows, ffl), vf(crow, width + 256), vf(rows, 2 * chans),
+        vf(here, width), vb(2, here, width), vb(here, width), vb(here, width),
+        vb(chans, width + 256), vb(width, 2 * chans), vb(n - 1, ffl // n, width), vb(n - 1, rows, ffl), vb(n - 1, crow, width + 256), vb(n - 1, rows, 2 * chans),
+        vb(rows, ffl), vb(crow, width + 256), vb(rows, 2 * chans), vb(4, rows // 4, ffl), vb(4, rows // 4, ffl),
+        vb(crow, width + 256), vb(4, rows // 4, 2 * chans),
         vf(16, chans), vf(n, 16, chans), vf(16, chans), vf(n, 16, chans), vf(16, chans), vf(4, 8, chans), vf(8, chans),
-        pltpu.SemaphoreType.DMA((90,)), pltpu.SemaphoreType.DMA((6, 4, n - 1)), pltpu.SemaphoreType.DMA((4, n)),
+        pltpu.SemaphoreType.DMA((120,)), pltpu.SemaphoreType.DMA((8, 4, n - 1)), pltpu.SemaphoreType.DMA((4, n)),
     ]
     return pl.pallas_call(
         branch_back,
         out_shape=outs,
-        in_specs=[VMEM] * 5 + [ANY] * 16,
+        in_specs=[VMEM] * 5 + [ANY] * 18,
         out_specs=[ANY] * len(outs),
         scratch_shapes=scratch,
         compiler_params=pltpu.CompilerParams(collective_id=3, has_side_effects=True, vmem_limit_bytes=LIMIT),
         name="branch_back",
-    )(chan, wr, wl, gain, gain2, gml, merged, wo, wgi, normed, gate, pad, conv, rate, inlet, decay, states, ends, gwv, x, gmid)
+    )(chan, wr, wl, gain, gain2, gml, merged, wo, wgi, normed, gate, pad, conv, rate, inlet, decay, states, ends, gwd, x, gmid, up, value)
 
 
 def body(
@@ -1255,11 +1344,11 @@
     count = jnp.sum(valid_lengths).astype(F32)
     if all((v // n_seq) % 64 == 0 for v in (width, chans)):
         scale = jnp.broadcast_to(jnp.where(mask, slots / count, 0.0), (here, 128))
-        result, grad_middle, gml, gain2, down_sum, up_sum, g_value = call_mlp(
+        result, grad_middle, gml, gain2, g_down, up_part, value_part = call_mlp(
             n2, wuv, w_down, middle, teacher.reshape(here, width), scale, gain[:, 1].reshape(1, -1))
-        grad_input, value_sum, gate_sum, input_sum, out_sum, rate_sum, inlet_sum, ch, gn = call_back(
+        grad_input, up_sum, value_sum, down_sum, gate_sum, input_sum, out_sum, rate_sum, inlet_sum, ch, gn = call_back(
             chan, w_rate, w_inlet, gain[:, 0].reshape(1, -1), gain2, gml, merged, w_out, wgi, normed, gate_tm, pad_tm,
-            conv_tm, rate_tm, inlet_tm, decay_tm, states_tm, ends, g_value, x, grad_middle)
+            conv_tm, rate_tm, inlet_tm, decay_tm, states_tm, ends, g_down, x, grad_middle, up_part, value_part)
         place = si * n_fs + fi
         per = chans // n_seq
         ch = lax.dynamic_slice_in_dim(ch, lax.rem(place, n_seq) * per, per, 1)

time: 464 us -> 401 us (0.86)
  Pallas kernels: 439 us -> 373 us
    pallas_call x1, Pallas kernels: 180 us -> 122 us  [call_mlp(): pl.pallas_call(mlp, out_shape=outs, in_specs=[ANY] * 5 + [VMEM] * 2, out_...]
    pallas_call x1, Pallas kernels: 120 us -> 101 us  [call_forward(): pl.pallas_call(forward_branch, out_shape=outs, in_specs=[VMEM] * 6 + [ANY...]
    pallas_call x1, Pallas kernels: 139 us -> 150 us  [call_back(): pl.pallas_call(branch_back, out_shape=outs, in_specs=[VMEM] * 5 + [ANY] *...]
    unnamed x30 -> x28, local copies, waits for them, and re-layouts: 8.53 us -> 10 us
where the time goes in v3:
time: 401 us; the launch traced here: 399 us
  Pallas kernels  373 us (93%)
  local copies, waits for them, and re-layouts  19.7 us (5%)
  other arithmetic  4.78 us (1%)
    pallas_call x1, Pallas kernels, call_back(): pl.pallas_call(branch_back, out_shape=outs, in_specs=[VMEM] * 5 + [ANY] *...  150 us
    pallas_call x1, Pallas kernels, call_mlp(): pl.pallas_call(mlp, out_shape=outs, in_specs=[ANY] * 5 + [VMEM] * 2, out_...  122 us
    pallas_call x1, Pallas kernels, call_forward(): pl.pallas_call(forward_branch, out_shape=outs, in_specs=[VMEM] * 6 + [ANY...  101 us
    unnamed x28, local copies, waits for them, and re-layouts  10 us

profile of v3, /device:TPU:0, one launch (start us, length us, event | category | flops | bytes accessed | tf_op | source)
XLA Modules:
  0.0 398.7 jit_solution(11941782076806622415)
XLA Ops:
  0.7 1.3 reduce_sum.9
  2.7 0.7 dynamic_slice.9
  3.4 0.1 fusion.10
  3.5 0.1 pad.2.clone
  3.5 0.7 reshape.82
  4.2 0.7 reshape.83
  4.9 0.7 broadcast_in_dim.60
  5.6 0.7 broadcast_in_dim.61
  6.3 0.7 broadcast_in_dim.62
  7.0 0.7 fusion.9
  7.6 0.7 maximum_maximum_fusion.gains
  8.3 1.9 concatenate.7.chan
  10.3 0.8 broadcast_in_dim.59.scale
  11.0 101.2 %forward_branch.1 = (bf16[1536,1024]{1,0:T(8,128)(2,1)}, bf16[1536,2304]{1,0:T(8,128)(2,1)}, bf16[1024,1536]{1,0:T(8,128)(2,1)}, bf16[1024,1536]{1,0:T(8,128)(2,...) custom-call(f32[256,1536]{1,0:T(8,128)} %bitcast.26, ...), custom_call_target="tpu_custom_call" | custom-call | tf_op jit(solution)/shard_map/forward_branch/pallas_call | solution.py:559
  112.2 1.5 fusion.11
  113.7 121.9 %mlp.1 = (f32[256,1536]{1,0:T(8,128)}, f32[256,1536]{1,0:T(8,128)}, bf16[1024,1536]{1,0:T(8,128)(2,1)}, f32[8,1536]{1,0:T(8,128)}, bf16[1152,1536]{1,0:T(8,128)(...) custom-call(bf16[1024,1536]{1,0:T(8,128)(2,1)} %get-tuple-element.50.n2_h, ...), custom_call_target="tpu_custom_call" | custom-call | tf_op jit(solution)/shard_map/mlp/pallas_call | solution.py:891
  235.6 149.6 %branch_back.1 = (f32[256,1536]{1,0:T(8,128)}, f32[48,4608]{1,0:T(8,128)}, f32[48,4608]{1,0:T(8,128)}, f32[144,1536]{1,0:T(8,128)}, f32[48,2048]{1,0:T(8,128)}, ...) custom-call(f32[16,512]{1,0:T(8,128)} %concatenate.7.chan, ...), custom_call_target="tpu_custom_call" | custom-call | tf_op jit(solution)/shard_map/branch_back/pallas_call | solution.py:1307
  385.3 0.0 copy-start
  385.3 0.8 reshape.81
  386.1 0.1 constant_dynamic-slice_fusion.1
  386.2 0.5 slice_bitcast_fusion
  386.7 0.8 constant_dynamic-slice_fusion
  387.5 0.6 slice.34
  388.1 0.5 slice_bitcast_fusion.1
  388.6 2.7 copy.45
  391.2 0.0 copy-done
  391.2 0.0 copy-start.6
  391.2 0.0 copy-start.5
  391.2 0.0 copy-start.8
  391.2 0.0 copy-start.7
  391.3 0.0 copy-start.4
  391.3 0.0 copy-start.3
  391.3 1.1 copy.46
  392.4 0.0 copy-done.6
  392.4 0.0 copy-start.2
  392.4 0.7 copy.47
  393.2 0.0 copy-done.5
  393.2 0.7 copy.48
  393.9 0.0 copy-done.8
  393.9 0.6 copy.49
  394.5 0.0 copy-done.7
  394.5 0.6 copy.50
  395.2 0.0 copy-done.4
  395.2 0.0 copy-start.1
  395.2 0.7 copy.51
  395.9 0.0 copy-done.3
  395.9 0.9 copy.52
  396.8 0.0 copy-done.2
  396.8 0.9 copy.53
  397.7 0.0 copy-done.1
  397.7 0.9 copy.54
  (3 shorter events, 0.0 us)
Async XLA Ops:
  385.3 6.0 %copy-start = (f32[256,1536]{1,0:T(8,128)S(1)}, f32[256,1536]{1,0:T(8,128)}, u32[]{:S(2)}) copy-start(f32[256,1536]{1,0:T(8,128)} %get-tuple-element.72) | copy-start | bytes 4718596
  391.2 1.2 copy-start.6
  391.2 1.9 copy-start.5
  391.2 2.7 copy-start.8
  391.2 3.3 copy-start.7
  391.3 3.9 copy-start.4
  391.3 4.6 %copy-start.3 = (f32[48,4608]{1,0:T(8,128)S(1)}, f32[48,4608]{1,0:T(8,128)}, u32[]{:S(2)}) copy-start(f32[48,4608]{1,0:T(8,128)} %get-tuple-element.124) | copy-start | bytes 2654212
  392.4 4.4 %copy-start.2 = (f32[48,4608]{1,0:T(8,128)S(1)}, f32[48,4608]{1,0:T(8,128)}, u32[]{:S(2)}) copy-start(f32[48,4608]{1,0:T(8,128)} %get-tuple-element.125) | copy-start | bytes 2654212
  395.2 2.6 copy-start.1

commit v4 on v3

--- a/solution.py
+++ b/solution.py
@@ -160,9 +160,13 @@
         self.over[r].wait_recv()
         self.pass_on[r].start()
 
+    def near(self):
+        for r in range(2):
+            self.core[r].wait_recv()
+
     def finish(self):
         for r in range(2):
-            self.core[r].wait()
+            self.core[r].wait_send()
             self.over[r].wait_send()
             self.pass_on[r].wait()
 
@@ -197,8 +201,7 @@
 
         self.core[0].wait_recv()
         partial(at.p2, add_over)
-        for r in range(2):
-            self.over[r].start()
+        self.over[0].start()
         between(1)
         partial(at.p1, put(self.core_out.at[1]))
         self.core[1].start()
@@ -228,7 +231,7 @@
                 for r in range(2):
                     sl = pl.ds(r * self.chunk, self.chunk)
                     self.over_out[sl, :] = (tile[sl, :] + self.core_in[0, sl, :].astype(F32)).astype(BF)
-                    self.over[r].start()
+                self.over[0].start()
 
             @pl.when(k == 2)
             def _():
@@ -248,17 +251,21 @@
 
         lax.fori_loop(0, 4, one, 0)
 
+    def second(self):
+        self.over[0].wait_send()
+        self.over[1].start()
+
     def arrived(self, r):
         self.over[r].wait_recv()
         return self.over_in[pl.ds(r * self.chunk, self.chunk), :].astype(F32)
 
     def finish(self):
-        for copy in self.core + self.over:
+        for copy in self.core + self.over[1:]:
             copy.wait_send()
 
 
 class Columns:
-    def __init__(self, at, sems, weights, buf):
+    def __init__(self, at, sems, weights, buf, with_own=True):
         rows, width = weights[0].shape
         part = width // 4
         cut = rows // 4
@@ -272,7 +279,8 @@
             mine = pl.ds(pl.multiple_of(at.f * rows, rows), rows)
             quarter = pl.ds(pl.multiple_of(h * cut, cut), cut)
             mine_cut = pl.ds(pl.multiple_of(at.f * rows + h * cut, cut), cut)
-            self.own.append(pltpu.make_async_copy(w.at[:, take(at.f)], buf.at[mine, cols], sems.take()))
+            if with_own:
+                self.own.append(pltpu.make_async_copy(w.at[:, take(at.f)], buf.at[mine, cols], sems.take()))
             self.near.append(sems.remote(w.at[:, take(at.p1)], buf.at[mine, cols], at.group(at.p1)))
             for p in (at.p2, at.p3):
                 self.far.append(sems.remote(w.at[quarter, take(p)], buf.at[mine_cut, cols], at.group(p)))
@@ -304,6 +312,18 @@
     return jnp.where(v > -0.25, series, jnp.exp(v) - 1.0)
 
 
+def decay_rows(param):
+    small = jnp.exp(-jnp.abs(param))
+    return (
+        -RATE_SCALE * (jnp.maximum(-param, 0.0) + jnp.log1p(small)),
+        RATE_SCALE * jnp.where(param > 0.0, small, 1.0) / (1.0 + small),
+    )
+
+
+def whole_gain(gain, row):
+    return jnp.concatenate([gain[p, row : row + 1, :] for p in range(4)], axis=1)
+
+
 def swap_rows(src, dst, outer, kind):
     total, width = src.shape
     inner = total // outer
@@ -317,10 +337,10 @@
     lax.fori_loop(0, width // 128, one, 0)
 
 
-def forward_branch(x, gains, chan, wr, wl, wo, wg, wi, wu, wv,
+def forward_branch(x, gain_one, gain_two, taps_w, conv_b, rate_b, inlet_b, decay_p, wr, wl, wo, wg, wi, wu, wv,
                    wgi_o, wuv_o, normed_o, n2_o, middle_o, gate_o, pad_o, conv_o, rate_o, inlet_o, decay_o, states_o,
-                   merged_o, ends_o, gain_o,
-                   wgi, normed, n2, middle, gain, gate, pad, conv, rate, inlet, decay, states, work, merged, ends,
+                   merged_o, ends_o, gain_o, chan_o,
+                   wgi, normed, n2, middle, gains, chan, gain, gate, pad, conv, rate, inlet, decay, states, work, merged, ends,
                    tot, core_out, core_in, over_out, over_in, sem, tsend, trecv):
     at = Place()
     here, width = x.shape
@@ -332,6 +352,12 @@
     group = 8
     halo = (taps - 1) * group
     sems = Sems(sem)
+    chan[0:taps, :] = taps_w[...].astype(F32)
+    for row, v in enumerate((conv_b, rate_b, inlet_b, decay_p)):
+        chan[taps + row : taps + row + 1, :] = v[...].astype(F32).reshape(1, chans)
+    for row, v in enumerate((gain_one, gain_two)):
+        gains[row : row + 1, :] = v[...].astype(F32).reshape(1, part)
+    gains[2:8, :] = jnp.zeros((6, part), F32)
     at.greet()
 
     shares = [
@@ -343,7 +369,7 @@
     gi = Columns(at, sems, [wg, wi], wgi)
     gi.start_far()
     gi.start_near()
-    uv = Columns(at, sems, [wu, wv], wuv_o)
+    uv = Columns(at, sems, [wu, wv], wuv_o, False)
     uv.start_near()
     ag1 = Gather(at, sems, normed, toks)
     for c in shares:
@@ -361,9 +387,10 @@
     ag1.relay(0)
     uv.start_far()
     ag1.relay(1)
+    ag1.near()
     ag1.finish()
     gi.finish()
-    saves = [sems.local(normed, normed_o), sems.local(wgi, wgi_o), sems.local(gain, gain_o)]
+    saves = [sems.local(normed, normed_o), sems.local(wgi, wgi_o), sems.local(gain, gain_o), sems.local(chan, chan_o)]
 
     def branch_rows(m, _):
         sl = rows_at(m, here)
@@ -400,6 +427,8 @@
     def _():
         tail.wait_send()
 
+
+    ends[16:17, :] = decay_rows(chan[7:8, :])[0]
 
     def gates(b, _):
         for h in range(chans // 128):
@@ -414,7 +443,7 @@
             blocks = pl.ds(h * 128, 128)
             r = jax.nn.sigmoid(mm(low, wr[blocks, :]) + chan[5:6, cols])
             i = jax.nn.sigmoid(mm(low, wl[blocks, :]) + chan[6:7, cols])
-            ld = r * chan[7:8, cols]
+            ld = r * ends[16:17, cols]
             conv[sl, cols] = low
             low = low.astype(F32)
             decay[sl, cols] = jnp.exp(ld)
@@ -513,6 +542,7 @@
             uv.relay(2 * k - 3)
 
     sc.run(partial, middle, between)
+    sc.second()
     ag2 = Gather(at, sems, n2, toks)
     for r in range(2):
         sl = pl.ds(r * toks, toks)
@@ -526,6 +556,7 @@
     saves += [sems.local(middle, middle_o)]
     for r in range(2):
         ag2.relay(r)
+    ag2.near()
     ag2.finish()
     sc.finish()
     saves += [sems.local(n2, n2_o)]
@@ -534,9 +565,9 @@
         c.wait()
 
 
-def call_forward(x, gains, chan, wr, wl, wo, wg, wi, wu, wv):
+def call_forward(x, gain_one, gain_two, taps_w, conv_b, rate_b, inlet_b, decay_p, wr, wl, wo, wg, wi, wu, wv):
     here, width = x.shape
-    chans = chan.shape[1]
+    chans = taps_w.shape[1]
     ffl = wu.shape[1] // 4
     every = here * 4
     n = lax.axis_size("seq")
@@ -547,10 +578,10 @@
     outs = [
         bf(width, 2 * chans), bf(width, 2 * ffl), bf(every, width), bf(every, width), f32(here, width),
         f32(every, chans), f32(every + 24, chans), bf(every, chans), f32(every, chans), f32(every, chans),
-        f32(every, chans), f32(every, chans), bf(every, chans), f32(24, chans), f32(4, 8, width // 4),
+        f32(every, chans), f32(every, chans), bf(every, chans), f32(24, chans), f32(4, 8, width // 4), f32(8, chans),
     ]
     scratch = [
-        vb(width, 2 * chans), vb(every, width), vb(every, width), vf(here, width), vf(4, 8, width // 4),
+        vb(width, 2 * chans), vb(every, width), vb(every, width), vf(here, width), vf(8, width // 4), vf(8, chans), vf(4, 8, width // 4),
         vf(every, chans), vf(every + 24, chans), vb(every, chans), vf(every, chans), vf(every, chans),
         vf(every, chans), vf(every, chans), vf(every, chans), vb(every, chans), vf(24, chans),
         vf(n, 16, chans), vb(2, here, width), vb(2, here, width), vb(here, width), vb(here, width),
@@ -559,12 +590,12 @@
     return pl.pallas_call(
         forward_branch,
         out_shape=outs,
-        in_specs=[VMEM] * 6 + [ANY] * 4,
+        in_specs=[VMEM] * 11 + [ANY] * 4,
         out_specs=[ANY] * len(outs),
         scratch_shapes=scratch,
         compiler_params=pltpu.CompilerParams(collective_id=1, has_side_effects=True, vmem_limit_bytes=LIMIT),
         name="forward_branch",
-    )(x, gains, chan, wr, wl, wo, wg, wi, wu, wv)
+    )(x, gain_one, gain_two, taps_w, conv_b, rate_b, inlet_b, decay_p, wr, wl, wo, wg, wi, wu, wv)
 
 
 class Hop:
@@ -724,7 +755,7 @@
             c.wait()
 
 
-def mlp(n2_h, wuv_h, wd_h, middle_h, teacher_h, scale, gain,
+def mlp(n2_h, wuv_h, wu_h, wv_h, wd_h, middle_h, teacher_h, lengths, gain,
         result_o, gmid_o, gml_o, gain_o, down_o, up_o, value_o,
         n2, wuv, wd, hidden, ge, gdi, gml, middle, own, gout, tile, core_out, core_in, over_out, over_in,
         gwd, gwu, gwv, slots_u, last_u, gain_acc, sem, ring_sem):
@@ -735,7 +766,15 @@
     ffl = hidden.shape[1]
     part = width // 4
     col = 384
-    loads = [sems.local(n2_h, n2), sems.local(wuv_h, wuv), sems.local(wd_h, wd)]
+    loads = [sems.local(n2_h, n2)]
+    mine = pl.ds(pl.multiple_of(at.f * part, part), part)
+    for k, w in enumerate((wu_h, wv_h)):
+        cols = pl.ds(pl.multiple_of(at.f * ffl, 128), ffl)
+        loads.append(sems.local(w.at[:, cols], wuv.at[mine, pl.ds(k * ffl, ffl)]))
+    for p in (at.p1, at.p2, at.p3):
+        rows = pl.ds(pl.multiple_of(p * part, part), part)
+        loads.append(sems.local(wuv_h.at[rows], wuv.at[rows]))
+    loads.append(sems.local(wd_h, wd))
     loads2 = [sems.local(middle_h, middle), sems.local(middle_h, own), sems.local(teacher_h, gout)]
     at.greet()
     for c in loads + loads2:
@@ -763,31 +802,7 @@
 
         lax.fori_loop(0, width // 512, out, 0)
 
-    sc = Scatter(at, sems, core_out, core_in, over_out, over_in, toks)
-    sc.run_tile(forward, tile, own)
-    ag = Gather(at, sems, gdi, toks)
-    for r in range(2):
-        sl = pl.ds(r * toks, toks)
-        v = own[sl, :] + sc.arrived(r)
-        own[sl, :] = v
-        v = (v - gout[sl, :]) * scale[sl, 0:1]
-        v = jnp.where(scale[sl, 0:1] > 0.0, v, 0.0)
-        gout[sl, :] = v
-        gdi[rows_at(at.f * 2 + r, toks), :] = v.astype(BF)
-        ag.send(r)
-    saves = [sems.local(own, result_o)]
-    for r in range(2):
-        ag.relay(r)
-    ag.finish()
-    sc.finish()
-    saves.pop().wait()
-
-    def down_rows(m, _):
-        cols = pl.ds(pl.multiple_of(m * 128, 128), 128)
-        gwd[rows_at(m, 128), :] = mm_lt(hidden[:, cols], gdi[...]).astype(BF)
-        return 0
-
-    def hidden_rows(o, _):
+    def hidden_rows(o):
         sl = rows_at(o, here)
 
         def some(c, _):
@@ -801,6 +816,37 @@
         lax.fori_loop(0, ffl // col, some, 0)
         return 0
 
+    sc = Scatter(at, sems, core_out, core_in, over_out, over_in, toks)
+    sc.run_tile(forward, tile, own)
+    sc.second()
+    count = lengths[0]
+    for j in range(1, lengths.shape[0]):
+        count = count + lengths[j]
+    weight = (lengths.shape[0] * toks * at.n) / jnp.full((1, 1), count, jnp.int32).astype(F32)
+    place = at.s * toks + lax.broadcasted_iota(jnp.int32, (toks, 1), 0)
+    ag = Gather(at, sems, gdi, toks)
+    for r in range(2):
+        sl = pl.ds(r * toks, toks)
+        v = own[sl, :] + sc.arrived(r)
+        own[sl, :] = v
+        v = jnp.where(place < lengths[at.f * 2 + r], v - gout[sl, :], 0.0) * weight
+        gout[sl, :] = v
+        gdi[rows_at(at.f * 2 + r, toks), :] = v.astype(BF)
+        ag.send(r)
+    saves = [sems.local(own, result_o)]
+    ag.near()
+    lax.fori_loop(0, 2, lambda k, _: hidden_rows(jnp.where(k == 0, at.f, at.p1)), 0)
+    for r in range(2):
+        ag.relay(r)
+    ag.finish()
+    sc.finish()
+    saves.pop().wait()
+
+    def down_rows(m, _):
+        cols = pl.ds(pl.multiple_of(m * 128, 128), 128)
+        gwd[rows_at(m, 128), :] = mm_lt(hidden[:, cols], gdi[...]).astype(BF)
+        return 0
+
     def weight_rows(grads, first):
         def one(m, _):
             cols = pl.ds(pl.multiple_of(m * 256, 256), 256)
@@ -821,7 +867,7 @@
 
     ring_u = Ring(at, gwu, slots_u, ring_sem.at[0], ring_sem.at[1], True)
     six = width // 256
-    lax.fori_loop(0, 4, hidden_rows, 0)
+    lax.fori_loop(0, 2, lambda k, _: hidden_rows(jnp.where(k == 0, at.p2, at.p3)), 0)
     lax.fori_loop(0, six, weight_rows(gwu, 0), 0)
     ring_u.start()
     sc2 = Scatter(at, sems, core_out, core_in, over_out, over_in, toks)
@@ -832,6 +878,7 @@
             ring_u.step(k - 2)
 
     sc2.run_tile(backward, tile, None, between)
+    sc2.second()
     lax.fori_loop(0, six, weight_rows(gwv, ffl), 0)
     ring_u.step(2)
     lax.fori_loop(0, ffl // 128, down_rows, 0)
@@ -845,7 +892,7 @@
         v = middle[sl, :]
         s = lax.rsqrt(jnp.mean(v * v, axis=-1, keepdims=True) + EPS_NORM)
         acc = acc + jnp.sum(g * v * s, axis=0, keepdims=True)
-        gg = g * gain[...]
+        gg = g * whole_gain(gain, 1)
         mean = jnp.mean(gg * v, axis=-1, keepdims=True)
         new = gout[sl, :] + s * gg - v * (s * s * s * mean)
         own[sl, :] = new
@@ -859,6 +906,7 @@
     ag2.relay(1)
     ring_u.last(last_u)
     saves += [sems.local(last_u, up_o)]
+    ag2.near()
     ag2.finish()
     sc2.finish()
     saves += [sems.local(gml, gml_o)]
@@ -867,7 +915,7 @@
         c.wait()
 
 
-def call_mlp(n2, wuv, wd, middle, teacher, scale, gain):
+def call_mlp(n2, wuv, wu, wv, wd, middle, teacher, lengths, gain):
     every, width = n2.shape
     here = middle.shape[0]
     ffl = wd.shape[0]
@@ -891,12 +939,12 @@
     return pl.pallas_call(
         mlp,
         out_shape=outs,
-        in_specs=[ANY] * 5 + [VMEM] * 2,
+        in_specs=[ANY] * 7 + [pl.BlockSpec(memory_space=pltpu.SMEM), VMEM],
         out_specs=[ANY] * len(outs),
         scratch_shapes=scratch,
         compiler_params=pltpu.CompilerParams(collective_id=2, has_side_effects=True, vmem_limit_bytes=LIMIT),
         name="mlp",
-    )(n2, wuv, wd, middle, teacher, scale, gain)
+    )(n2, wuv, wu, wv, wd, middle, teacher, lengths, gain)
 
 
 class Line:
@@ -940,7 +988,7 @@
                 gml, merged, wo, wgi, gate, pad, conv, rate, inlet, decay, states, ends, gwd, gwv, own,
                 work, gconv, pair, heads_r, heads_l, acc, tile, core_in, over_out, over_in,
                 go, ggi, slots_d, slots_v, slots_o, slots_g, last_u, last_o, last_g, came_u, came_v, came_o, came_g,
-                passed, tot, small, small_in, small_sum, group_in, gains,
+                passed, tot, small, small_in, small_sum, group_in, gains, slope8,
                 sem, ring_sem, line_sem):
     at = Place()
     sems = Sems(sem)
@@ -969,9 +1017,10 @@
     ring_v = Ring(at, gwv, slots_v, ring_sem.at[6], ring_sem.at[7], True)
     ring_o = Ring(at, go, slots_o, ring_sem.at[2], ring_sem.at[3], True)
     ring_g = Ring(at, ggi, slots_g, ring_sem.at[4], ring_sem.at[5], True)
-    for c in early:
+    early[0].wait()
+    ring_v.start()
+    for c in early[1:]:
         c.wait()
-    ring_v.start()
     regroup = Regroup(at, sems, gwd_h, gwd)
     spread_u = Spread(at, sems, last_u, came_u)
     spread_u.start()
@@ -1075,13 +1124,15 @@
         gconv.at[pl.ds(0, halo)], gconv.at[pl.ds(every, halo)], at.line(lax.rem(at.s + n - 1, n))
     )
 
+    slope8[0:1, :], slope8[1:2, :] = decay_rows(chan[7:8, :])
+
     def gates(b, _):
         size = 128
         start = pl.multiple_of(b * size, size)
         sl = pl.ds(start, size)
         for h in range(chans // 128):
             cols = pl.ds(h * 128, 128)
-            sp8 = chan[7:8, cols]
+            sp8 = slope8[0:1, cols]
             r, i, dec, adj = rate[sl, cols], inlet[sl, cols], decay[sl, cols], gate[sl, cols]
             low_bf = conv[sl, cols]
             low = low_bf.astype(F32)
@@ -1128,7 +1179,7 @@
     ring_v.step(2)
     for k in range(8):
         small[k : k + 1, :] = jnp.sum(acc[k], axis=0, keepdims=True)
-    small[7:8, :] = small[7:8, :] * chan[8:9, :]
+    small[7:8, :] = small[7:8, :] * slope8[1:2, :]
 
     @pl.when(at.s < n - 1)
     def _():
@@ -1182,6 +1233,7 @@
                 ring.step(step)
 
     sc.run_tile(back, tile, None, between)
+    sc.second()
     ring_g.step(0)
     spread_v = Spread(at, sems, last_u, came_v)
     ring_v.last(last_u)
@@ -1199,7 +1251,7 @@
         v = jnp.concatenate([pad[pl.ds(k * here + r * toks, toks), :] for k in range(thirds)], axis=1)
         s = lax.rsqrt(jnp.mean(v * v, axis=-1, keepdims=True) + EPS_NORM)
         gain1 = gain1 + jnp.sum(g * v * s, axis=0, keepdims=True)
-        gg = g * gain[...]
+        gg = g * whole_gain(gain, 0)
         mean = jnp.mean(gg * v, axis=-1, keepdims=True)
         own[sl, :] = own[sl, :] + s * gg - v * (s * s * s * mean)
     saves = [sems.local(own, ginput_o)]
@@ -1301,7 +1353,7 @@
         vb(chans, width + 256), vb(width, 2 * chans), vb(n - 1, ffl // n, width), vb(n - 1, rows, ffl), vb(n - 1, crow, width + 256), vb(n - 1, rows, 2 * chans),
         vb(rows, ffl), vb(crow, width + 256), vb(rows, 2 * chans), vb(4, rows // 4, ffl), vb(4, rows // 4, ffl),
         vb(crow, width + 256), vb(4, rows // 4, 2 * chans),
-        vf(16, chans), vf(n, 16, chans), vf(16, chans), vf(n, 16, chans), vf(16, chans), vf(4, 8, chans), vf(8, chans),
+        vf(16, chans), vf(n, 16, chans), vf(16, chans), vf(n, 16, chans), vf(16, chans), vf(4, 8, chans), vf(8, chans), vf(8, chans),
         pltpu.SemaphoreType.DMA((120,)), pltpu.SemaphoreType.DMA((8, 4, n - 1)), pltpu.SemaphoreType.DMA((4, n)),
     ]
     return pl.pallas_call(
@@ -1313,6 +1365,53 @@
         compiler_params=pltpu.CompilerParams(collective_id=3, has_side_effects=True, vmem_limit_bytes=LIMIT),
         name="branch_back",
     )(chan, wr, wl, gain, gain2, gml, merged, wo, wgi, normed, gate, pad, conv, rate, inlet, decay, states, ends, gwd, x, gmid, up, value)
+
+
+def collect(chan, gains, *refs):
+    count = (len(refs) - 1 - 7) // 3
+    sources, results, small = refs[:count], refs[count : 2 * count], refs[2 * count : 2 * count + 7]
+    held, sem = refs[2 * count + 7 : -1], refs[-1]
+    loads = [pltpu.make_async_copy(a, b, sem.at[0, k]) for k, (a, b) in enumerate(zip(sources, held))]
+    copies = [pltpu.make_async_copy(a, b, sem.at[1, k]) for k, (a, b) in enumerate(zip(held, results))]
+    for c in loads:
+        c.start()
+    for a, b in zip(loads, copies):
+        a.wait()
+        b.start()
+    taps_o, bias_o, rate_o, inlet_o, decay_o, one_o, two_o = small
+    n = lax.axis_size("seq")
+    place = lax.axis_index("seq") * 4 + lax.axis_index("fsdp")
+    per, chans = taps_o.shape[1], chan.shape[1]
+    mine = pltpu.roll(chan[...], lax.rem(chans - lax.rem(place, n) * per, chans), 1)[:, :per]
+    taps_o[...] = mine[0:4, :]
+    for k, o in enumerate((bias_o, rate_o, inlet_o, decay_o)):
+        o[...] = mine[4 + k : 5 + k, :].reshape(per)
+    per = one_o.shape[0]
+    thirds = 4 * n * per // chans
+    for row, o in enumerate((one_o, two_o)):
+        line = jnp.concatenate([gains[row * thirds + k : row * thirds + k + 1, :] for k in range(thirds)], axis=1)
+        line = jnp.broadcast_to(line, (8, thirds * chans))
+        line = pltpu.roll(line, lax.rem(thirds * chans - place * per, thirds * chans), 1)
+        o[...] = line[0:1, :per].reshape(per)
+    for c in copies:
+        c.wait()
+
+
+def call_collect(chan, gains, big):
+    n = lax.axis_size("seq")
+    chans = chan.shape[1]
+    f32 = lambda *s: jax.ShapeDtypeStruct(s, F32)
+    per, own = chans // n, big[0].shape[1] // (4 * n)
+    outs = [f32(*v.shape) for v in big] + [f32(4, per)] + [f32(per)] * 4 + [f32(own)] * 2
+    return pl.pallas_call(
+        collect,
+        out_shape=outs,
+        in_specs=[VMEM] * 2 + [ANY] * len(big),
+        out_specs=[ANY] * len(big) + [VMEM] * 7,
+        scratch_shapes=[pltpu.VMEM(v.shape, F32) for v in big] + [pltpu.SemaphoreType.DMA((2, len(big)))],
+        compiler_params=pltpu.CompilerParams(has_side_effects=True, vmem_limit_bytes=LIMIT),
+        name="collect",
+    )(chan, gains, *big)
 
 
 def body(
@@ -1330,39 +1429,36 @@
     taps = conv_weight.shape[0]
 
     cw = conv_weight.astype(F32)
-    sp = jax.nn.softplus(-decay_param.astype(F32))
     x = block_input.reshape(here, width)
-    gains = jnp.concatenate([norm_gain[None].astype(F32), mlp_gain[None].astype(F32), jnp.zeros((6, width // 4), F32)])
-    vec = lambda v: v.astype(F32)[None]
-    chan = jnp.concatenate([cw, vec(conv_bias), vec(bias_rate), vec(bias_inlet), vec(-RATE_SCALE * sp), vec(RATE_SCALE * jax.nn.sigmoid(-decay_param.astype(F32))), jnp.zeros((7, chans), F32)])
-    (wgi, wuv, normed, n2, middle, gate_tm, pad_tm, conv_tm, rate_tm, inlet_tm, decay_tm, states_tm, merged, ends, gain) = call_forward(
-        x, gains, chan, w_rate, w_inlet, w_out, w_gate, w_input, w_up, w_value)
+    (wgi, wuv, normed, n2, middle, gate_tm, pad_tm, conv_tm, rate_tm, inlet_tm, decay_tm, states_tm, merged, ends, gain, chan) = call_forward(
+        x, norm_gain, mlp_gain, conv_weight, conv_bias, bias_rate, bias_inlet, decay_param, w_rate, w_inlet, w_out, w_gate, w_input, w_up, w_value)
     lens = lax.dynamic_slice_in_dim(valid_lengths, fi * rows_dev, rows_dev)
     pos = si * toks + jnp.arange(toks, dtype=jnp.int32)
     mask = (pos[None, :] < lens[:, None]).reshape(here, 1)
     slots = valid_lengths.shape[0] * toks * n_seq
     count = jnp.sum(valid_lengths).astype(F32)
     if all((v // n_seq) % 64 == 0 for v in (width, chans)):
-        scale = jnp.broadcast_to(jnp.where(mask, slots / count, 0.0), (here, 128))
         result, grad_middle, gml, gain2, g_down, up_part, value_part = call_mlp(
-            n2, wuv, w_down, middle, teacher.reshape(here, width), scale, gain[:, 1].reshape(1, -1))
+            n2, wuv, w_up, w_value, w_down, middle, teacher.reshape(here, width), valid_lengths, gain)
         grad_input, up_sum, value_sum, down_sum, gate_sum, input_sum, out_sum, rate_sum, inlet_sum, ch, gn = call_back(
-            chan, w_rate, w_inlet, gain[:, 0].reshape(1, -1), gain2, gml, merged, w_out, wgi, normed, gate_tm, pad_tm,
+            chan, w_rate, w_inlet, gain, gain2, gml, merged, w_out, wgi, normed, gate_tm, pad_tm,
             conv_tm, rate_tm, inlet_tm, decay_tm, states_tm, ends, g_down, x, grad_middle, up_part, value_part)
-        place = si * n_fs + fi
-        per = chans // n_seq
-        ch = lax.dynamic_slice_in_dim(ch, lax.rem(place, n_seq) * per, per, 1)
-        per = width // (n_seq * n_fs)
-        gn = lax.dynamic_slice_in_dim(gn[:6].reshape(2, width), place * per, per, 1)
+        (result, grad_input, up_sum, value_sum, down_sum, gate_sum, input_sum, out_sum, rate_sum, inlet_sum,
+         s_taps, s_bias, s_rate, s_inlet, s_decay, s_one, s_two) = call_collect(
+            ch, gn, [result, grad_input, up_sum, value_sum, down_sum, gate_sum, input_sum, out_sum, rate_sum, inlet_sum])
         return (
-            result.reshape(block_input.shape), grad_input.reshape(block_input.shape), gn[0], gate_sum, input_sum,
-            ch[:4], ch[4], rate_sum, ch[5], inlet_sum, ch[6], ch[7], out_sum, gn[1], up_sum, value_sum, down_sum,
+            result.reshape(block_input.shape), grad_input.reshape(block_input.shape), s_one, gate_sum, input_sum,
+            s_taps, s_bias, rate_sum, s_rate, inlet_sum, s_inlet, s_decay, out_sum, s_two, up_sum, value_sum, down_sum,
         )
 
+    sp = jax.nn.softplus(-decay_param.astype(F32))
     heads_shape = (heads, hb, hb)
     wr, wl = w_rate.reshape(heads_shape), w_inlet.reshape(heads_shape)
     wg, wi = wgi[:, :chans], wgi[:, chans:]
-    wu, wv = wuv[:, :wuv.shape[1]//2], wuv[:, wuv.shape[1]//2:]
+    ffl = w_down.shape[0]
+    own = jnp.concatenate([lax.dynamic_slice_in_dim(w, fi * ffl, ffl, 1) for w in (w_up, w_value)], 1)
+    wuv = lax.dynamic_update_slice_in_dim(wuv, own, fi * (width // n_fs), 0)
+    wu, wv = wuv[:, :ffl], wuv[:, ffl:]
     gain_one, gain_two = gain[:, 0].reshape(-1), gain[:, 1].reshape(-1)
     s1 = lax.rsqrt(jnp.mean(x * x, axis=-1, keepdims=True) + EPS_NORM)
     s2 = lax.rsqrt(jnp.mean(middle * middle, axis=-1, keepdims=True) + EPS_NORM)

time: 401 us -> 381 us (0.950)
  local copies, waits for them, and re-layouts: 19.7 us -> 0 us
  Pallas kernels: 373 us -> 379 us
  other arithmetic: 4.78 us -> 0 us
    unnamed x28 -> x0, local copies, waits for them, and re-layouts: 10 us -> none
    pallas_call x2 -> x3, Pallas kernels: 223 us -> 228 us  [the longest x1 120 us: call_mlp(): pl.pallas_call(mlp, out_shape=outs, in_specs=[ANY] * 7 + [pl.BlockSpec(me...]
where the time goes in v4:
time: 381 us; the launch traced here: 380 us
  Pallas kernels  379 us (99%)
    pallas_call x1, Pallas kernels, call_back(): pl.pallas_call(branch_back, out_shape=outs, in_specs=[VMEM] * 5 + [ANY] *...  151 us
    pallas_call x1, Pallas kernels, call_mlp(): pl.pallas_call(mlp, out_shape=outs, in_specs=[ANY] * 7 + [pl.BlockSpec(me...  120 us
    pallas_call x1, Pallas kernels, call_forward(): pl.pallas_call(forward_branch, out_shape=outs, in_specs=[VMEM] * 11 + [AN...  101 us

profile of v4, /device:TPU:0, one launch (start us, length us, event | category | flops | bytes accessed | tf_op | source)
XLA Modules:
  0.0 379.9 jit_solution(4587886447883770920)
XLA Ops:
  0.7 101.5 %forward_branch.1 = (bf16[1536,1024]{1,0:T(8,128)(2,1)}, bf16[1536,2304]{1,0:T(8,128)(2,1)}, bf16[1024,1536]{1,0:T(8,128)(2,1)}, bf16[1024,1536]{1,0:T(8,128)(2,...) custom-call(f32[256,1536]{1,0:T(8,128)} %bitcast.4, ...), custom_call_target="tpu_custom_call" | custom-call | tf_op jit(solution)/shard_map/forward_branch/pallas_call | solution.py:590
  102.1 120.1 %mlp.1 = (f32[256,1536]{1,0:T(8,128)}, f32[256,1536]{1,0:T(8,128)}, bf16[1024,1536]{1,0:T(8,128)(2,1)}, f32[8,1536]{1,0:T(8,128)}, bf16[1152,1536]{1,0:T(8,128)(...) custom-call(bf16[1024,1536]{1,0:T(8,128)(2,1)} %get-tuple-element.70.n2_h, ...), custom_call_target="tpu_custom_call" | custom-call | tf_op jit(solution)/shard_map/mlp/pallas_call | solution.py:939
  222.3 150.6 %branch_back.1 = (f32[256,1536]{1,0:T(8,128)}, f32[48,4608]{1,0:T(8,128)}, f32[48,4608]{1,0:T(8,128)}, f32[144,1536]{1,0:T(8,128)}, f32[48,2048]{1,0:T(8,128)}, ...) custom-call(f32[8,512]{1,0:T(8,128)} %get-tuple-element.68.chan, ...), custom_call_target="tpu_custom_call" | custom-call | tf_op jit(solution)/shard_map/branch_back/pallas_call | solution.py:1359
  372.9 6.8 %collect.1 = (f32[256,1536]{1,0:T(8,128)}, f32[256,1536]{1,0:T(8,128)}, f32[48,4608]{1,0:T(8,128)}, f32[48,4608]{1,0:T(8,128)}, f32[144,1536]{1,0:T(8,128)}, /*i...) custom-call(f32[8,512]{1,0:T(8,128)} %get-tuple-element.90.chan, ...), custom_call_target="tpu_custom_call" | custom-call | tf_op jit(solution)/shard_map/collect/pallas_call | solution.py:1406

commit v5 on v4

--- a/solution.py
+++ b/solution.py
@@ -287,8 +287,8 @@
                 came = buf.at[pl.ds(pl.multiple_of(p * rows + h * cut, cut), cut), cols]
                 self.side.append([sems.remote(came, came, mate) for mate in mates])
 
-    def start_far(self):
-        for c in self.far:
+    def start_far(self, first=0, end=4):
+        for c in self.far[first:end]:
             c.start()
 
     def start_near(self):
@@ -337,10 +337,10 @@
     lax.fori_loop(0, width // 128, one, 0)
 
 
-def forward_branch(x, gain_one, gain_two, taps_w, conv_b, rate_b, inlet_b, decay_p, wr, wl, wo, wg, wi, wu, wv,
+def forward_branch(x, gain_one, gain_two, taps_w, conv_b, rate_b, inlet_b, decay_p, wr, wl, wo_h, wg, wi, wu, wv,
                    wgi_o, wuv_o, normed_o, n2_o, middle_o, gate_o, pad_o, conv_o, rate_o, inlet_o, decay_o, states_o,
                    merged_o, ends_o, gain_o, chan_o,
-                   wgi, normed, n2, middle, gains, chan, gain, gate, pad, conv, rate, inlet, decay, states, work, merged, ends,
+                   wo, wgi, normed, n2, middle, gains, chan, gain, gate, pad, conv, rate, inlet, decay, states, work, merged, ends,
                    tot, core_out, core_in, over_out, over_in, sem, tsend, trecv):
     at = Place()
     here, width = x.shape
@@ -352,6 +352,7 @@
     group = 8
     halo = (taps - 1) * group
     sems = Sems(sem)
+    late = sems.local(wo_h, wo)
     chan[0:taps, :] = taps_w[...].astype(F32)
     for row, v in enumerate((conv_b, rate_b, inlet_b, decay_p)):
         chan[taps + row : taps + row + 1, :] = v[...].astype(F32).reshape(1, chans)
@@ -372,12 +373,15 @@
     uv = Columns(at, sems, [wu, wv], wuv_o, False)
     uv.start_near()
     ag1 = Gather(at, sems, normed, toks)
+    scales = []
+    for r in range(2):
+        v = x[pl.ds(r * toks, toks), :]
+        scales.append(lax.rsqrt(jnp.mean(v * v, axis=-1, keepdims=True) + EPS_NORM))
     for c in shares:
         c.wait()
     for r in range(2):
         sl = pl.ds(r * toks, toks)
-        v = x[sl, :]
-        scale = lax.rsqrt(jnp.mean(v * v, axis=-1, keepdims=True) + EPS_NORM)
+        scale = scales[r]
         for p in range(4):
             cols = pl.ds(p * part, part)
             normed[rows_at(at.f * 2 + r, toks), cols] = (x[sl, cols] * scale * gain[p, 0:1, :]).astype(BF)
@@ -497,6 +501,8 @@
         return 0
 
     lax.fori_loop(at.s + 1, at.n, sent_total, 0)
+    uv.relay(0)
+    uv.relay(1)
     ends[16:24, :] = state_in
 
     def scan(b, h):
@@ -525,6 +531,7 @@
     saves += [sems.local(merged, merged_o)]
 
     middle[...] = x[...]
+    late.wait()
     sc = Scatter(at, sems, core_out, core_in, over_out, over_in, toks)
 
     def partial(o, store):
@@ -537,9 +544,9 @@
         lax.fori_loop(0, 2, half, 0)
 
     def between(k):
-        if k >= 2:
-            uv.relay(2 * k - 4)
-            uv.relay(2 * k - 3)
+        if k == 2:
+            uv.relay(2)
+            uv.relay(3)
 
     sc.run(partial, middle, between)
     sc.second()
@@ -581,7 +588,7 @@
         f32(every, chans), f32(every, chans), bf(every, chans), f32(24, chans), f32(4, 8, width // 4), f32(8, chans),
     ]
     scratch = [
-        vb(width, 2 * chans), vb(every, width), vb(every, width), vf(here, width), vf(8, width // 4), vf(8, chans), vf(4, 8, width // 4),
+        vb(chans, width), vb(width, 2 * chans), vb(every, width), vb(every, width), vf(here, width), vf(8, width // 4), vf(8, chans), vf(4, 8, width // 4),
         vf(every, chans), vf(every + 24, chans), vb(every, chans), vf(every, chans), vf(every, chans),
         vf(every, chans), vf(every, chans), vf(every, chans), vb(every, chans), vf(24, chans),
         vf(n, 16, chans), vb(2, here, width), vb(2, here, width), vb(here, width), vb(here, width),
@@ -590,7 +597,7 @@
     return pl.pallas_call(
         forward_branch,
         out_shape=outs,
-        in_specs=[VMEM] * 11 + [ANY] * 4,
+        in_specs=[VMEM] * 10 + [ANY] * 5,
         out_specs=[ANY] * len(outs),
         scratch_shapes=scratch,
         compiler_params=pltpu.CompilerParams(collective_id=1, has_side_effects=True, vmem_limit_bytes=LIMIT),
@@ -691,12 +698,14 @@
             slot[...] = value.astype(BF)
             self.copy(i, k + 1, slot).start()
 
-    def last(self, out, after=lambda i: None):
+    def last(self, out, store=None):
         k = self.at.n - 2
         for i in range(4):
             _, value = self.summed(i, k)
-            out[self.cut[i]] = value.astype(out.dtype)
-            after(i)
+            if store is None:
+                out[self.cut[i]] = value.astype(out.dtype)
+            else:
+                store(i, value)
 
     def finish(self):
         def one(k, _):
@@ -709,10 +718,10 @@
 
 
 class Regroup:
-    def __init__(self, at, sems, src, dst):
+    def __init__(self, at, sems, src, dst, parts=None):
         size = src.shape[0] // at.n
         self.far, self.near = [], []
-        for h in range(at.n // 4):
+        for h in parts or range(at.n // 4):
             slot = dst.at[pl.ds(pl.multiple_of((at.f * (at.n // 4) + h) * size, 16), size)]
             block = lambda p: src.at[pl.ds(pl.multiple_of((p + 4 * h) * size, 16), size)]
             for p in (at.p2, at.p3, at.p1):
@@ -758,7 +767,7 @@
 def mlp(n2_h, wuv_h, wu_h, wv_h, wd_h, middle_h, teacher_h, lengths, gain,
         result_o, gmid_o, gml_o, gain_o, down_o, up_o, value_o,
         n2, wuv, wd, hidden, ge, gdi, gml, middle, own, gout, tile, core_out, core_in, over_out, over_in,
-        gwd, gwu, gwv, slots_u, last_u, gain_acc, sem, ring_sem):
+        gwd, gwu, gwv, acc_u, slots_u, last_u, gain_acc, sem, ring_sem):
     at = Place()
     sems = Sems(sem)
     here, width = middle.shape
@@ -774,10 +783,10 @@
     for p in (at.p1, at.p2, at.p3):
         rows = pl.ds(pl.multiple_of(p * part, part), part)
         loads.append(sems.local(wuv_h.at[rows], wuv.at[rows]))
-    loads.append(sems.local(wd_h, wd))
+    late = sems.local(wd_h, wd)
     loads2 = [sems.local(middle_h, middle), sems.local(middle_h, own), sems.local(teacher_h, gout)]
     at.greet()
-    for c in loads + loads2:
+    for c in loads:
         c.wait()
 
     def forward(o):
@@ -795,6 +804,10 @@
 
         lax.fori_loop(0, ffl // col, some, 0)
 
+        @pl.when(o == at.p3)
+        def _():
+            late.wait()
+
         def out(c, _):
             cols = pl.ds(pl.multiple_of(c * 512, 128), 512)
             tile[:, cols] = mm(hidden[sl, :], wd[:, cols])
@@ -817,7 +830,14 @@
         return 0
 
     sc = Scatter(at, sems, core_out, core_in, over_out, over_in, toks)
-    sc.run_tile(forward, tile, own)
+
+    def between(k):
+        @pl.when(k == 2)
+        def _():
+            for c in loads2:
+                c.wait()
+
+    sc.run_tile(forward, tile, own, between)
     sc.second()
     count = lengths[0]
     for j in range(1, lengths.shape[0]):
@@ -836,6 +856,16 @@
     saves = [sems.local(own, result_o)]
     ag.near()
     lax.fori_loop(0, 2, lambda k, _: hidden_rows(jnp.where(k == 0, at.f, at.p1)), 0)
+    chip = pl.ds(pl.multiple_of(lax.div(at.f, 2) * 2 * here, 2 * here), 2 * here)
+    other = pl.ds(pl.multiple_of((1 - lax.div(at.f, 2)) * 2 * here, 2 * here), 2 * here)
+    pair = 2 * (width // at.n)
+
+    def up_near(m, _):
+        rows = pl.ds(pl.multiple_of(m * pair, 128), pair)
+        acc_u[rows, :] = mm_lt(n2[chip, rows], ge[chip, 0:ffl])
+        return 0
+
+    lax.fori_loop(0, width // pair, up_near, 0)
     for r in range(2):
         ag.relay(r)
     ag.finish()
@@ -868,21 +898,35 @@
     ring_u = Ring(at, gwu, slots_u, ring_sem.at[0], ring_sem.at[1], True)
     six = width // 256
     lax.fori_loop(0, 2, lambda k, _: hidden_rows(jnp.where(k == 0, at.p2, at.p3)), 0)
-    lax.fori_loop(0, six, weight_rows(gwu, 0), 0)
-    ring_u.start()
+    def up_far(m):
+        rows = pl.ds(pl.multiple_of(m * pair, 128), pair)
+        gwu[rows, :] = (acc_u[rows, :] + mm_lt(n2[other, rows], ge[other, 0:ffl])).astype(BF)
+        return 0
+
     sc2 = Scatter(at, sems, core_out, core_in, over_out, over_in, toks)
 
     def between(k):
-        @pl.when(k >= 2)
+        @pl.when(k == 1)
         def _():
-            ring_u.step(k - 2)
+            z = lax.div(at.s, 2)
+            behind = lax.div(ring_u.owner(lax.rem(ring_u.q + at.n - 1, at.n)), 2)
+            ahead = lax.div(ring_u.owner(lax.rem(ring_u.q + 1, at.n)), 2)
+            lax.fori_loop(0, 2, lambda k, _: up_far(jnp.where(k == 0, behind, ahead)), 0)
+            ring_u.start()
+            at_end = jnp.logical_or(z == 0, z == 3)
+            rest = lambda p: jnp.where(at_end, lax.rem(p + 2, 4), p + 1 - 2 * lax.rem(p, 2))
+            lax.fori_loop(0, 2, lambda k, _: up_far(jnp.where(k == 0, rest(behind), rest(ahead))), 0)
+
+        @pl.when(k == 3)
+        def _():
+            ring_u.step(0)
 
     sc2.run_tile(backward, tile, None, between)
     sc2.second()
     lax.fori_loop(0, six, weight_rows(gwv, ffl), 0)
+    ring_u.step(1)
+    lax.fori_loop(0, ffl // 128, down_rows, 0)
     ring_u.step(2)
-    lax.fori_loop(0, ffl // 128, down_rows, 0)
-    ring_u.step(3)
     saves += [sems.local(gwv, value_o), sems.local(gwd, down_o)]
     ag2 = Gather(at, sems, gml, toks)
     acc = jnp.zeros((1, width), F32)
@@ -900,6 +944,7 @@
         ag2.send(r)
     gain_acc[...] = jnp.broadcast_to(acc, gain_acc.shape)
     saves += [sems.local(own, gmid_o), sems.local(gain_acc, gain_o)]
+    ring_u.step(3)
     ring_u.step(4)
     ag2.relay(0)
     ring_u.step(5)
@@ -932,7 +977,7 @@
         vb(every, width), vb(width, 2 * ffl), vb(ffl, width), vb(every, ffl), vb(every, 2 * ffl), vb(every, width),
         vb(every, width), vf(here, width), vf(here, width), vf(here, width), vf(here, width),
         vb(2, here, width), vb(2, here, width), vb(here, width), vb(here, width),
-        vb(ffl, width), vb(width, ffl), vb(width, ffl), vb(n - 1, width // n, ffl),
+        vb(ffl, width), vb(width, ffl), vb(width, ffl), vf(width, ffl), vb(n - 1, width // n, ffl),
         vb(width // n, ffl), vf(8, width),
         pltpu.SemaphoreType.DMA((100,)), pltpu.SemaphoreType.DMA((2, 4, n - 1)),
     ]
@@ -987,7 +1032,7 @@
                 ginput_o, up_o, value_o, down_o, gate_o, input_o, out_o, rate_o, inlet_o, chan_o, gains_o,
                 gml, merged, wo, wgi, gate, pad, conv, rate, inlet, decay, states, ends, gwd, gwv, own,
                 work, gconv, pair, heads_r, heads_l, acc, tile, core_in, over_out, over_in,
-                go, ggi, slots_d, slots_v, slots_o, slots_g, last_u, last_o, last_g, came_u, came_v, came_o, came_g,
+                go, ggi, slots_d, slots_v, slots_o, slots_g, last_u, came_u, came_v, go_own,
                 passed, tot, small, small_in, small_sum, group_in, gains, slope8,
                 sem, ring_sem, line_sem):
     at = Place()
@@ -1015,16 +1060,16 @@
     at.greet(hop)
     ring_d = Ring(at, gwd, slots_d, ring_sem.at[0], ring_sem.at[1], False)
     ring_v = Ring(at, gwv, slots_v, ring_sem.at[6], ring_sem.at[7], True)
-    ring_o = Ring(at, go, slots_o, ring_sem.at[2], ring_sem.at[3], True)
+    ring_o = Ring(at, go_own, slots_o, ring_sem.at[2], ring_sem.at[3], True)
     ring_g = Ring(at, ggi, slots_g, ring_sem.at[4], ring_sem.at[5], True)
     early[0].wait()
     ring_v.start()
     for c in early[1:]:
         c.wait()
-    regroup = Regroup(at, sems, gwd_h, gwd)
+    regroup = [Regroup(at, sems, gwd_h, gwd, part) for part in (range(n // 8), range(n // 8, n // 4))]
     spread_u = Spread(at, sems, last_u, came_u)
     spread_u.start()
-    regroup.start()
+    regroup[0].start()
 
     def staged(came, first, size, outs, base=0):
         rows = came.shape[1]
@@ -1175,7 +1220,8 @@
     ]
     go[:, width : width + 128] = heads_r[...].astype(BF)
     go[:, width + 128 :] = heads_l[...].astype(BF)
-    ring_o.start()
+    regroup_o = Regroup(at, sems, go, go_own)
+    regroup_o.start()
     ring_v.step(2)
     for k in range(8):
         small[k : k + 1, :] = jnp.sum(acc[k], axis=0, keepdims=True)
@@ -1226,7 +1272,7 @@
     sc = Scatter(at, sems, core_out, core_in, over_out, over_in, toks)
 
     def between(k):
-        for j, ring, step in ((1, ring_v, 4), (2, ring_o, 0), (3, ring_v, 5)):
+        for j, ring, step in ((1, ring_v, 4), (2, ring_g, 0), (3, ring_v, 5)):
 
             @pl.when(k == j)
             def _():
@@ -1234,14 +1280,13 @@
 
     sc.run_tile(back, tile, None, between)
     sc.second()
-    ring_g.step(0)
     spread_v = Spread(at, sems, last_u, came_v)
     ring_v.last(last_u)
     spread_v.start()
-    regroup.wait()
-    ring_d.start()
-    ring_o.step(1)
     ring_g.step(1)
+    regroup_o.wait()
+    ring_o.start()
+    ring_g.step(2)
     gain1 = jnp.zeros((1, width), F32)
     for c in inputs:
         c.wait()
@@ -1254,22 +1299,20 @@
         gg = g * whole_gain(gain, 0)
         mean = jnp.mean(gg * v, axis=-1, keepdims=True)
         own[sl, :] = own[sl, :] + s * gg - v * (s * s * s * mean)
+    regroup[1].start()
     saves = [sems.local(own, ginput_o)]
-    ring_d.step(0)
-    ring_g.step(2)
-    ring_o.step(2)
+    ring_o.step(0)
+    ring_g.step(3)
     for k in range(3):
         small[8 + k : 9 + k, :] = gain1[:, k * chans : (k + 1) * chans]
         small[11 + k : 12 + k, :] = gain2[0:1, k * chans : (k + 1) * chans]
     small[14:16, :] = jnp.zeros((2, chans), F32)
     share = Line(at, small, small_in, line_sem.at[2], line_sem.at[3])
     share.send(0, n)
-    ring_d.step(1)
+    ring_o.step(1)
+    ring_g.step(4)
     spread_v.wait()
     saves += staged(came_v, 0, ffl, value_o)
-    ring_g.step(3)
-    ring_o.step(3)
-    ring_d.step(2)
     small_in[at.s] = small[...]
 
     def arrive(j, total):
@@ -1280,52 +1323,69 @@
         return total + small_in[j]
 
     small_sum[...] = lax.fori_loop(0, n, arrive, jnp.zeros(small.shape, F32))
-    ring_g.step(4)
-    ring_o.step(4)
-    ring_d.step(3)
+    ring_o.step(2)
+    ring_g.step(5)
     hops = [hop.start(sems, small_sum.at[pl.ds(0, 8)], chan_o)]
     lower = small_sum.at[pl.ds(8, 8)]
     around = [sems.remote(lower, group_in.at[at.f], at.group(p)) for p in (at.p1, at.p2, at.p3)]
     for c in around:
         c.start()
     group_in[at.f] = small_sum[8:16, :]
-    ring_g.step(5)
-    ring_o.step(5)
-    ring_d.step(4)
+    ring_o.step(3)
+    last_g = last_u.at[:, pl.ds(0, 2 * chans)]
+    ring_g.last(last_g)
+    for c in regroup:
+        c.wait()
+    ring_d.start()
+    for c in around:
+        c.wait()
+    gains[...] = group_in[0] + group_in[1] + group_in[2] + group_in[3]
+    came_g = came_u.at[:, :, pl.ds(0, 2 * chans)]
     spread_g = Spread(at, sems, last_g, came_g)
-    ring_g.last(last_g)
     spread_g.start()
-    ring_o.last(last_o)
-    hops.append(hop.start(sems, last_o, came_o))
+    ring_o.step(4)
+    ring_d.step(0)
     for c in saves:
         c.wait()
-    ring_d.step(5)
-    ring_d.last(tile)
-    saves = [sems.local(tile.at[pl.ds(0, gwd.shape[0] // n)], down_o)]
-    hop.wait(hops[1])
-    crow = came_o.shape[0]
-    for k in range(thirds + 1):
-        size = min(chans, came_o.shape[1] - k * chans)
-        rate[k * crow : (k + 1) * crow, 0:size] = came_o[:, k * chans : k * chans + size].astype(F32)
+    saves = [sems.local(gains, gains_o)]
+    ring_o.step(5)
+    ring_d.step(1)
+    crow = rate_o.shape[0]
+
+    def store_out(i, value):
+        rows = ring_o.cut[i][0]
+        for k in range(thirds + 1):
+            size = min(chans, width + 256 - k * chans)
+            rate[pl.ds(k * crow + rows.start, rows.size), 0:size] = value[:, k * chans : k * chans + size]
+
+    ring_o.last(None, store_out)
     saves += [
         sems.local(rate.at[pl.ds(k * crow, crow)], out_o.at[:, pl.ds(k * chans, chans)]) for k in range(thirds)
     ]
     saves += [
         sems.local(rate.at[pl.ds(thirds * crow, crow), pl.ds(k * 128, 128)], o) for k, o in enumerate((rate_o, inlet_o))
     ]
-    for c in around:
-        c.wait()
-    gains[...] = group_in[0] + group_in[1] + group_in[2] + group_in[3]
-    saves += [sems.local(gains, gains_o)]
+    ring_d.step(2)
+    spread_g.wait()
+    saves += staged(came_g, 0, chans, gate_o) + staged(came_g, chans, chans, input_o, here // 2)
     share.sent(0, n)
     sc.finish()
-    for r in (ring_v, ring_d, ring_o, ring_g):
+    hop.wait(hops[0])
+    for r in (ring_v, ring_o, ring_g):
         r.finish()
-    spread_g.wait()
-    for c in saves:
-        c.wait()
-    saves = staged(came_g, 0, chans, gate_o) + staged(came_g, chans, chans, input_o, here // 2)
-    hop.wait(hops[0])
+    ring_d.step(3)
+    ring_d.step(4)
+    ring_d.step(5)
+    drow, dcol = gwd.shape[0] // n, width // 4
+
+    def store_down(i, value):
+        work[i * drow : (i + 1) * drow, 0:dcol] = value
+
+    ring_d.last(None, store_down)
+    saves += [
+        sems.local(work.at[pl.ds(i * drow, drow), pl.ds(0, dcol)], down_o.at[:, pl.ds(i * dcol, dcol)]) for i in range(4)
+    ]
+    ring_d.finish()
     for c in saves:
         c.wait()
 
@@ -1351,10 +1411,9 @@
         vf(every, chans), vf(every + 24, chans), vb(every, 2 * chans), vf(chans, 128), vf(chans, 128), vf(8, 8, chans),
         vf(here, width), vb(2, here, width), vb(here, width), vb(here, width),
         vb(chans, width + 256), vb(width, 2 * chans), vb(n - 1, ffl // n, width), vb(n - 1, rows, ffl), vb(n - 1, crow, width + 256), vb(n - 1, rows, 2 * chans),
-        vb(rows, ffl), vb(crow, width + 256), vb(rows, 2 * chans), vb(4, rows // 4, ffl), vb(4, rows // 4, ffl),
-        vb(crow, width + 256), vb(4, rows // 4, 2 * chans),
+        vb(rows, ffl), vb(4, rows // 4, ffl), vb(4, rows // 4, ffl), vb(chans, width + 256),
         vf(16, chans), vf(n, 16, chans), vf(16, chans), vf(n, 16, chans), vf(16, chans), vf(4, 8, chans), vf(8, chans), vf(8, chans),
-        pltpu.SemaphoreType.DMA((120,)), pltpu.SemaphoreType.DMA((8, 4, n - 1)), pltpu.SemaphoreType.DMA((4, n)),
+        pltpu.SemaphoreType.DMA((140,)), pltpu.SemaphoreType.DMA((8, 4, n - 1)), pltpu.SemaphoreType.DMA((4, n)),
     ]
     return pl.pallas_call(
         branch_back,
@@ -1437,7 +1496,7 @@
     mask = (pos[None, :] < lens[:, None]).reshape(here, 1)
     slots = valid_lengths.shape[0] * toks * n_seq
     count = jnp.sum(valid_lengths).astype(F32)
-    if all((v // n_seq) % 64 == 0 for v in (width, chans)):
+    if n_seq == 8 and all((v // n_seq) % 64 == 0 for v in (width, chans)):
         result, grad_middle, gml, gain2, g_down, up_part, value_part = call_mlp(
             n2, wuv, w_up, w_value, w_down, middle, teacher.reshape(here, width), valid_lengths, gain)
         grad_input, up_sum, value_sum, down_sum, gate_sum, input_sum, out_sum, rate_sum, inlet_sum, ch, gn = call_back(

time: 381 us -> 363 us (0.953)
  Pallas kernels: 379 us -> 362 us
    pallas_call x1, Pallas kernels: 120 us -> 112 us  [call_mlp(): pl.pallas_call(mlp, out_shape=outs, in_specs=[ANY] * 7 + [pl.BlockSpec(me...]
    pallas_call x1, Pallas kernels: 151 us -> 143 us  [call_back(): pl.pallas_call(branch_back, out_shape=outs, in_specs=[VMEM] * 5 + [ANY] *...]
where the time goes in v5:
time: 363 us
  Pallas kernels  362 us (100%)
    pallas_call x1, Pallas kernels, call_back(): pl.pallas_call(branch_back, out_shape=outs, in_specs=[VMEM] * 5 + [ANY] *...  143 us
    pallas_call x1, Pallas kernels, call_mlp(): pl.pallas_call(mlp, out_shape=outs, in_specs=[ANY] * 7 + [pl.BlockSpec(me...  112 us
    pallas_call x1, Pallas kernels, call_forward(): pl.pallas_call(forward_branch, out_shape=outs, in_specs=[VMEM] * 10 + [AN...  100 us

profile of v5, /device:TPU:0, one launch (start us, length us, event | category | flops | bytes accessed | tf_op | source)
XLA Modules:
  0.0 362.8 jit_solution(13486017144645658268)
XLA Ops:
  0.7 100.0 %forward_branch.1 = (bf16[1536,1024]{1,0:T(8,128)(2,1)}, bf16[1536,2304]{1,0:T(8,128)(2,1)}, bf16[1024,1536]{1,0:T(8,128)(2,1)}, bf16[1024,1536]{1,0:T(8,128)(2,...) custom-call(f32[256,1536]{1,0:T(8,128)} %bitcast.4, ...), custom_call_target="tpu_custom_call" | custom-call | tf_op jit(solution)/shard_map/forward_branch/pallas_call | solution.py:597
  100.7 111.9 %mlp.1 = (f32[256,1536]{1,0:T(8,128)}, f32[256,1536]{1,0:T(8,128)}, bf16[1024,1536]{1,0:T(8,128)(2,1)}, f32[8,1536]{1,0:T(8,128)}, bf16[1152,1536]{1,0:T(8,128)(...) custom-call(bf16[1024,1536]{1,0:T(8,128)(2,1)} %get-tuple-element.70.n2_h, ...), custom_call_target="tpu_custom_call" | custom-call | tf_op jit(solution)/shard_map/mlp/pallas_call | solution.py:984
  212.6 143.2 %branch_back.1 = (f32[256,1536]{1,0:T(8,128)}, f32[48,4608]{1,0:T(8,128)}, f32[48,4608]{1,0:T(8,128)}, f32[144,1536]{1,0:T(8,128)}, f32[48,2048]{1,0:T(8,128)}, ...) custom-call(f32[8,512]{1,0:T(8,128)} %get-tuple-element.68.chan, ...), custom_call_target="tpu_custom_call" | custom-call | tf_op jit(solution)/shard_map/branch_back/pallas_call | solution.py:1418
  355.8 6.8 %collect.1 = (f32[256,1536]{1,0:T(8,128)}, f32[256,1536]{1,0:T(8,128)}, f32[48,4608]{1,0:T(8,128)}, f32[48,4608]{1,0:T(8,128)}, f32[144,1536]{1,0:T(8,128)}, /*i...) custom-call(f32[8,512]{1,0:T(8,128)} %get-tuple-element.90.chan, ...), custom_call_target="tpu_custom_call" | custom-call | tf_op jit(solution)/shard_map/collect/pallas_call | solution.py:1465

commit v6 on v5

--- a/solution.py
+++ b/solution.py
@@ -265,7 +265,7 @@
 
 
 class Columns:
-    def __init__(self, at, sems, weights, buf, with_own=True):
+    def __init__(self, at, sems, weights, buf, with_own=True, first=0):
         rows, width = weights[0].shape
         part = width // 4
         cut = rows // 4
@@ -274,7 +274,7 @@
         mates = [at.line(at.s - h + m) for m in (one, lax.rem(h + 2, 4), lax.rem(one + 2, 4))]
         self.near, self.own, self.far, self.side = [], [], [], []
         for k, w in enumerate(weights):
-            cols = pl.ds(k * part, part)
+            cols = pl.ds(first + k * part, part)
             take = lambda f: pl.ds(pl.multiple_of(f * part, 128), part)
             mine = pl.ds(pl.multiple_of(at.f * rows, rows), rows)
             quarter = pl.ds(pl.multiple_of(h * cut, cut), cut)
@@ -337,13 +337,13 @@
     lax.fori_loop(0, width // 128, one, 0)
 
 
-def forward_branch(x, gain_one, gain_two, taps_w, conv_b, rate_b, inlet_b, decay_p, wr, wl, wo_h, wg, wi, wu, wv,
+def forward_branch(x_h, gain_one, gain_two, taps_w, conv_b, rate_b, inlet_b, decay_p, wr, wl, wo_h, wg, wi, wu, wv,
                    wgi_o, wuv_o, normed_o, n2_o, middle_o, gate_o, pad_o, conv_o, rate_o, inlet_o, decay_o, states_o,
                    merged_o, ends_o, gain_o, chan_o,
-                   wo, wgi, normed, n2, middle, gains, chan, gain, gate, pad, conv, rate, inlet, decay, states, work, merged, ends,
+                   wo, wgi, normed, n2, middle, gains, chan, gain, gate, pad, conv, rate, inlet, decay, states, work, hold, merged, ends,
                    tot, core_out, core_in, over_out, over_in, sem, tsend, trecv):
     at = Place()
-    here, width = x.shape
+    here, width = middle.shape
     toks = here // 2
     chans = chan.shape[1]
     part = width // 4
@@ -352,6 +352,7 @@
     group = 8
     halo = (taps - 1) * group
     sems = Sems(sem)
+    x, first = middle, sems.local(x_h, middle)
     late = sems.local(wo_h, wo)
     chan[0:taps, :] = taps_w[...].astype(F32)
     for row, v in enumerate((conv_b, rate_b, inlet_b, decay_p)):
@@ -367,12 +368,15 @@
     for c in shares:
         c.start()
     gain[at.f] = gains[...]
-    gi = Columns(at, sems, [wg, wi], wgi)
-    gi.start_far()
-    gi.start_near()
+    ci = Columns(at, sems, [wi], wgi, True, chans)
+    ci.start_far()
+    ci.start_near()
+    cg = Columns(at, sems, [wg], wgi)
+    cg.start_near()
     uv = Columns(at, sems, [wu, wv], wuv_o, False)
     uv.start_near()
     ag1 = Gather(at, sems, normed, toks)
+    first.wait()
     scales = []
     for r in range(2):
         v = x[pl.ds(r * toks, toks), :]
@@ -386,15 +390,16 @@
             cols = pl.ds(p * part, part)
             normed[rows_at(at.f * 2 + r, toks), cols] = (x[sl, cols] * scale * gain[p, 0:1, :]).astype(BF)
         ag1.send(r)
-    for k in range(4):
-        gi.relay(k)
+    for k in range(2):
+        ci.relay(k)
     ag1.relay(0)
-    uv.start_far()
+    cg.start_far()
+    uv.start_far(0, 2)
     ag1.relay(1)
     ag1.near()
     ag1.finish()
-    gi.finish()
-    saves = [sems.local(normed, normed_o), sems.local(wgi, wgi_o), sems.local(gain, gain_o), sems.local(chan, chan_o)]
+    ci.finish()
+    saves = [sems.local(normed, normed_o), sems.local(gain, gain_o), sems.local(chan, chan_o)]
 
     def branch_rows(m, _):
         sl = rows_at(m, here)
@@ -415,22 +420,9 @@
     def _():
         pad[0:halo, :] = jnp.zeros((halo, chans), F32)
 
-    def gate_rows(m, _):
-        sl = rows_at(m, here)
-        work[sl, :] = mm(normed[sl, :], wgi[:, :chans])
-        return 0
-
-    lax.fori_loop(0, 4, gate_rows, 0)
-    swap_rows(work, gate, group, F32)
-
-    @pl.when(at.s > 0)
-    def _():
-        tail.wait_recv()
-
-    @pl.when(at.s < at.n - 1)
-    def _():
-        tail.wait_send()
-
+    for k in range(2):
+        cg.relay(k)
+    uv.start_far(2, 4)
 
     ends[16:17, :] = decay_rows(chan[7:8, :])[0]
 
@@ -456,9 +448,20 @@
             inlet[sl, cols] = i
         return 0
 
-    lax.fori_loop(0, steps * group // 128, gates, 0)
+    lax.fori_loop(1, steps * group // 128, gates, 0)
+
+    @pl.when(at.s > 0)
+    def _():
+        tail.wait_recv()
+
+    @pl.when(at.s < at.n - 1)
+    def _():
+        tail.wait_send()
+
+
+    gates(0, 0)
     saves += [
-        sems.local(gate, gate_o), sems.local(pad, pad_o), sems.local(conv, conv_o), sems.local(rate, rate_o),
+        sems.local(pad, pad_o), sems.local(conv, conv_o), sems.local(rate, rate_o),
         sems.local(inlet, inlet_o), sems.local(decay, decay_o),
     ]
 
@@ -489,6 +492,18 @@
         return 0
 
     lax.fori_loop(at.s + 1, at.n, send_total, 0)
+    cg.finish()
+    saves.append(sems.local(wgi, wgi_o))
+
+    def gate_rows(m, _):
+        sl = rows_at(m, here)
+        hold[sl, :] = mm(normed[sl, :], wgi[:, :chans])
+        return 0
+
+    lax.fori_loop(0, 4, gate_rows, 0)
+    swap_rows(hold, gate, group, F32)
+
+    saves.append(sems.local(gate, gate_o))
 
     def enter(j, state):
         total_copy(j, j).wait_recv()
@@ -530,7 +545,6 @@
     swap_rows(work, merged, steps, BF)
     saves += [sems.local(merged, merged_o)]
 
-    middle[...] = x[...]
     late.wait()
     sc = Scatter(at, sems, core_out, core_in, over_out, over_in, toks)
 
@@ -590,14 +604,14 @@
     scratch = [
         vb(chans, width), vb(width, 2 * chans), vb(every, width), vb(every, width), vf(here, width), vf(8, width // 4), vf(8, chans), vf(4, 8, width // 4),
         vf(every, chans), vf(every + 24, chans), vb(every, chans), vf(every, chans), vf(every, chans),
-        vf(every, chans), vf(every, chans), vf(every, chans), vb(every, chans), vf(24, chans),
+        vf(every, chans), vf(every, chans), vf(every, chans), vf(every, chans), vb(every, chans), vf(24, chans),
         vf(n, 16, chans), vb(2, here, width), vb(2, here, width), vb(here, width), vb(here, width),
         pltpu.SemaphoreType.DMA((170,)), pltpu.SemaphoreType.DMA((n,)), pltpu.SemaphoreType.DMA((n,)),
     ]
     return pl.pallas_call(
         forward_branch,
         out_shape=outs,
-        in_specs=[VMEM] * 10 + [ANY] * 5,
+        in_specs=[ANY] + [VMEM] * 9 + [ANY] * 5,
         out_specs=[ANY] * len(outs),
         scratch_shapes=scratch,
         compiler_params=pltpu.CompilerParams(collective_id=1, has_side_effects=True, vmem_limit_bytes=LIMIT),
@@ -952,9 +966,10 @@
     ring_u.last(last_u)
     saves += [sems.local(last_u, up_o)]
     ag2.near()
+    saves += [sems.local(gml.at[chip], gml_o.at[chip])]
     ag2.finish()
+    saves += [sems.local(gml.at[other], gml_o.at[other])]
     sc2.finish()
-    saves += [sems.local(gml, gml_o)]
     ring_u.finish()
     for c in saves:
         c.wait()
@@ -1026,11 +1041,11 @@
         self.copy(j, j).wait_recv()
 
 
-def branch_back(chan, wr, wl, gain, gain2,
+def branch_back(chan_h, wr_h, wl_h, gain_h, gain2_h,
                 gml_h, merged_h, wo_h, wgi_h, normed_h, gate_h, pad_h, conv_h, rate_h, inlet_h, decay_h, states_h, ends_h,
                 gwd_h, x_h, gmid_h, up_h, value_h,
                 ginput_o, up_o, value_o, down_o, gate_o, input_o, out_o, rate_o, inlet_o, chan_o, gains_o,
-                gml, merged, wo, wgi, gate, pad, conv, rate, inlet, decay, states, ends, gwd, gwv, own,
+                chan, wr, wl, gain, gain2, gml, merged, wo, wgi, gate, pad, conv, rate, inlet, decay, states, ends, gwd, gwv, own,
                 work, gconv, pair, heads_r, heads_l, acc, tile, core_in, over_out, over_in,
                 go, ggi, slots_d, slots_v, slots_o, slots_g, last_u, came_u, came_v, go_own,
                 passed, tot, small, small_in, small_sum, group_in, gains, slope8,
@@ -1055,6 +1070,10 @@
     fourth = [
         sems.local(a, b)
         for a, b in ((pad_h, pad), (conv_h, conv), (rate_h, rate), (inlet_h, inlet), (wgi_h, wgi), (gmid_h, own))
+    ]
+    fourth += [
+        sems.local(a, b)
+        for a, b in ((chan_h, chan), (wr_h, wr), (wl_h, wl), (gain_h, gain), (gain2_h, gain2))
     ]
     hop = Hop(at)
     at.greet(hop)
@@ -1405,6 +1424,7 @@
         f32(crow, 128), f32(crow, 128), f32(8, chans), f32(8, chans),
     ]
     scratch = [
+        vf(8, chans), vb(chans, 128), vb(chans, 128), vf(4, 8, width // 4), vf(8, width),
         vb(every, width), vb(every, chans), vb(2, here, width), vb(width, 2 * chans),
         vf(every, chans), vf(every + 24, chans), vb(every, chans), vf(every, chans), vf(every, chans), vf(every, chans),
         vf(every + 8, chans), vf(24, chans), vb(ffl, width), vb(width, ffl), vf(here, width),
@@ -1413,12 +1433,12 @@
         vb(chans, width + 256), vb(width, 2 * chans), vb(n - 1, ffl // n, width), vb(n - 1, rows, ffl), vb(n - 1, crow, width + 256), vb(n - 1, rows, 2 * chans),
         vb(rows, ffl), vb(4, rows // 4, ffl), vb(4, rows // 4, ffl), vb(chans, width + 256),
         vf(16, chans), vf(n, 16, chans), vf(16, chans), vf(n, 16, chans), vf(16, chans), vf(4, 8, chans), vf(8, chans), vf(8, chans),
-        pltpu.SemaphoreType.DMA((140,)), pltpu.SemaphoreType.DMA((8, 4, n - 1)), pltpu.SemaphoreType.DMA((4, n)),
+        pltpu.SemaphoreType.DMA((150,)), pltpu.SemaphoreType.DMA((8, 4, n - 1)), pltpu.SemaphoreType.DMA((4, n)),
     ]
     return pl.pallas_call(
         branch_back,
         out_shape=outs,
-        in_specs=[VMEM] * 5 + [ANY] * 18,
+        in_specs=[ANY] * 23,
         out_specs=[ANY] * len(outs),
         scratch_shapes=scratch,
         compiler_params=pltpu.CompilerParams(collective_id=3, has_side_effects=True, vmem_limit_bytes=LIMIT),

time: 363 us -> 358 us (0.986)
  Pallas kernels: 362 us -> 357 us
    pallas_call x2, Pallas kernels: 243 us -> 237 us  [the longest x1 141 us: call_back(): pl.pallas_call(branch_back, out_shape=outs, in_specs=[ANY] * 23, out_spec...]
where the time goes in v6:
time: 358 us
  Pallas kernels  357 us (100%)
    pallas_call x1, Pallas kernels, call_back(): pl.pallas_call(branch_back, out_shape=outs, in_specs=[ANY] * 23, out_spec...  141 us
    pallas_call x1, Pallas kernels, call_mlp(): pl.pallas_call(mlp, out_shape=outs, in_specs=[ANY] * 7 + [pl.BlockSpec(me...  113 us
    pallas_call x1, Pallas kernels, call_forward(): pl.pallas_call(forward_branch, out_shape=outs, in_specs=[ANY] + [VMEM] *...  95.1 us

profile of v6, /device:TPU:0, one launch (start us, length us, event | category | flops | bytes accessed | tf_op | source)
XLA Modules:
  0.0 357.6 jit_solution(14161806684196256052)
XLA Ops:
  0.7 95.1 %forward_branch.1 = (bf16[1536,1024]{1,0:T(8,128)(2,1)}, bf16[1536,2304]{1,0:T(8,128)(2,1)}, bf16[1024,1536]{1,0:T(8,128)(2,1)}, bf16[1024,1536]{1,0:T(8,128)(2,...) custom-call(f32[256,1536]{1,0:T(8,128)} %bitcast.4, ...), custom_call_target="tpu_custom_call" | custom-call | tf_op jit(solution)/shard_map/forward_branch/pallas_call | solution.py:611
  95.8 113.4 %mlp.1 = (f32[256,1536]{1,0:T(8,128)}, f32[256,1536]{1,0:T(8,128)}, bf16[1024,1536]{1,0:T(8,128)(2,1)}, f32[8,1536]{1,0:T(8,128)}, bf16[1152,1536]{1,0:T(8,128)(...) custom-call(bf16[1024,1536]{1,0:T(8,128)(2,1)} %get-tuple-element.70.n2_h, ...), custom_call_target="tpu_custom_call" | custom-call | tf_op jit(solution)/shard_map/mlp/pallas_call | solution.py:999
  209.1 141.4 %branch_back.1 = (f32[256,1536]{1,0:T(8,128)}, f32[48,4608]{1,0:T(8,128)}, f32[48,4608]{1,0:T(8,128)}, f32[144,1536]{1,0:T(8,128)}, f32[48,2048]{1,0:T(8,128)}, ...) custom-call(f32[8,512]{1,0:T(8,128)} %get-tuple-element.68.chan_h, ...), custom_call_target="tpu_custom_call" | custom-call | tf_op jit(solution)/shard_map/branch_back/pallas_call | solution.py:1438
  350.6 6.8 %collect.1 = (f32[256,1536]{1,0:T(8,128)}, f32[256,1536]{1,0:T(8,128)}, f32[48,4608]{1,0:T(8,128)}, f32[48,4608]{1,0:T(8,128)}, f32[144,1536]{1,0:T(8,128)}, /*i...) custom-call(f32[8,512]{1,0:T(8,128)} %get-tuple-element.90.chan, ...), custom_call_target="tpu_custom_call" | custom-call | tf_op jit(solution)/shard_map/collect/pallas_call | solution.py:1485
